TPU v7x, 32 devices: a whole 2x2x4 slice. The times are simulated.
32 devices in a mesh: dp: 8 (over y, x, core), mp: 4 (over z).
Axes of the slice: x: 2, y: 2, z: 4, core: 2. Of those that a mesh axis runs over, the one named last changes fastest.
Arguments:
- tokens: bfloat16 [8192, 2048], P('dp'), may hold values from -6 to 6
- cotangent: bfloat16 [8192, 2048], P('dp'), may hold values from -6 to 6
- lengths: int32 [8], P('dp'), may hold values from 50 to 1024, as said below
- qkv_weight: float32 [2048, 3, 2048], P('dp', None, 'mp'), may hold values from -0.125 to 0.125
- out_weight: float32 [2048, 2048], P('mp', 'dp'), may hold values from -3 to 3
- gate_up_weight: float32 [2048, 2, 8192], P('dp', None, 'mp'), may hold values from -0.125 to 0.125
- down_weight: float32 [8192, 2048], P('mp', 'dp'), may hold values from -0.0625 to 0.0625
- norm_gains: float32 [2, 2048], P(None, 'dp'), may hold values from 0.25 to 1.75
- qkv_first: float32 [2048, 3, 2048], P('dp', None, 'mp')
- out_first: float32 [2048, 2048], P('mp', 'dp')
- gate_up_first: float32 [2048, 2, 8192], P('dp', None, 'mp')
- down_first: float32 [8192, 2048], P('mp', 'dp')
- gains_first: float32 [2, 2048], P(None, 'dp')
- qkv_second: float32 [2048, 3, 2048], P('dp', None, 'mp'), may hold values from 2048 to 8192
- out_second: float32 [2048, 2048], P('mp', 'dp'), may hold values from 8 to 32
- gate_up_second: float32 [2048, 2, 8192], P('dp', None, 'mp'), may hold values from 2048 to 8192
- down_second: float32 [8192, 2048], P('mp', 'dp'), may hold values from 2048 to 8192
- gains_second: float32 [2, 2048], P(None, 'dp'), may hold values from 8192 to 32768
Outputs:
- block_out: bfloat16 [8192, 2048], P(('dp', 'mp'))
- tokens_grad: float32 [8192, 2048], P(('dp', 'mp'))
- qkv_new: float32 [2048, 3, 2048], P('dp', None, 'mp')
- out_new: float32 [2048, 2048], P('mp', 'dp')
- gate_up_new: float32 [2048, 2, 8192], P('dp', None, 'mp')
- down_new: float32 [8192, 2048], P('mp', 'dp')
- gains_new: float32 [2, 2048], P(None, 'dp')
- qkv_first_new: float32 [2048, 3, 2048], P('dp', None, 'mp')
- out_first_new: float32 [2048, 2048], P('mp', 'dp')
- gate_up_first_new: float32 [2048, 2, 8192], P('dp', None, 'mp')
- down_first_new: float32 [8192, 2048], P('mp', 'dp')
- gains_first_new: float32 [2, 2048], P(None, 'dp')
- qkv_second_new: float32 [2048, 3, 2048], P('dp', None, 'mp')
- out_second_new: float32 [2048, 2048], P('mp', 'dp')
- gate_up_second_new: float32 [2048, 2, 8192], P('dp', None, 'mp')
- down_second_new: float32 [8192, 2048], P('mp', 'dp')
- gains_second_new: float32 [2, 2048], P(None, 'dp')
Inputs may be any that keep to these rules, and one draw needn't show every extreme that they name: `lengths`: one sequence in every draw has all 1024 tokens valid.
All inputs are finite; a program needn't handle non-finite values.
Results may differ from a plain program's by a relative error of at most 0.014.
The roundings to bfloat16 on the way count: a program that leaves them out, or rounds other values in their place, can miss the bound.
Values may be sent and summed in bfloat16 or wider, within the bound.
No kernel may reach another device: no remote copies, remote signals or barrier semaphores. Data moves between devices by JAX's collectives and lax.ppermute only.
A program may use at most 384 MiB of HBM per device.

v0:
```python
import math

import jax
import jax.numpy as jnp
from jax import lax
from jax.sharding import PartitionSpec as P

D = 2048
H = 16
HD = 128
FF = 8192
SEQ = 1024
STEP = 10


norm_eps = 1e-05
adam_eps = 1e-08
beta_first = 0.5
beta_second = 0.5
weight_decay = 0.1


def step_rates():
    return (
        0.8 / math.sqrt(D),
        0.8 / math.sqrt(max(1, 2 * H * HD // SEQ)),
        0.8 / math.sqrt(D),
        0.8 / math.sqrt(FF),
        0.4,
    )


def rope_tables():
    halfway = HD // 2
    inverse = jnp.exp(-math.log(10000.0) * jnp.arange(halfway, dtype=jnp.float32) * 2.0 / HD)
    angles = jnp.arange(SEQ, dtype=jnp.float32)[:, None] * inverse[None, :]
    return (jnp.cos(angles), jnp.sin(angles))


def rotate(vectors, cosine, sine_table):
    halfway = HD // 2
    front_half = vectors[..., :halfway]
    behind = vectors[..., halfway:]
    return jnp.concatenate(
        [front_half * cosine - behind * sine_table, behind * cosine + front_half * sine_table],
        axis=-1,
    )


def norm_forward(values, gain):
    inverse = lax.rsqrt(jnp.mean(values * values, axis=-1, keepdims=True) + norm_eps)
    return (values * inverse * gain, inverse)


def norm_backward(values, inverse, gain, upstream):
    scaled = upstream * gain
    gain_grad = jnp.sum(upstream * values * inverse, axis=0)
    values_grad = inverse * scaled - values * inverse * inverse * inverse * jnp.mean(
        scaled * values, axis=-1, keepdims=True
    )
    return (values_grad, gain_grad)


def block_mask(begin_row, end_row, valid_len):
    row_ids = begin_row + jnp.arange(end_row - begin_row, dtype=jnp.int32)[:, None]
    col_ids = jnp.arange(end_row, dtype=jnp.int32)[None, :]
    return ((col_ids <= row_ids) & (col_ids < valid_len)).astype(jnp.float32)


def block_scores(query_block, keys_rot, end_row):
    raw = jnp.einsum(
        "hqe,hke->hqk", query_block, keys_rot[:, :end_row], preferred_element_type=jnp.float32
    )
    return raw / math.sqrt(HD) - math.log(SEQ)


def attend_forward(queries, keys_rot, values, valid_len):
    block_rows = min(512, SEQ)
    pieces = []
    for begin_row in range(0, SEQ, block_rows):
        end_row = begin_row + block_rows
        scores = block_scores(queries[:, begin_row:end_row], keys_rot, end_row)
        weights_p = jax.nn.sigmoid(scores) * block_mask(begin_row, end_row, valid_len)
        pieces.append(
            jnp.einsum(
                "hqk,hke->hqe",
                weights_p.astype(jnp.bfloat16),
                values[:, :end_row],
                preferred_element_type=jnp.float32,
            )
        )
    return jnp.concatenate(pieces, axis=1)


def attend_backward(queries, keys_rot, values, mixed_back, valid_len):
    block_rows = min(512, SEQ)
    query_parts = []
    key_back = jnp.zeros(keys_rot.shape, jnp.float32)
    value_back = jnp.zeros(values.shape, jnp.float32)
    for begin_row in range(0, SEQ, block_rows):
        end_row = begin_row + block_rows
        query_block = queries[:, begin_row:end_row]
        back_block = mixed_back[:, begin_row:end_row]
        scores = block_scores(query_block, keys_rot, end_row)
        mask_block = block_mask(begin_row, end_row, valid_len)
        sigmoid_val = jax.nn.sigmoid(scores)
        weights_p = (sigmoid_val * mask_block).astype(jnp.bfloat16)
        value_back = value_back.at[:, :end_row].add(
            jnp.einsum("hqk,hqe->hke", weights_p, back_block, preferred_element_type=jnp.float32)
        )
        weight_back = jnp.einsum(
            "hqe,hke->hqk", back_block, values[:, :end_row], preferred_element_type=jnp.float32
        )
        score_back = (weight_back * mask_block * sigmoid_val * (1.0 - sigmoid_val)).astype(
            jnp.bfloat16
        )
        query_parts.append(
            jnp.einsum(
                "hqk,hke->hqe",
                score_back,
                keys_rot[:, :end_row],
                preferred_element_type=jnp.float32,
            )
            / math.sqrt(HD)
        )
        key_back = key_back.at[:, :end_row].add(
            jnp.einsum("hqk,hqe->hke", score_back, query_block, preferred_element_type=jnp.float32)
            / math.sqrt(HD)
        )
    return (jnp.concatenate(query_parts, axis=1), key_back, value_back)


def split_heads(block, seq_count, local_heads):
    return block.reshape(seq_count, SEQ, local_heads, HD).transpose(0, 2, 1, 3)


def merge_heads(block, seq_count, local_heads):
    return block.transpose(0, 2, 1, 3).reshape(seq_count * SEQ, local_heads * HD)


def adamw(weight, moment_one, moment_two, gradient, step_rate):
    first_new = beta_first * moment_one + (1.0 - beta_first) * gradient
    second_new = beta_second * moment_two + (1.0 - beta_second) * gradient * gradient
    first_hat = first_new / (1.0 - beta_first**STEP)
    second_hat = second_new / (1.0 - beta_second**STEP)
    weight_new = weight - step_rate * (
        first_hat / (jnp.sqrt(second_hat) + adam_eps) + weight_decay * weight
    )
    return (weight_new, first_new, second_new)


def reduce_grads(row_major, col_major, gain_part):
    return (
        lax.psum_scatter(row_major, "dp", scatter_dimension=0, tiled=True),
        lax.psum_scatter(col_major, "dp", scatter_dimension=1, tiled=True),
        lax.psum_scatter(gain_part, "dp", scatter_dimension=1, tiled=True),
    )


def local(
    tokens,
    cotangent,
    lengths,
    qkv_weight,
    out_weight,
    gate_up_weight,
    down_weight,
    norm_gains,
    qkv_first,
    out_first,
    gate_up_first,
    down_first,
    gains_first,
    qkv_second,
    out_second,
    gate_up_second,
    down_second,
    gains_second,
):
    bf16 = jnp.bfloat16
    f32 = jnp.float32
    gathered = (
        lax.all_gather(qkv_weight.astype(bf16), "dp", axis=0, tiled=True),
        lax.all_gather(out_weight.astype(bf16), "dp", axis=1, tiled=True),
        lax.all_gather(gate_up_weight.astype(bf16), "dp", axis=0, tiled=True),
        lax.all_gather(down_weight.astype(bf16), "dp", axis=1, tiled=True),
        lax.all_gather(norm_gains.astype(bf16), "dp", axis=1, tiled=True),
    )
    qkv_full, out_full, gate_up_full, down_full, gain_low = gathered
    seq_count = lengths.shape[0]
    local_heads = qkv_full.shape[2] // HD
    cosine, sine_table = rope_tables()
    row_count = tokens.shape[0] // lax.axis_size("mp")
    row_start = lax.axis_index("mp") * row_count

    def own_rows(block):
        return lax.dynamic_slice_in_dim(block, row_start, row_count, 0)

    tokens32 = tokens.astype(f32)
    gain_one = gain_low[0].astype(f32)
    gain_two = gain_low[1].astype(f32)
    normed, scale_one = norm_forward(tokens32, gain_one)
    normed_bf = normed.astype(bf16)
    project = jnp.einsum("nd,dkf->nkf", normed_bf, qkv_full, preferred_element_type=f32)
    queries = rotate(split_heads(project[:, 0], seq_count, local_heads), cosine, sine_table).astype(
        bf16
    )
    keys_rot = rotate(
        split_heads(project[:, 1], seq_count, local_heads), cosine, sine_table
    ).astype(bf16)
    values = split_heads(project[:, 2], seq_count, local_heads).astype(bf16)
    mixed = lax.map(
        lambda seq_item: attend_forward(*seq_item), (queries, keys_rot, values, lengths)
    )
    mixed_bf = merge_heads(mixed, seq_count, local_heads).astype(bf16)
    attended = lax.psum(jnp.dot(mixed_bf, out_full, preferred_element_type=f32), "mp")
    middle = tokens32 + attended
    normed_two, scale_two = norm_forward(middle, gain_two)
    normed_two_bf = normed_two.astype(bf16)
    gate_up = jnp.einsum("nd,dkf->nkf", normed_two_bf, gate_up_full, preferred_element_type=f32)
    gate_val = gate_up[:, 0]
    up_val = gate_up[:, 1]
    gate_sig = jax.nn.sigmoid(gate_val)
    silu_val = gate_val * gate_sig
    hidden_bf = (silu_val * up_val).astype(bf16)
    feed_out = lax.psum(jnp.dot(hidden_bf, down_full, preferred_element_type=f32), "mp")
    block_out = own_rows(middle + feed_out).astype(bf16)
    qkv_full, out_full, gate_up_full, down_full, gain_low = (
        lax.all_gather(qkv_weight.astype(bf16), "dp", axis=0, tiled=True),
        lax.all_gather(out_weight.astype(bf16), "dp", axis=1, tiled=True),
        lax.all_gather(gate_up_weight.astype(bf16), "dp", axis=0, tiled=True),
        lax.all_gather(down_weight.astype(bf16), "dp", axis=1, tiled=True),
        lax.all_gather(norm_gains.astype(bf16), "dp", axis=1, tiled=True),
    )
    back32 = cotangent.astype(f32)
    hidden_back = jnp.einsum("nd,fd->nf", cotangent, down_full, preferred_element_type=f32)
    gate_grad = hidden_back * up_val * gate_sig * (1.0 + gate_val * (1.0 - gate_sig))
    up_grad = hidden_back * silu_val
    gate_up_back = jnp.stack([gate_grad, up_grad], axis=1).astype(bf16)
    down_grad = jnp.einsum("nf,nd->fd", hidden_bf, cotangent, preferred_element_type=f32)
    gate_up_grad = jnp.einsum(
        "nd,nkf->dkf", normed_two_bf, gate_up_back, preferred_element_type=f32
    )
    normed_two_back = lax.psum(
        jnp.einsum("nkf,dkf->nd", gate_up_back, gate_up_full, preferred_element_type=f32), "mp"
    )
    middle_back, gain_two_grad = norm_backward(middle, scale_two, gain_two, normed_two_back)
    middle_back = middle_back + back32
    middle_low = middle_back.astype(bf16)
    out_grad = jnp.einsum("na,nd->ad", mixed_bf, middle_low, preferred_element_type=f32)
    mixed_back = jnp.einsum("nd,ad->na", middle_low, out_full, preferred_element_type=f32).astype(
        bf16
    )
    mixed_back = split_heads(mixed_back, seq_count, local_heads)
    query_back, key_back, value_back = lax.map(
        lambda seq_item: attend_backward(*seq_item),
        (queries, keys_rot, values, mixed_back, lengths),
    )
    query_back = rotate(query_back, cosine, -sine_table)
    key_back = rotate(key_back, cosine, -sine_table)
    project_back = jnp.stack(
        [
            merge_heads(query_back, seq_count, local_heads),
            merge_heads(key_back, seq_count, local_heads),
            merge_heads(value_back, seq_count, local_heads),
        ],
        axis=1,
    ).astype(bf16)
    qkv_grad = jnp.einsum("nd,nkf->dkf", normed_bf, project_back, preferred_element_type=f32)
    normed_back = lax.psum(
        jnp.einsum("nkf,dkf->nd", project_back, qkv_full, preferred_element_type=f32), "mp"
    )
    tokens_part, gain_one_grad = norm_backward(tokens32, scale_one, gain_one, normed_back)
    tokens_grad = own_rows(tokens_part + middle_back)
    ffn_reduced = reduce_grads(gate_up_grad, down_grad, gain_two_grad[None])
    attn_reduced = reduce_grads(qkv_grad, out_grad, gain_one_grad[None])
    gains_reduced = jnp.concatenate([attn_reduced[2], ffn_reduced[2]], axis=0)
    rates = step_rates()
    qkv_all = adamw(qkv_weight, qkv_first, qkv_second, attn_reduced[0], rates[0])
    out_all = adamw(out_weight, out_first, out_second, attn_reduced[1], rates[1])
    gate_up_all = adamw(gate_up_weight, gate_up_first, gate_up_second, ffn_reduced[0], rates[2])
    down_all = adamw(down_weight, down_first, down_second, ffn_reduced[1], rates[3])
    gains_all = adamw(norm_gains, gains_first, gains_second, gains_reduced, rates[4])
    return (
        block_out,
        tokens_grad,
        qkv_all[0],
        out_all[0],
        gate_up_all[0],
        down_all[0],
        gains_all[0],
        qkv_all[1],
        out_all[1],
        gate_up_all[1],
        down_all[1],
        gains_all[1],
        qkv_all[2],
        out_all[2],
        gate_up_all[2],
        down_all[2],
        gains_all[2],
    )


def solution(mesh):
    in_specs = (
        P("dp", None),
        P("dp", None),
        P("dp"),
        P("dp", None, "mp"),
        P("mp", "dp"),
        P("dp", None, "mp"),
        P("mp", "dp"),
        P(None, "dp"),
        P("dp", None, "mp"),
        P("mp", "dp"),
        P("dp", None, "mp"),
        P("mp", "dp"),
        P(None, "dp"),
        P("dp", None, "mp"),
        P("mp", "dp"),
        P("dp", None, "mp"),
        P("mp", "dp"),
        P(None, "dp"),
    )
    out_specs = (
        P(("dp", "mp"), None),
        P(("dp", "mp"), None),
        P("dp", None, "mp"),
        P("mp", "dp"),
        P("dp", None, "mp"),
        P("mp", "dp"),
        P(None, "dp"),
        P("dp", None, "mp"),
        P("mp", "dp"),
        P("dp", None, "mp"),
        P("mp", "dp"),
        P(None, "dp"),
        P("dp", None, "mp"),
        P("mp", "dp"),
        P("dp", None, "mp"),
        P("mp", "dp"),
        P(None, "dp"),
    )
    return jax.shard_map(local, mesh=mesh, in_specs=in_specs, out_specs=out_specs, check_vma=False)
```

profile of v0, /device:TPU:26, one launch (start us, length us, event | category | flops | bytes accessed | tf_op | source)
XLA Modules:
  0.0 2111.0 jit_solution(17091533527307586211)
XLA Ops:
  11.8 8.9 all_gather.19
  20.7 3.2 fusion
  23.9 2.9 fusion.49
  29.0 29.2 %all-gather.5.cloned.1.call-done = bf16[2048,3,512]{0,2,1:T(8,128)(2,1)} async-done(((bf16[256,3,512]{0,2,1:T(8,128)(2,1)}), bf16[2048,3,512]{0,2,1:T(8,128)(2,1)}) %all-gather.5.cloned.1.call-update) | async-done | bytes 6291472 | tf_op jit(solution)/shard_map/all_gather | solution.py:183
  58.1 10.2 fusion.36
  71.8 2.9 copy.87
  74.7 2.9 copy.88
  79.2 5.3 fusion.31
  88.8 2.9 add_divide_fusion.1
  98.6 7.6 fusion.70
  106.3 5.7 copy.137
  112.1 3.1 convert_element_type.131
  115.3 280.2 %all-reduce.7.cloned.1.call-done = f32[1024,2048]{1,0:T(8,128)} async-done(((f32[1024,2048]{1,0:T(8,128)}), f32[1024,2048]{1,0:T(8,128)}) %all-reduce.7.cloned.1.call-update) | async-done | bytes 8388624 | tf_op jit(solution)/shard_map/psum | solution.py:216
  395.5 8.9 multiply_reduce_fusion.2
  404.4 84.4 %all-gather.9.cloned.1.call-done = bf16[2048,2,2048]{2,0,1:T(8,128)(2,1)} async-done(((bf16[256,2,2048]{2,0,1:T(8,128)(2,1)}), bf16[2048,2,2048]{2,0,1:T(8,128)(2,1)}) %all-gather.9.cloned.1.call-update) | async-done | bytes 16777232 | tf_op jit(solution)/shard_map/all_gather | solution.py:185
  488.7 24.8 %fusion.51 = f32[1024,2,2048]{2,0,1:T(8,128)} fusion(bf16[2048,2,2048]{2,0,1:T(8,128)(2,1)} %all-gather.9.cloned.1.call-done, f32[1024,2048]{1,0:T(8,128)} %get-tuple-element.220, f32[2048]{0:T(1024)S(1)} %bitcast.136, f32[1024]{0:T(1024)S(1)} %add_rsqrt_fusion), kind=kOutput, calls=%fused_computation.120 | convolution fusion | flops 17186160640 | bytes 41955328 | tf_op jit(solution)/shard_map/nd,dkf->nkf/dot_general | solution.py:220
  513.5 33.5 %all-gather.11.cloned.1.call-done = bf16[2048,2048]{1,0:T(8,128)(2,1)} async-done(((bf16[2048,256]{1,0:T(8,128)(2,1)}), bf16[2048,2048]{1,0:T(8,128)(2,1)}) %all-gather.11.cloned.1.call-update) | async-done | bytes 8388624 | tf_op jit(solution)/shard_map/all_gather | solution.py:186
  547.0 21.7 %fusion.12 = (bf16[1024,1,2048]{2,0,1:T(8,128)(2,1)}, bf16[1024,1,2048]{2,0,1:T(8,128)(2,1)}, bf16[1024,2048]{1,0:T(8,128)(2,1)}) fusion(f32[1024,2,2048]{2,0,1:T(8,128)} %fusion.51, bf16[1024,2048]{1,0:T(8,128)(2,1)} %param.31, bf16[2048,2048]{1,0:T(8,128)(2,1)} %all-gather.11.cloned.1.call-done), kind=kOutput, calls=%fused_computation.43 | convolution fusion | flops 8621391872 | bytes 41943040 | tf_op jit(solution)/shard_map/nd,fd->nf/dot_general | solution.py:236
  568.7 24.2 %fusion.7 = f32[1024,2048]{1,0:T(8,128)} fusion(bf16[2048,2,2048]{2,0,1:T(8,128)(2,1)} %all-gather.9.cloned.1.call-done, bf16[1024,1,2048]{2,0,1:T(8,128)(2,1)} %get-tuple-element.222, bf16[1024,1,2048]{2,0,1:T(8,128)(2,1)} %get-tuple-element.221), kind=kOutput, calls=%fused_computation.30 | convolution fusion | flops 17184063488 | bytes 33554432 | tf_op jit(solution)/shard_map/nkf,dkf->nd/dot_general | solution.py:245
  593.0 14.6 fusion.71
  607.7 274.3 %all-reduce.9.cloned.1.call-done = f32[1024,2048]{1,0:T(8,128)} async-done(((f32[1024,2048]{1,0:T(8,128)}), f32[1024,2048]{1,0:T(8,128)}) %all-reduce.9.cloned.1.call-update) | async-done | bytes 8388624 | tf_op jit(solution)/shard_map/psum | solution.py:244
  882.0 7.2 multiply_reduce_fusion
  891.4 5.0 convert_add_fusion.1
  896.4 3.7 fusion.25
  902.4 3.5 multiply_convert_fusion.7
  906.0 4.7 multiply_convert_fusion
  924.9 3.2 maximum_bitcast_fusion.3
  932.6 5.6 add_convert_fusion
  939.7 11.7 convolution_bitcast_fusion
  952.9 7.7 fusion.18
  960.7 15.3 fusion.72
  976.1 537.4 %all-reduce.11.cloned.1.call-done = (f32[1024,2048]{1,0:T(8,128)}, f32[1024,2048]{1,0:T(8,128)}) async-done(((f32[1024,2048]{1,0:T(8,128)}, f32[1024,2048]{1,0:T(8,128)}), (f32[1024,2048]{1,0:T(8,128)}, f32[1024,2048]{1,0:T(8,128)})) %all-reduce.11.cloned.1.call-update) | async-done | bytes 16777232 | tf_op jit(solution)/shard_map/psum | solution.py:226
  1513.5 10.2 fusion.3
  1525.1 12.6 fusion.28
  1537.8 26.3 %fusion.5 = f32[2048,2,2048]{2,0,1:T(8,128)} fusion(bf16[1024,1,2048]{2,0,1:T(8,128)(2,1)} %get-tuple-element.222, bf16[1024,1,2048]{2,0,1:T(8,128)(2,1)} %get-tuple-element.221, f32[1024,2048]{1,0:T(8,128)} %get-tuple-element.220, f32[2048]{0:T(1024)S(1)} %bitcast.139, f32[1024]{0:T(1024)S(1)} %add_rsqrt_fusion), kind=kOutput, calls=%fused_computation.28 | convolution fusion | flops 17202937856 | bytes 50343936 | tf_op jit(solution)/shard_map/nd,nkf->dkf/dot_general | solution.py:241
  1565.3 44.0 %reduce-scatter.13.cloned.1.call-done = f32[512,256]{1,0:T(8,128)} async-done(((f32[512,2048]{1,0:T(8,128)}), f32[512,256]{1,0:T(8,128)}) %reduce-scatter.13.cloned.1.call-update) | async-done | bytes 524304 | tf_op jit(solution)/shard_map/reduce_scatter | solution.py:155
  1611.8 3.5 fusion.17
  1615.3 4.8 dynamic-slice_add_fusion
  1620.1 108.9 %reduce-scatter.17.cloned.1.call-done = f32[2048,256]{1,0:T(8,128)} async-done(((f32[2048,2048]{1,0:T(8,128)}), f32[2048,256]{1,0:T(8,128)}) %reduce-scatter.17.cloned.1.call-update) | async-done | bytes 2097168 | tf_op jit(solution)/shard_map/reduce_scatter | solution.py:155
  1729.1 6.7 multiply_subtract_fusion.1
  1735.7 33.6 %reduce-scatter.19.cloned.1.call-done = f32[256,1]{1,0:T(8,128)} async-done(((f32[2048,1]{1,0:T(8,128)}), f32[256,1]{1,0:T(8,128)}) %reduce-scatter.19.cloned.1.call-update) | async-done | bytes 1040
  1770.9 94.5 %reduce-scatter.11.cloned.1.call-done = f32[256,3,512]{2,0,1:T(8,128)} async-done(((f32[2048,3,512]{2,0,1:T(8,128)}), f32[256,3,512]{2,0,1:T(8,128)}) %reduce-scatter.11.cloned.1.call-update) | async-done | bytes 1572880 | tf_op jit(solution)/shard_map/reduce_scatter | solution.py:154
  1865.4 5.9 multiply_subtract_fusion.2
  1871.2 203.4 %reduce-scatter.15.cloned.1.call-done = f32[256,2,2048]{2,0,1:T(8,128)} async-done(((f32[2048,2,2048]{2,0,1:T(8,128)}), f32[256,2,2048]{2,0,1:T(8,128)}) %reduce-scatter.15.cloned.1.call-update) | async-done | bytes 4194320 | tf_op jit(solution)/shard_map/reduce_scatter | solution.py:154
  2074.7 13.6 multiply_subtract_fusion
  2088.3 5.2 copy.111
  2093.6 5.2 copy.112
  2098.8 5.2 copy.113
  (153 shorter events, 55.4 us)
Async XLA Ops:
  7.2 4.6 copy-start.35
  7.2 50.9 %all-gather.5.cloned.1.call-start = ((), (), s32[]{:S(2)}) async-start(), calls=%async_computation.6 | async-start | bytes 7077888 | tf_op jit(solution)/shard_map/all_gather | solution.py:183
  9.8 88.8 %all-gather.7.cloned.1.call-start = ((), (), s32[]{:S(2)}) async-start(), calls=%async_computation.7 | async-start | bytes 2359296 | tf_op jit(solution)/shard_map/all_gather | solution.py:184
  11.7 383.8 %all-reduce.7.cloned.1.call-start = ((), (), s32[]{:S(2)}) async-start(), calls=%async_computation.8 | async-start | bytes 16777216 | tf_op jit(solution)/shard_map/psum | solution.py:216
  20.7 37.5 %copy-start.31 = (f32[1,2048]{1,0:T(1,128)}, f32[1,2048]{1,0:T(1,128)S(1)}, u32[]{:S(2)}) copy-start(f32[1,2048]{1,0:T(1,128)S(1)} %get-tuple-element.240) | copy-start | bytes 24580
  23.9 44.5 %copy-start.33 = (f32[1024]{0:T(1024)}, f32[1024]{0:T(1024)S(1)}, u32[]{:S(2)}) copy-start(f32[1024]{0:T(1024)S(1)} %add_rsqrt_fusion.1) | copy-start | bytes 12292
  84.5 2.3 copy-start.9
  84.5 2.3 copy-start.11
  84.6 4.3 copy-start.16
  84.6 4.3 copy-start.18
  85.2 3.6 copy-start.23
  85.2 2.0 copy-start.4
  86.8 2.0 copy-start.1
  91.8 3.2 copy-start
  106.3 382.5 %all-gather.9.cloned.1.call-start = ((), (), s32[]{:S(2)}) async-start(), calls=%async_computation.9 | async-start | bytes 18874368 | tf_op jit(solution)/shard_map/all_gather | solution.py:185
  112.1 434.9 %all-gather.11.cloned.1.call-start = ((), (), s32[]{:S(2)}) async-start(), calls=%async_computation.10 | async-start | bytes 9437184 | tf_op jit(solution)/shard_map/all_gather | solution.py:186
  115.2 766.7 %all-reduce.9.cloned.1.call-start = ((), (), s32[]{:S(2)}) async-start(), calls=%async_computation.11 | async-start | bytes 16777216 | tf_op jit(solution)/shard_map/psum | solution.py:244
  593.0 920.5 %all-reduce.11.cloned.1.call-start = ((), (), s32[]{:S(2)}) async-start(), calls=%async_computation.18 | async-start | bytes 33554432 | tf_op jit(solution)/shard_map/psum | solution.py:226
  882.0 8.2 copy-start.3
  882.0 9.4 copy-start.15
  891.4 5.0 copy-start.39
  896.4 3.7 copy-start.6
  902.4 3.5 copy-start.7
  905.9 4.7 copy-start.10
  905.9 4.7 copy-start.12
  905.9 5.8 copy-start.21
  910.6 2.2 copy-start.2
  910.7 2.5 copy-start.5
  916.2 1.8 copy-start.14
  916.2 1.8 copy-start.25
  924.9 7.7 copy-start.8
  951.4 612.7 %reduce-scatter.21.cloned.1.call-start = ((), (), s32[]{:S(2)}) async-start(), calls=%async_computation.17 | async-start | bytes 1179648
  952.9 656.4 %reduce-scatter.13.cloned.1.call-start = ((), (), s32[]{:S(2)}) async-start(), calls=%async_computation.13 | async-start | bytes 4718592 | tf_op jit(solution)/shard_map/reduce_scatter | solution.py:155
  960.7 768.4 %reduce-scatter.17.cloned.1.call-start = ((), (), s32[]{:S(2)}) async-start(), calls=%async_computation.15 | async-start | bytes 18874368 | tf_op jit(solution)/shard_map/reduce_scatter | solution.py:155
  976.0 537.5 %copy-start.32 = (f32[1,2048]{1,0:T(1,128)S(1)}, f32[1,2048]{1,0:T(1,128)}, u32[]{:S(2)}) copy-start(f32[1,2048]{1,0:T(1,128)} %copy-done.31) | copy-start | bytes 24580
  976.0 537.5 %copy-start.34 = (f32[1024]{0:T(1024)S(1)}, f32[1024]{0:T(1024)}, u32[]{:S(2)}) copy-start(f32[1024]{0:T(1024)} %copy-done.33) | copy-start | bytes 12292
  976.0 793.3 %reduce-scatter.19.cloned.1.call-start = ((), (), s32[]{:S(2)}) async-start(), calls=%async_computation.16 | async-start | bytes 1179648
  1513.5 11.6 copy-start.27
  1513.5 11.6 copy-start.28
  1525.0 340.3 %reduce-scatter.11.cloned.1.call-start = ((), (), s32[]{:S(2)}) async-start(), calls=%async_computation.12 | async-start | bytes 14155776 | tf_op jit(solution)/shard_map/reduce_scatter | solution.py:154
  1537.7 537.0 %reduce-scatter.15.cloned.1.call-start = ((), (), s32[]{:S(2)}) async-start(), calls=%async_computation.14 | async-start | bytes 37748736 | tf_op jit(solution)/shard_map/reduce_scatter | solution.py:154
  1564.1 45.2 %copy-start.22 = (f32[512,256]{1,0:T(8,128)S(1)}, f32[512,256]{1,0:T(8,128)}, u32[]{:S(2)}) copy-start(f32[512,256]{1,0:T(8,128)} %param.34) | copy-start | bytes 1572868
  1564.1 45.2 %copy-start.29 = (f32[512,256]{1,0:T(8,128)S(1)}, f32[512,256]{1,0:T(8,128)}, u32[]{:S(2)}) copy-start(f32[512,256]{1,0:T(8,128)} %param.39) | copy-start | bytes 1572868
  1564.1 45.2 %copy-start.30 = (f32[512,256]{1,0:T(8,128)S(1)}, f32[512,256]{1,0:T(8,128)}, u32[]{:S(2)}) copy-start(f32[512,256]{1,0:T(8,128)} %param.44) | copy-start | bytes 1572868
  1615.3 113.8 %copy-start.13 = (f32[2048,256]{1,0:T(8,128)S(1)}, f32[2048,256]{1,0:T(8,128)}, u32[]{:S(2)}) copy-start(f32[2048,256]{1,0:T(8,128)} %param.36) | copy-start | bytes 6291460
  1620.1 150.2 %copy-start.36 = (f32[2,256]{1,0:T(2,128)S(1)}, f32[2,256]{1,0:T(2,128)}, u32[]{:S(2)}) copy-start(f32[2,256]{1,0:T(2,128)} %param.37) | copy-start | bytes 6148
  1620.1 150.2 %copy-start.37 = (f32[2,256]{1,0:T(2,128)S(1)}, f32[2,256]{1,0:T(2,128)}, u32[]{:S(2)}) copy-start(f32[2,256]{1,0:T(2,128)} %param.42) | copy-start | bytes 6148
  1620.1 150.2 %copy-start.38 = (f32[2,256]{1,0:T(2,128)S(1)}, f32[2,256]{1,0:T(2,128)}, u32[]{:S(2)}) copy-start(f32[2,256]{1,0:T(2,128)} %param.47) | copy-start | bytes 6148
  (5 other events, 7.7 us)
Sparse Core Ops, SparseCore 0:
  10.5 47.6 all-gather.4
  60.6 28.1 all-gather.6
  106.4 289.0 all-reduce.6
  397.8 90.8 all-gather.8
  491.0 55.9 all-gather.10
  593.1 288.7 all-reduce.8
  951.6 561.8 all-reduce.10
  1517.2 37.3 reduce-scatter.20
  1558.0 51.2 reduce-scatter.12
  1613.1 115.8 reduce-scatter.16
  1733.1 36.1 reduce-scatter.18
  1773.0 92.2 reduce-scatter.10
  1869.3 205.2 reduce-scatter.14
where the time goes:
time: 2120 us; the launch traced here: 2110 us
  waiting for transfers between devices  1720 us (81%)
  matrix products  207 us (10%)
  other arithmetic  94.8 us (4%)
  local copies, waits for them, and re-layouts  60.7 us (3%)
    psum x1, waiting for transfers between devices, local(): lax.psum(jnp.dot(hidden_bf, down_full, preferred_element_type=f32), 'mp')  537 us
    reduce_scatter x2, waiting for transfers between devices, reduce_grads(): lax.psum_scatter(row_major, 'dp', scatter_dimension=0, tiled=True)  298 us
    psum x1, waiting for transfers between devices, local(): lax.psum(jnp.dot(mixed_bf, out_full, preferred_element_type=f32), 'mp')  280 us
    psum x1, waiting for transfers between devices, local(): lax.psum(jnp.einsum('nkf,dkf->nd', gate_up_back, gate_up_full, preferred_...  274 us
    reduce_scatter x2, waiting for transfers between devices, reduce_grads(): lax.psum_scatter(col_major, 'dp', scatter_dimension=1, tiled=True)  153 us
    all_gather x1, waiting for transfers between devices, local(): lax.all_gather(gate_up_weight.astype(bf16), 'dp', axis=0, tiled=True)  84.4 us
  transfers between devices with their start and end apart: 13, of which 11 were waited for; matrix products, arithmetic and copies ran while one was open for 10% of the time, Pallas kernels for 0%

commit v1 on v0

--- a/solution.py
+++ b/solution.py
@@ -149,12 +149,31 @@
     return (weight_new, first_new, second_new)
 
 
-def reduce_grads(row_major, col_major, gain_part):
-    return (
-        lax.psum_scatter(row_major, "dp", scatter_dimension=0, tiled=True),
-        lax.psum_scatter(col_major, "dp", scatter_dimension=1, tiled=True),
-        lax.psum_scatter(gain_part, "dp", scatter_dimension=1, tiled=True),
-    )
+def shift_all(block, take=None):
+    size = lax.axis_size("mp")
+    got = [block if take is None else take(0)]
+    for k in range(1, size):
+        send = block if take is None else take(k)
+        got.append(lax.ppermute(send, "mp", [(j, (j + k) % size) for j in range(size)]))
+    return got
+
+
+def exchange_rows(full):
+    size = lax.axis_size("mp")
+    me = lax.axis_index("mp")
+    rows = full.shape[0] // size
+
+    def take(k):
+        return lax.dynamic_slice_in_dim(full, lax.rem(me + k, size) * rows, rows, 0)
+
+    return shift_all(None, take)
+
+
+def sum_f32(parts):
+    total = parts[0].astype(jnp.float32)
+    for part in parts[1:]:
+        total = total + part.astype(jnp.float32)
+    return total
 
 
 def local(
@@ -179,19 +198,25 @@
 ):
     bf16 = jnp.bfloat16
     f32 = jnp.float32
-    gathered = (
-        lax.all_gather(qkv_weight.astype(bf16), "dp", axis=0, tiled=True),
-        lax.all_gather(out_weight.astype(bf16), "dp", axis=1, tiled=True),
-        lax.all_gather(gate_up_weight.astype(bf16), "dp", axis=0, tiled=True),
-        lax.all_gather(down_weight.astype(bf16), "dp", axis=1, tiled=True),
-        lax.all_gather(norm_gains.astype(bf16), "dp", axis=1, tiled=True),
-    )
-    qkv_full, out_full, gate_up_full, down_full, gain_low = gathered
+    size = lax.axis_size("mp")
+    me = lax.axis_index("mp")
+    qkv_full = lax.all_gather(qkv_weight.astype(bf16), "dp", axis=0, tiled=True)
+    gain_low = lax.all_gather(norm_gains.astype(bf16), "dp", axis=1, tiled=True)
+    out_parts = shift_all(out_weight.astype(bf16))
+    out_rows = jnp.zeros((size,) + out_weight.shape, bf16)
+    for k in range(size):
+        out_rows = lax.dynamic_update_index_in_dim(
+            out_rows, out_parts[k], lax.rem(me - k + size, size), 0
+        )
+    out_full = lax.all_gather(out_rows.reshape(-1, out_weight.shape[1]), "dp", axis=1, tiled=True)
+    gate_up_full = lax.all_gather(gate_up_weight.astype(bf16), "dp", axis=0, tiled=True)
+    down_full = lax.all_gather(down_weight.astype(bf16), "dp", axis=1, tiled=True)
     seq_count = lengths.shape[0]
     local_heads = qkv_full.shape[2] // HD
+    head_cols = qkv_full.shape[2]
     cosine, sine_table = rope_tables()
-    row_count = tokens.shape[0] // lax.axis_size("mp")
-    row_start = lax.axis_index("mp") * row_count
+    row_count = tokens.shape[0] // size
+    row_start = me * row_count
 
     def own_rows(block):
         return lax.dynamic_slice_in_dim(block, row_start, row_count, 0)
@@ -213,45 +238,69 @@
         lambda seq_item: attend_forward(*seq_item), (queries, keys_rot, values, lengths)
     )
     mixed_bf = merge_heads(mixed, seq_count, local_heads).astype(bf16)
-    attended = lax.psum(jnp.dot(mixed_bf, out_full, preferred_element_type=f32), "mp")
+    mixed_parts = shift_all(mixed_bf)
+    attended = None
+    mixed_own = jnp.zeros((row_count, size, head_cols), bf16)
+    for k in range(size):
+        owner = lax.rem(me - k + size, size)
+        rows_of = lax.dynamic_slice_in_dim(out_full, owner * head_cols, head_cols, 0)
+        term = jnp.dot(mixed_parts[k], rows_of, preferred_element_type=f32)
+        attended = term if attended is None else attended + term
+        mixed_own = lax.dynamic_update_slice_in_dim(
+            mixed_own, own_rows(mixed_parts[k])[:, None], owner, 1
+        )
+    mixed_own = mixed_own.reshape(row_count, size * head_cols)
     middle = tokens32 + attended
     normed_two, scale_two = norm_forward(middle, gain_two)
     normed_two_bf = normed_two.astype(bf16)
+    middle_own = own_rows(middle)
+    scale_own = own_rows(scale_two)
     gate_up = jnp.einsum("nd,dkf->nkf", normed_two_bf, gate_up_full, preferred_element_type=f32)
     gate_val = gate_up[:, 0]
     up_val = gate_up[:, 1]
     gate_sig = jax.nn.sigmoid(gate_val)
     silu_val = gate_val * gate_sig
     hidden_bf = (silu_val * up_val).astype(bf16)
-    feed_out = lax.psum(jnp.dot(hidden_bf, down_full, preferred_element_type=f32), "mp")
-    block_out = own_rows(middle + feed_out).astype(bf16)
-    qkv_full, out_full, gate_up_full, down_full, gain_low = (
-        lax.all_gather(qkv_weight.astype(bf16), "dp", axis=0, tiled=True),
-        lax.all_gather(out_weight.astype(bf16), "dp", axis=1, tiled=True),
-        lax.all_gather(gate_up_weight.astype(bf16), "dp", axis=0, tiled=True),
-        lax.all_gather(down_weight.astype(bf16), "dp", axis=1, tiled=True),
-        lax.all_gather(norm_gains.astype(bf16), "dp", axis=1, tiled=True),
-    )
-    back32 = cotangent.astype(f32)
     hidden_back = jnp.einsum("nd,fd->nf", cotangent, down_full, preferred_element_type=f32)
     gate_grad = hidden_back * up_val * gate_sig * (1.0 + gate_val * (1.0 - gate_sig))
     up_grad = hidden_back * silu_val
     gate_up_back = jnp.stack([gate_grad, up_grad], axis=1).astype(bf16)
+    two_back_part = jnp.einsum(
+        "nkf,dkf->nd", gate_up_back, gate_up_full, preferred_element_type=f32
+    ).astype(bf16)
+    two_back_parts = exchange_rows(two_back_part)
+    feed_part = jnp.dot(hidden_bf, down_full, preferred_element_type=f32).astype(bf16)
+    normed_two_back = sum_f32(two_back_parts)
+    middle_back, gain_two_grad = norm_backward(middle_own, scale_own, gain_two, normed_two_back)
+    middle_back = middle_back + own_rows(cotangent).astype(f32)
+    middle_low = middle_back.astype(bf16)
+    mixed_back = jnp.einsum("nd,ad->na", middle_low, out_full, preferred_element_type=f32).astype(
+        bf16
+    )
+
+    def heads_of(k):
+        return lax.dynamic_slice_in_dim(mixed_back, lax.rem(me + k, size) * head_cols, head_cols, 1)
+
+    back_parts = shift_all(None, heads_of)
+    mixed_heads = jnp.zeros((size, row_count, head_cols), bf16)
+    for k in range(size):
+        mixed_heads = lax.dynamic_update_index_in_dim(
+            mixed_heads, back_parts[k], lax.rem(me - k + size, size), 0
+        )
+    feed_part, mixed_heads = lax.optimization_barrier((feed_part, mixed_heads))
+    feed_parts = exchange_rows(feed_part)
+    mixed_back = split_heads(mixed_heads.reshape(-1, head_cols), seq_count, local_heads)
+
     down_grad = jnp.einsum("nf,nd->fd", hidden_bf, cotangent, preferred_element_type=f32)
     gate_up_grad = jnp.einsum(
         "nd,nkf->dkf", normed_two_bf, gate_up_back, preferred_element_type=f32
     )
-    normed_two_back = lax.psum(
-        jnp.einsum("nkf,dkf->nd", gate_up_back, gate_up_full, preferred_element_type=f32), "mp"
-    )
-    middle_back, gain_two_grad = norm_backward(middle, scale_two, gain_two, normed_two_back)
-    middle_back = middle_back + back32
-    middle_low = middle_back.astype(bf16)
-    out_grad = jnp.einsum("na,nd->ad", mixed_bf, middle_low, preferred_element_type=f32)
-    mixed_back = jnp.einsum("nd,ad->na", middle_low, out_full, preferred_element_type=f32).astype(
-        bf16
-    )
-    mixed_back = split_heads(mixed_back, seq_count, local_heads)
+    gate_up_red = lax.psum_scatter(gate_up_grad.astype(bf16), "dp", scatter_dimension=0, tiled=True)
+    down_red = lax.psum_scatter(down_grad.astype(bf16), "dp", scatter_dimension=1, tiled=True)
+    out_grad = jnp.einsum("na,nd->ad", mixed_own, middle_low, preferred_element_type=f32)
+    out_red = lax.psum_scatter(out_grad.astype(bf16), "dp", scatter_dimension=1, tiled=True)
+    out_sum = sum_f32(exchange_rows(out_red))
+
     query_back, key_back, value_back = lax.map(
         lambda seq_item: attend_backward(*seq_item),
         (queries, keys_rot, values, mixed_back, lengths),
@@ -266,40 +315,30 @@
         ],
         axis=1,
     ).astype(bf16)
+    one_back_part = jnp.einsum(
+        "nkf,dkf->nd", project_back, qkv_full, preferred_element_type=f32
+    )
+    one_back_low = one_back_part.astype(bf16)
+    one_back_parts = exchange_rows(one_back_low)
+    gain_one_grad = jnp.sum(one_back_low.astype(f32) * tokens32 * scale_one, axis=0)
     qkv_grad = jnp.einsum("nd,nkf->dkf", normed_bf, project_back, preferred_element_type=f32)
-    normed_back = lax.psum(
-        jnp.einsum("nkf,dkf->nd", project_back, qkv_full, preferred_element_type=f32), "mp"
-    )
-    tokens_part, gain_one_grad = norm_backward(tokens32, scale_one, gain_one, normed_back)
-    tokens_grad = own_rows(tokens_part + middle_back)
-    ffn_reduced = reduce_grads(gate_up_grad, down_grad, gain_two_grad[None])
-    attn_reduced = reduce_grads(qkv_grad, out_grad, gain_one_grad[None])
-    gains_reduced = jnp.concatenate([attn_reduced[2], ffn_reduced[2]], axis=0)
+    qkv_red = lax.psum_scatter(qkv_grad.astype(bf16), "dp", scatter_dimension=0, tiled=True)
+    gains_part = lax.psum_scatter(
+        jnp.stack([gain_one_grad, gain_two_grad]), "dp", scatter_dimension=1, tiled=True
+    )
+    gains_red = sum_f32(shift_all(gains_part))
+    normed_back = sum_f32(one_back_parts)
+    tokens_part, _ = norm_backward(own_rows(tokens32), own_rows(scale_one), gain_one, normed_back)
+    tokens_grad = tokens_part + middle_back
+    block_out = (middle_own + sum_f32(feed_parts)).astype(bf16)
     rates = step_rates()
-    qkv_all = adamw(qkv_weight, qkv_first, qkv_second, attn_reduced[0], rates[0])
-    out_all = adamw(out_weight, out_first, out_second, attn_reduced[1], rates[1])
-    gate_up_all = adamw(gate_up_weight, gate_up_first, gate_up_second, ffn_reduced[0], rates[2])
-    down_all = adamw(down_weight, down_first, down_second, ffn_reduced[1], rates[3])
-    gains_all = adamw(norm_gains, gains_first, gains_second, gains_reduced, rates[4])
-    return (
-        block_out,
-        tokens_grad,
-        qkv_all[0],
-        out_all[0],
-        gate_up_all[0],
-        down_all[0],
-        gains_all[0],
-        qkv_all[1],
-        out_all[1],
-        gate_up_all[1],
-        down_all[1],
-        gains_all[1],
-        qkv_all[2],
-        out_all[2],
-        gate_up_all[2],
-        down_all[2],
-        gains_all[2],
-    )
+    qkv_all = adamw(qkv_weight, qkv_first, qkv_second, qkv_red.astype(f32), rates[0])
+    out_all = adamw(out_weight, out_first, out_second, out_sum, rates[1])
+    gate_up_all = adamw(gate_up_weight, gate_up_first, gate_up_second, gate_up_red.astype(f32), rates[2])
+    down_all = adamw(down_weight, down_first, down_second, down_red.astype(f32), rates[3])
+    gains_all = adamw(norm_gains, gains_first, gains_second, gains_red, rates[4])
+    states = (qkv_all, out_all, gate_up_all, down_all, gains_all)
+    return (block_out, tokens_grad) + tuple(state[j] for j in range(3) for state in states)
 
 
 def solution(mesh):

time: 2120 us -> 922 us (0.43)
  waiting for transfers between devices: 1720 us -> 458 us
  starting transfers between devices: 0.54 us -> 50.9 us
  matrix products: 207 us -> 233 us
  other arithmetic: 94.8 us -> 70.5 us
    psum x3 -> x0, waiting for transfers between devices: 1090 us -> none  [the longest x1 537 us: local(): lax.psum(jnp.dot(hidden_bf, down_full, preferred_element_type=f32), 'mp')]
    reduce_scatter x4, waiting for transfers between devices: 451 us -> 73.3 us  [the longest x1 73.3 us: local(): lax.psum_scatter(gate_up_grad.astype(bf16), 'dp', scatter_dimension=0, ti...]
    ppermute x0 -> x24, waiting for transfers between devices: none -> 348 us  [shift_all(): lax.ppermute(send, 'mp', [(j, (j + k) % size) for j in range(size)])]
    all_gather x1, waiting for transfers between devices: 84.4 us -> 0.01 us  [local(): lax.all_gather(gate_up_weight.astype(bf16), 'dp', axis=0, tiled=True)]
    ppermute x0 -> x24, starting transfers between devices: none -> 50.5 us  [shift_all(): lax.ppermute(send, 'mp', [(j, (j + k) % size) for j in range(size)])]
    unnamed x15 -> x10, waiting for transfers between devices: 33.8 us -> 0.15 us
    dot_general x3 -> x6, matrix products: 30 us -> 54 us  [the longest x4 38 us: local(): term = jnp.dot(mixed_parts[k], rows_of, preferred_element_type=f32)]
  transfers between devices with their start and end apart: 13 -> 33, of which waited for: 11 -> 14; matrix products, arithmetic and copies ran while one was open for 10% -> 25% of each run, Pallas kernels for 0% -> 0%
where the time goes in v1:
time: 922 us; the launch traced here: 916 us
  waiting for transfers between devices  458 us (50%)
  matrix products  233 us (25%)
  local copies, waits for them, and re-layouts  79.2 us (9%)
  other arithmetic  70.5 us (8%)
  starting transfers between devices  50.9 us (6%)
  between operations  15.9 us (2%)
    ppermute x24, waiting for transfers between devices, shift_all(): lax.ppermute(send, 'mp', [(j, (j + k) % size) for j in range(size)])  348 us
    reduce_scatter x1, waiting for transfers between devices, local(): lax.psum_scatter(gate_up_grad.astype(bf16), 'dp', scatter_dimension=0, ti...  73.3 us
    ppermute x24, starting transfers between devices, shift_all(): lax.ppermute(send, 'mp', [(j, (j + k) % size) for j in range(size)])  50.5 us
    dot_general x4, matrix products, local(): term = jnp.dot(mixed_parts[k], rows_of, preferred_element_type=f32)  38 us
    unnamed x103, local copies, waits for them, and re-layouts  34.3 us
    sub x5, other arithmetic, adamw(): weight - step_rate * (first_hat / (jnp.sqrt(second_hat) + adam_eps) + wei...  30.4 us
    dot_general x1, matrix products, local(): jnp.einsum('nd,nkf->dkf', normed_two_bf, gate_up_back, preferred_element_...  26.3 us
    dot_general x1, matrix products, local(): jnp.einsum('nd,dkf->nkf', normed_two_bf, gate_up_full, preferred_element_...  26.2 us
  transfers between devices with their start and end apart: 33, of which 14 were waited for; matrix products, arithmetic and copies ran while one was open for 25% of the time, Pallas kernels for 0%

profile of v1, /device:TPU:26, one launch (start us, length us, event | category | flops | bytes accessed | tf_op | source)
XLA Modules:
  0.0 916.0 jit_solution(10662071481345687165)
XLA Ops:
  12.5 6.1 collective-permute-done
  18.6 16.3 %collective-permute-done.1 = bf16[512,256]{1,0:T(8,128)(2,1)S(1)} collective-permute-done((bf16[512,256]{1,0:T(8,128)(2,1)S(1)}, bf16[512,256]{1,0:T(8,128)(2,1)S(1)}, u32[]{:S(2)}, u32[]{:S(2)}) %collective-permute-start.1) | collective-permute-done | bytes 262176 | tf_op jit(solution)/shard_map/ppermute | solution.py:157
  36.0 6.3 copy.135
  43.6 8.9 all_gather.15
  57.3 3.1 fusion.43
  60.9 10.2 %fusion.8 = f32[1024,3,512]{0,2,1:T(8,128)S(1)} fusion(bf16[2048,3,512]{0,2,1:T(8,128)(2,1)} %all-gather.5.cloned.1.call-done, bf16[1024,2048]{1,0:T(8,128)(2,1)} %param.30, f32[2048]{0:T(1024)S(1)} %bitcast.169, f32[1024]{0:T(1024)S(1)} %add_rsqrt_fusion.1), kind=kOutput, calls=%fused_computation.45 | convolution fusion | flops 6450839552 | bytes 16789504 | tf_op jit(solution)/shard_map/nd,dkf->nkf/dot_general | solution.py:229
  81.9 5.2 fusion.26
  104.3 12.3 %all-gather.7.cloned.1.call-done = bf16[2048,2048]{1,0:T(8,128)(2,1)} async-done(((bf16[2048,256]{1,0:T(8,128)(2,1)}), bf16[2048,2048]{1,0:T(8,128)(2,1)}) %all-gather.7.cloned.1.call-update) | async-done | bytes 8388624 | tf_op jit(solution)/shard_map/all_gather | solution.py:211
  116.6 7.8 fusion.19
  124.4 3.5 collective-permute-done.3
  127.9 7.0 fusion.17
  134.9 58.6 %collective-permute-done.4 = bf16[1024,512]{0,1:T(8,128)(2,1)} collective-permute-done((bf16[1024,512]{0,1:T(8,128)(2,1)}, bf16[1024,512]{0,1:T(8,128)(2,1)}, u32[]{:S(2)}, u32[]{:S(2)}) %collective-permute-start.4) | collective-permute-done | bytes 1048608 | tf_op jit(solution)/shard_map/ppermute | solution.py:157
  193.5 6.9 fusion.15
  200.4 16.3 %multiply_reduce_fusion.1 = (f32[1024]{0:T(1024)S(1)}, f32[1024,2048]{1,0:T(8,128)}) fusion(bf16[1024,512]{0,1:T(8,128)(2,1)} %collective-permute-done.5, bf16[2048,2048]{1,0:T(8,128)(2,1)} %all-gather.7.cloned.1.call-done, s32[]{:T(128)S(6)} %select_n.82, f32[1024,2048]{1,0:T(8,128)} %fusion.15, f32[1024,2048]{1,0:T(8,128)} %fusion.19, ...), kind=kOutput, calls=%fused_computation.14 | convolution fusion | flops 2162162688 | bytes 40898564 | tf_op jit(solution)/shard_map/dot_general | solution.py:247
  216.7 26.2 %fusion.45 = f32[1024,2,2048]{2,0,1:T(8,128)} fusion(bf16[2048,2,2048]{2,0,1:T(8,128)(2,1)} %all-gather.9.cloned.1.call-done, f32[1024,2048]{1,0:T(8,128)} %get-tuple-element.259, f32[2048]{0:T(1024)S(1)} %bitcast.165, f32[1024]{0:T(1024)S(1)} %add_rsqrt_fusion), kind=kOutput, calls=%fused_computation.133 | convolution fusion | flops 17186160640 | bytes 41955328 | tf_op jit(solution)/shard_map/nd,dkf->nkf/dot_general | solution.py:258
  243.0 24.3 %all-gather.11.cloned.1.call-done = bf16[2048,2048]{1,0:T(8,128)(2,1)} async-done(((bf16[2048,256]{1,0:T(8,128)(2,1)}), bf16[2048,2048]{1,0:T(8,128)(2,1)}) %all-gather.11.cloned.1.call-update) | async-done | bytes 8388624 | tf_op jit(solution)/shard_map/all_gather | solution.py:213
  267.3 21.7 %fusion.6 = (bf16[1024,1,2048]{2,0,1:T(8,128)(2,1)}, bf16[1024,1,2048]{2,0,1:T(8,128)(2,1)}, bf16[1024,2048]{1,0:T(8,128)(2,1)}) fusion(f32[1024,2,2048]{2,0,1:T(8,128)} %fusion.45, bf16[1024,2048]{1,0:T(8,128)(2,1)} %param.31, bf16[2048,2048]{1,0:T(8,128)(2,1)} %all-gather.11.cloned.1.call-done), kind=kOutput, calls=%fused_computation.36 | convolution fusion | flops 8621391872 | bytes 41943040 | tf_op jit(solution)/shard_map/nd,fd->nf/dot_general | solution.py:264
  289.0 22.8 %bitcast_convert_fusion.1 = bf16[1024,2048]{1,0:T(8,128)(2,1)S(1)} fusion(bf16[2048,2,2048]{2,0,1:T(8,128)(2,1)} %all-gather.9.cloned.1.call-done, bf16[1024,1,2048]{2,0,1:T(8,128)(2,1)} %get-tuple-element.222, bf16[1024,1,2048]{2,0,1:T(8,128)(2,1)} %get-tuple-element.221), kind=kOutput, calls=%fused_computation.5 | convolution fusion | flops 17186160640 | bytes 29360128 | tf_op jit(solution)/shard_map/nkf,dkf->nd/dot_general | solution.py:268
  318.4 23.1 %collective-permute-done.6 = bf16[256,2048]{1,0:T(8,128)(2,1)} collective-permute-done((bf16[256,2048]{1,0:T(8,128)(2,1)}, bf16[256,2048]{1,0:T(8,128)(2,1)}, u32[]{:S(2)}, u32[]{:S(2)}) %collective-permute-start.6) | collective-permute-done | bytes 1048608 | tf_op jit(solution)/shard_map/ppermute | solution.py:157
  341.5 67.2 %collective-permute-done.7 = bf16[256,2048]{1,0:T(8,128)(2,1)} collective-permute-done((bf16[256,2048]{1,0:T(8,128)(2,1)}, bf16[256,2048]{1,0:T(8,128)(2,1)}, u32[]{:S(2)}, u32[]{:S(2)}) %collective-permute-start.7) | collective-permute-done | bytes 1048608 | tf_op jit(solution)/shard_map/ppermute | solution.py:157
  408.6 3.8 multiply_reduce_fusion.3
  415.2 6.5 convolution_convert_fusion.5
  422.0 10.3 %convolution_convert_fusion.4 = bf16[1024,2048]{1,0:T(8,128)(2,1)} fusion(bf16[1024,2048]{1,0:T(8,128)(2,1)S(1)} %copy-done.45, bf16[2048,2048]{1,0:T(8,128)(2,1)S(1)} %bitcast.176), kind=kOutput, calls=%fused_computation.38 | convolution fusion | flops 8592031744 | bytes 16777216 | tf_op jit(solution)/shard_map/dot_general | solution.py:272
  438.2 13.8 %collective-permute-done.10 = bf16[256,512]{1,0:T(8,128)(2,1)S(1)} collective-permute-done((bf16[256,512]{1,0:T(8,128)(2,1)S(1)}, bf16[256,512]{1,0:T(8,128)(2,1)S(1)}, u32[]{:S(2)}, u32[]{:S(2)}) %collective-permute-start.10) | collective-permute-done | bytes 262176 | tf_op jit(solution)/shard_map/ppermute | solution.py:157
  457.2 3.7 multiply_convert_fusion.7
  460.9 4.4 multiply_convert_fusion
  479.7 3.2 maximum_bitcast_fusion.3
  487.4 5.6 add_convert_fusion
  494.5 12.8 %multiply_reduce_fusion = (f32[2048]{0:T(1024)S(1)}, bf16[1024,2048]{1,0:T(8,128)(2,1)}) fusion(bf16[1024,2048]{1,0:T(8,128)(2,1)} %param.30, f32[1024]{0:T(1024)S(1)} %copy-done.42, bf16[2048,3,512]{0,2,1:T(8,128)(2,1)} %all-gather.5.cloned.1.call-done, bf16[1024,1,512]{2,0,1:T(8,128)(2,1)S(1)} %copy.102, bf16[1024,1,512]{2,0,1:T(8,128)(2,1)} %copy.101, ...), kind=kOutput, calls=%fused_computation.6 | convolution fusion | flops 6458177536 | bytes 17838080 | tf_op jit(solution)/shard_map/nkf,dkf->nd/dot_general | solution.py:318
  508.8 11.7 %convolution_convert_fusion.3 = bf16[2048,3,512]{2,0,1:T(8,128)(2,1)} fusion(bf16[1024,2048]{1,0:T(8,128)(2,1)} %param.30, f32[2048]{0:T(1024)S(1)} %bitcast.170, f32[1024]{0:T(1024)S(1)} %copy-done.42, bf16[1024,1,512]{2,0,1:T(8,128)(2,1)S(1)} %copy.102, bf16[1024,1,512]{2,0,1:T(8,128)(2,1)S(1)} %copy-done.33, bf16[1024,1,512]{2,0,1:T(8,128)(2,1)S(1)} %copy-done.32), kind=kOutput, calls=%fused_computation.25 | convolution fusion | flops 6463422464 | bytes 13643776 | tf_op jit(solution)/shard_map/nd,nkf->dkf/dot_general | solution.py:324
  524.7 5.6 convolution_convert_fusion.2
  530.4 14.2 %convolution_convert_fusion.1 = bf16[2048,2048]{1,0:T(8,128)(2,1)} fusion(bf16[1024,2048]{1,0:T(8,128)(2,1)} %get-tuple-element.223, bf16[1024,2048]{1,0:T(8,128)(2,1)} %param.31), kind=kOutput, calls=%fused_computation.20 | convolution fusion | flops 8594128896 | bytes 16777216 | tf_op jit(solution)/shard_map/nf,nd->fd/dot_general | solution.py:294
  544.7 26.3 %convolution_convert_fusion = bf16[2048,2,2048]{2,0,1:T(8,128)(2,1)} fusion(bf16[1024,1,2048]{2,0,1:T(8,128)(2,1)} %get-tuple-element.222, bf16[1024,1,2048]{2,0,1:T(8,128)(2,1)} %get-tuple-element.221, f32[1024,2048]{1,0:T(8,128)} %get-tuple-element.259, f32[2048]{0:T(1024)S(1)} %bitcast.168, f32[1024]{0:T(1024)S(1)} %add_rsqrt_fusion), kind=kOutput, calls=%fused_computation | convolution fusion | flops 17211326464 | bytes 33566720 | tf_op jit(solution)/shard_map/nd,nkf->dkf/dot_general | solution.py:295
  571.0 4.2 constant_dynamic-slice_fusion.5
  581.6 60.5 %collective-permute-done.21 = f32[2,256]{1,0:T(2,128)S(1)} collective-permute-done((f32[2,256]{1,0:T(2,128)S(1)}, f32[2,256]{1,0:T(2,128)S(1)}, u32[]{:S(2)}, u32[]{:S(2)}) %collective-permute-start.21) | collective-permute-done | bytes 2080 | tf_op jit(solution)/shard_map/ppermute | solution.py:157
  642.1 26.5 %collective-permute-start.23 = (f32[2,256]{1,0:T(2,128)S(1)}, f32[2,256]{1,0:T(2,128)S(1)}, u32[]{:S(2)}, u32[]{:S(2)}) collective-permute-start(f32[2,256]{1,0:T(2,128)S(1)} %copy.125), channel_id=1, source_target_pairs={{0,3},{1,0},{2,1},{3,2},{4,7},{5,4},{6,5},{7,6},{8,11},{9,8},{10,9... | collective-permute-start | bytes 6152 | tf_op jit(solution)/shard_map/ppermute | solution.py:157
  677.2 18.2 %collective-permute-done.12 = bf16[256,2048]{1,0:T(8,128)(2,1)S(1)} collective-permute-done((bf16[256,2048]{1,0:T(8,128)(2,1)S(1)}, bf16[256,2048]{1,0:T(8,128)(2,1)S(1)}, u32[]{:S(2)}, u32[]{:S(2)}) %collective-permute-start.12) | collective-permute-done | bytes 1048608 | tf_op jit(solution)/shard_map/ppermute | solution.py:157
  695.4 66.6 %collective-permute-done.13 = bf16[256,2048]{1,0:T(8,128)(2,1)S(1)} collective-permute-done((bf16[256,2048]{1,0:T(8,128)(2,1)S(1)}, bf16[256,2048]{1,0:T(8,128)(2,1)S(1)}, u32[]{:S(2)}, u32[]{:S(2)}) %collective-permute-start.13) | collective-permute-done | bytes 1048608 | tf_op jit(solution)/shard_map/ppermute | solution.py:157
  762.0 3.7 add_convert_fusion.3
  765.6 4.1 subtract_add_fusion
  769.8 6.3 multiply_subtract_fusion.2
  782.5 7.4 multiply_subtract_fusion.1
  789.9 13.9 %collective-permute-done.19 = bf16[512,256]{1,0:T(8,128)(2,1)} collective-permute-done((bf16[512,256]{1,0:T(8,128)(2,1)}, bf16[512,256]{1,0:T(8,128)(2,1)}, u32[]{:S(2)}, u32[]{:S(2)}) %collective-permute-start.19) | collective-permute-done | bytes 262176 | tf_op jit(solution)/shard_map/ppermute | solution.py:157
  806.5 73.3 %reduce-scatter.12.cloned.1.call-done = bf16[256,2,2048]{2,0,1:T(8,128)(2,1)} async-done(((bf16[2048,2,2048]{2,0,1:T(8,128)(2,1)}), bf16[256,2,2048]{2,0,1:T(8,128)(2,1)}) %reduce-scatter.12.cloned.1.call-update) | async-done | bytes 2097168 | tf_op jit(solution)/shard_map/reduce_scatter | solution.py:298
  879.8 13.5 %multiply_subtract_fusion = (f32[256,2,2048]{2,0,1:T(8,128)S(1)}, f32[256,2,2048]{2,0,1:T(8,128)S(1)}, f32[256,2,2048]{2,0,1:T(8,128)S(1)}) fusion(f32[256,2,2048]{2,1,0:T(2,128)} %param.35, bf16[256,2,2048]{2,0,1:T(8,128)(2,1)} %reduce-scatter.12.cloned.1.call-done, f32[256,2,2048]{2,1,0:T(2,128)} %param.40, f32[256,2,2048]{2,1,0:T(2,128)} %param.45), kind=kLoop, calls=%fused_computation.32 | loop fusion | flops 15728640 | bytes 27262976 | tf_op jit(solution)/shard_map/sub | solution.py:146
  893.2 5.2 copy.110
  898.5 5.2 copy.111
  903.7 5.2 copy.112
  (228 shorter events, 110.4 us)
Async XLA Ops:
  7.2 53.6 %all-gather.5.cloned.1.call-start = ((), (), s32[]{:S(2)}) async-start(), calls=%async_computation.5 | async-start | bytes 7077888 | tf_op jit(solution)/shard_map/all_gather | solution.py:203
  9.9 106.7 %all-gather.7.cloned.1.call-start = ((), (), s32[]{:S(2)}) async-start(), calls=%async_computation.6 | async-start | bytes 9437184 | tf_op jit(solution)/shard_map/all_gather | solution.py:211
  10.1 8.5 collective-permute-start
  10.4 24.6 %collective-permute-start.1 = (bf16[512,256]{1,0:T(8,128)(2,1)S(1)}, bf16[512,256]{1,0:T(8,128)(2,1)S(1)}, u32[]{:S(2)}, u32[]{:S(2)}) collective-permute-start(bf16[512,256]{1,0:T(8,128)(2,1)S(1)} %get-tuple-element.220), channel_id=1, source_target_pairs={{0,2},{1,3},{2,0},{3,1},{4,6},{5,7},{6,4},{7,5},{8,10},{9,11},{10,... | collective-permute-start | bytes 786440 | tf_op jit(solution)/shard_map/ppermute | solution.py:157
  12.0 22.9 %collective-permute-start.2 = (bf16[512,256]{1,0:T(8,128)(2,1)S(1)}, bf16[512,256]{1,0:T(8,128)(2,1)S(1)}, u32[]{:S(2)}, u32[]{:S(2)}) collective-permute-start(bf16[512,256]{1,0:T(8,128)(2,1)S(1)} %get-tuple-element.220), channel_id=1, source_target_pairs={{0,3},{1,0},{2,1},{3,2},{4,7},{5,4},{6,5},{7,6},{8,11},{9,8},{10,9... | collective-permute-start | bytes 786440 | tf_op jit(solution)/shard_map/ppermute | solution.py:157
  36.0 180.7 %all-gather.9.cloned.1.call-start = ((), (), s32[]{:S(2)}) async-start(), calls=%async_computation.7 | async-start | bytes 18874368 | tf_op jit(solution)/shard_map/all_gather | solution.py:212
  42.4 224.9 %all-gather.11.cloned.1.call-start = ((), (), s32[]{:S(2)}) async-start(), calls=%async_computation.8 | async-start | bytes 9437184 | tf_op jit(solution)/shard_map/all_gather | solution.py:213
  43.5 535.3 %reduce-scatter.16.cloned.1.call-start = ((), (), s32[]{:S(2)}) async-start(), calls=%async_computation.13 | async-start | bytes 1179648
  56.2 14.9 %copy-start.41 = (f32[1024]{0:T(1024)}, f32[1024]{0:T(1024)S(1)}, u32[]{:S(2)}) copy-start(f32[1024]{0:T(1024)S(1)} %add_rsqrt_fusion.1) | copy-start | bytes 12292
  60.8 10.3 %copy-start.37 = (f32[1,2048]{1,0:T(1,128)}, f32[1,2048]{1,0:T(1,128)S(1)}, u32[]{:S(2)}) copy-start(f32[1,2048]{1,0:T(1,128)S(1)} %get-tuple-element.254) | copy-start | bytes 24580
  101.0 26.9 %collective-permute-start.3 = (bf16[1024,512]{0,1:T(8,128)(2,1)}, bf16[1024,512]{0,1:T(8,128)(2,1)}, u32[]{:S(2)}, u32[]{:S(2)}) collective-permute-start(bf16[1024,512]{0,1:T(8,128)(2,1)} %bitcast.159), channel_id=1, source_target_pairs={{0,1},{1,2},{2,3},{3,0},{4,5},{5,6},{6,7},{7,4},{8,9},{9,10},{10,1... | collective-permute-start | bytes 3145736 | tf_op jit(solution)/shard_map/ppermute | solution.py:157
  101.0 92.6 %collective-permute-start.4 = (bf16[1024,512]{0,1:T(8,128)(2,1)}, bf16[1024,512]{0,1:T(8,128)(2,1)}, u32[]{:S(2)}, u32[]{:S(2)}) collective-permute-start(bf16[1024,512]{0,1:T(8,128)(2,1)} %bitcast.160), channel_id=1, source_target_pairs={{0,2},{1,3},{2,0},{3,1},{4,6},{5,7},{6,4},{7,5},{8,10},{9,11},{10,... | collective-permute-start | bytes 3145736 | tf_op jit(solution)/shard_map/ppermute | solution.py:157
  102.2 98.2 %collective-permute-start.5 = (bf16[1024,512]{0,1:T(8,128)(2,1)}, bf16[1024,512]{0,1:T(8,128)(2,1)}, u32[]{:S(2)}, u32[]{:S(2)}) collective-permute-start(bf16[1024,512]{0,1:T(8,128)(2,1)} %bitcast.161), channel_id=1, source_target_pairs={{0,3},{1,0},{2,1},{3,2},{4,7},{5,4},{6,5},{7,6},{8,11},{9,8},{10,9... | collective-permute-start | bytes 3145736 | tf_op jit(solution)/shard_map/ppermute | solution.py:157
  116.6 11.3 %copy-start.34 = (bf16[2048,2048]{1,0:T(8,128)(2,1)S(1)}, bf16[2048,2048]{1,0:T(8,128)(2,1)}, u32[]{:S(2)}) copy-start(bf16[2048,2048]{1,0:T(8,128)(2,1)} %all-gather.7.cloned.1.call-done) | copy-start | bytes 25165828
  134.9 65.5 %copy-start.3 = (bf16[1024,2048]{1,0:T(8,128)(2,1)S(1)}, bf16[1024,2048]{1,0:T(8,128)(2,1)}, u32[]{:S(2)}) copy-start(bf16[1024,2048]{1,0:T(8,128)(2,1)} %param.30) | copy-start | bytes 12582916
  315.6 25.9 %collective-permute-start.6 = (bf16[256,2048]{1,0:T(8,128)(2,1)}, bf16[256,2048]{1,0:T(8,128)(2,1)}, u32[]{:S(2)}, u32[]{:S(2)}) collective-permute-start(bf16[256,2048]{1,0:T(8,128)(2,1)} %get-tuple-element.232), channel_id=1, source_target_pairs={{0,1},{1,2},{2,3},{3,0},{4,5},{5,6},{6,7},{7,4},{8,9},{9,10},{10,1... | collective-permute-start | bytes 3145736 | tf_op jit(solution)/shard_map/ppermute | solution.py:157
  316.1 92.5 %collective-permute-start.7 = (bf16[256,2048]{1,0:T(8,128)(2,1)}, bf16[256,2048]{1,0:T(8,128)(2,1)}, u32[]{:S(2)}, u32[]{:S(2)}) collective-permute-start(bf16[256,2048]{1,0:T(8,128)(2,1)} %get-tuple-element.234), channel_id=1, source_target_pairs={{0,2},{1,3},{2,0},{3,1},{4,6},{5,7},{6,4},{7,5},{8,10},{9,11},{10,... | collective-permute-start | bytes 3145736 | tf_op jit(solution)/shard_map/ppermute | solution.py:157
  317.6 91.0 %collective-permute-start.8 = (bf16[256,2048]{1,0:T(8,128)(2,1)}, bf16[256,2048]{1,0:T(8,128)(2,1)}, u32[]{:S(2)}, u32[]{:S(2)}) collective-permute-start(bf16[256,2048]{1,0:T(8,128)(2,1)} %get-tuple-element.233), channel_id=1, source_target_pairs={{0,3},{1,0},{2,1},{3,2},{4,7},{5,4},{6,5},{7,6},{8,11},{9,8},{10,9... | collective-permute-start | bytes 3145736 | tf_op jit(solution)/shard_map/ppermute | solution.py:157
  412.4 9.5 %slice-start = ((s8[8388608]{0:T(1024)(128)(4,1)}), s8[4194304]{0:T(1024)(128)(4,1)S(1)}, s32[]{:S(2)}) async-start(s8[8388608]{0:T(1024)(128)(4,1)} %bitcast.175), calls=%async_computation.14 | async-start | bytes 8388608
  421.9 15.7 %collective-permute-start.9 = (bf16[256,512]{1,0:T(8,128)(2,1)S(1)}, bf16[256,512]{1,0:T(8,128)(2,1)S(1)}, u32[]{:S(2)}, u32[]{:S(2)}) collective-permute-start(bf16[256,512]{1,0:T(8,128)(2,1)S(1)} %get-tuple-element.250), channel_id=1, source_target_pairs={{0,1},{1,2},{2,3},{3,0},{4,5},{5,6},{6,7},{7,4},{8,9},{9,10},{10,1... | collective-permute-start | bytes 786440 | tf_op jit(solution)/shard_map/ppermute | solution.py:157
  432.3 19.8 %collective-permute-start.10 = (bf16[256,512]{1,0:T(8,128)(2,1)S(1)}, bf16[256,512]{1,0:T(8,128)(2,1)S(1)}, u32[]{:S(2)}, u32[]{:S(2)}) collective-permute-start(bf16[256,512]{1,0:T(8,128)(2,1)S(1)} %get-tuple-element.249), channel_id=1, source_target_pairs={{0,2},{1,3},{2,0},{3,1},{4,6},{5,7},{6,4},{7,5},{8,10},{9,11},{10,... | collective-permute-start | bytes 786440 | tf_op jit(solution)/shard_map/ppermute | solution.py:157
  433.8 19.0 %collective-permute-start.11 = (bf16[256,512]{1,0:T(8,128)(2,1)S(1)}, bf16[256,512]{1,0:T(8,128)(2,1)S(1)}, u32[]{:S(2)}, u32[]{:S(2)}) collective-permute-start(bf16[256,512]{1,0:T(8,128)(2,1)S(1)} %get-tuple-element.248), channel_id=1, source_target_pairs={{0,3},{1,0},{2,1},{3,2},{4,7},{5,4},{6,5},{7,6},{8,11},{9,8},{10,9... | collective-permute-start | bytes 786440 | tf_op jit(solution)/shard_map/ppermute | solution.py:157
  457.2 10.0 %copy-start.9 = (bf16[1,1024,4,128]{3,1,2,0:T(8,128)(2,1)}, bf16[1,1024,4,128]{3,1,2,0:T(8,128)(2,1)S(1)}, u32[]{:S(2)}) copy-start(bf16[1,1024,4,128]{3,1,2,0:T(8,128)(2,1)S(1)} %copy.138) | copy-start | bytes 3145732
  479.7 7.7 copy-start.10
  494.5 14.3 %copy-start.32 = (bf16[1024,1,512]{2,0,1:T(8,128)(2,1)S(1)}, bf16[1024,1,512]{2,0,1:T(8,128)(2,1)}, u32[]{:S(2)}) copy-start(bf16[1024,1,512]{2,0,1:T(8,128)(2,1)} %copy.100) | copy-start | bytes 3145732
  494.5 14.3 %copy-start.33 = (bf16[1024,1,512]{2,0,1:T(8,128)(2,1)S(1)}, bf16[1024,1,512]{2,0,1:T(8,128)(2,1)}, u32[]{:S(2)}) copy-start(bf16[1024,1,512]{2,0,1:T(8,128)(2,1)} %copy.101) | copy-start | bytes 3145732
  494.5 14.3 %copy-start.38 = (f32[1,2048]{1,0:T(1,128)S(1)}, f32[1,2048]{1,0:T(1,128)}, u32[]{:S(2)}) copy-start(f32[1,2048]{1,0:T(1,128)} %copy-done.37) | copy-start | bytes 24580
  508.7 261.1 %reduce-scatter.8.cloned.1.call-start = ((), (), s32[]{:S(2)}) async-start(), calls=%async_computation.9 | async-start | bytes 7077888 | tf_op jit(solution)/shard_map/reduce_scatter | solution.py:325
  520.6 255.6 %reduce-scatter.10.cloned.1.call-start = ((), (), s32[]{:S(2)}) async-start(), calls=%async_computation.10 | async-start | bytes 9437184 | tf_op jit(solution)/shard_map/reduce_scatter | solution.py:301
  530.4 252.1 %reduce-scatter.14.cloned.1.call-start = ((), (), s32[]{:S(2)}) async-start(), calls=%async_computation.12 | async-start | bytes 9437184 | tf_op jit(solution)/shard_map/reduce_scatter | solution.py:299
  544.6 335.1 %reduce-scatter.12.cloned.1.call-start = ((), (), s32[]{:S(2)}) async-start(), calls=%async_computation.11 | async-start | bytes 18874368 | tf_op jit(solution)/shard_map/reduce_scatter | solution.py:298
  575.2 96.9 %collective-permute-start.15 = (bf16[256,2048]{1,0:T(8,128)(2,1)}, bf16[256,2048]{1,0:T(8,128)(2,1)S(1)}, u32[]{:S(2)}, u32[]{:S(2)}) collective-permute-start(bf16[256,2048]{1,0:T(8,128)(2,1)} %get-tuple-element.226), channel_id=1, source_target_pairs={{0,1},{1,2},{2,3},{3,0},{4,5},{5,6},{6,7},{7,4},{8,9},{9,10},{10,1... | collective-permute-start | bytes 3145736 | tf_op jit(solution)/shard_map/ppermute | solution.py:157
  575.3 99.6 %collective-permute-start.16 = (bf16[256,2048]{1,0:T(8,128)(2,1)}, bf16[256,2048]{1,0:T(8,128)(2,1)}, u32[]{:S(2)}, u32[]{:S(2)}) collective-permute-start(bf16[256,2048]{1,0:T(8,128)(2,1)} %get-tuple-element.228), channel_id=1, source_target_pairs={{0,2},{1,3},{2,0},{3,1},{4,6},{5,7},{6,4},{7,5},{8,10},{9,11},{10,... | collective-permute-start | bytes 3145736 | tf_op jit(solution)/shard_map/ppermute | solution.py:157
  576.7 98.1 %collective-permute-start.17 = (bf16[256,2048]{1,0:T(8,128)(2,1)}, bf16[256,2048]{1,0:T(8,128)(2,1)}, u32[]{:S(2)}, u32[]{:S(2)}) collective-permute-start(bf16[256,2048]{1,0:T(8,128)(2,1)} %get-tuple-element.227), channel_id=1, source_target_pairs={{0,3},{1,0},{2,1},{3,2},{4,7},{5,4},{6,5},{7,6},{8,11},{9,8},{10,9... | collective-permute-start | bytes 3145736 | tf_op jit(solution)/shard_map/ppermute | solution.py:157
  579.7 93.3 %copy-start.4 = (bf16[1024,2048]{1,0:T(8,128)(2,1)S(1)}, bf16[1024,2048]{1,0:T(8,128)(2,1)}, u32[]{:S(2)}) copy-start(bf16[1024,2048]{1,0:T(8,128)(2,1)} %param.30) | copy-start | bytes 12582916
  579.7 62.3 %collective-permute-start.21 = (f32[2,256]{1,0:T(2,128)S(1)}, f32[2,256]{1,0:T(2,128)S(1)}, u32[]{:S(2)}, u32[]{:S(2)}) collective-permute-start(f32[2,256]{1,0:T(2,128)S(1)} %copy.125), channel_id=1, source_target_pairs={{0,1},{1,2},{2,3},{3,0},{4,5},{5,6},{6,7},{7,4},{8,9},{9,10},{10,1... | collective-permute-start | bytes 6152 | tf_op jit(solution)/shard_map/ppermute | solution.py:157
  581.6 89.1 %collective-permute-start.22 = (f32[2,256]{1,0:T(2,128)S(1)}, f32[2,256]{1,0:T(2,128)S(1)}, u32[]{:S(2)}, u32[]{:S(2)}) collective-permute-start(f32[2,256]{1,0:T(2,128)S(1)} %copy.125), channel_id=1, source_target_pairs={{0,2},{1,3},{2,0},{3,1},{4,6},{5,7},{6,4},{7,5},{8,10},{9,11},{10,... | collective-permute-start | bytes 6152 | tf_op jit(solution)/shard_map/ppermute | solution.py:157
  642.1 28.7 %collective-permute-start.23 = (f32[2,256]{1,0:T(2,128)S(1)}, f32[2,256]{1,0:T(2,128)S(1)}, u32[]{:S(2)}, u32[]{:S(2)}) collective-permute-start(f32[2,256]{1,0:T(2,128)S(1)} %copy.125), channel_id=1, source_target_pairs={{0,3},{1,0},{2,1},{3,2},{4,7},{5,4},{6,5},{7,6},{8,11},{9,8},{10,9... | collective-permute-start | bytes 6152 | tf_op jit(solution)/shard_map/ppermute | solution.py:157
  670.7 24.7 %collective-permute-start.12 = (bf16[256,2048]{1,0:T(8,128)(2,1)S(1)}, bf16[256,2048]{1,0:T(8,128)(2,1)S(1)}, u32[]{:S(2)}, u32[]{:S(2)}) collective-permute-start(bf16[256,2048]{1,0:T(8,128)(2,1)S(1)} %get-tuple-element.229), channel_id=1, source_target_pairs={{0,1},{1,2},{2,3},{3,0},{4,5},{5,6},{6,7},{7,4},{8,9},{9,10},{10,1... | collective-permute-start | bytes 3145736 | tf_op jit(solution)/shard_map/ppermute | solution.py:157
  670.7 91.2 %collective-permute-start.13 = (bf16[256,2048]{1,0:T(8,128)(2,1)S(1)}, bf16[256,2048]{1,0:T(8,128)(2,1)S(1)}, u32[]{:S(2)}, u32[]{:S(2)}) collective-permute-start(bf16[256,2048]{1,0:T(8,128)(2,1)S(1)} %get-tuple-element.231), channel_id=1, source_target_pairs={{0,2},{1,3},{2,0},{3,1},{4,6},{5,7},{6,4},{7,5},{8,10},{9,11},{10,... | collective-permute-start | bytes 3145736 | tf_op jit(solution)/shard_map/ppermute | solution.py:157
  672.2 89.8 %collective-permute-start.14 = (bf16[256,2048]{1,0:T(8,128)(2,1)S(1)}, bf16[256,2048]{1,0:T(8,128)(2,1)S(1)}, u32[]{:S(2)}, u32[]{:S(2)}) collective-permute-start(bf16[256,2048]{1,0:T(8,128)(2,1)S(1)} %get-tuple-element.230), channel_id=1, source_target_pairs={{0,3},{1,0},{2,1},{3,2},{4,7},{5,4},{6,5},{7,6},{8,11},{9,8},{10,9... | collective-permute-start | bytes 3145736 | tf_op jit(solution)/shard_map/ppermute | solution.py:157
  769.8 12.7 %copy-start.16 = (f32[2048,256]{1,0:T(8,128)S(1)}, f32[2048,256]{1,0:T(8,128)}, u32[]{:S(2)}) copy-start(f32[2048,256]{1,0:T(8,128)} %param.36) | copy-start | bytes 6291460
  778.2 11.7 %collective-permute-start.18 = (bf16[512,256]{1,0:T(8,128)(2,1)}, bf16[512,256]{1,0:T(8,128)(2,1)S(1)}, u32[]{:S(2)}, u32[]{:S(2)}) collective-permute-start(bf16[512,256]{1,0:T(8,128)(2,1)} %get-tuple-element.243), channel_id=1, source_target_pairs={{0,1},{1,2},{2,3},{3,0},{4,5},{5,6},{6,7},{7,4},{8,9},{9,10},{10,1... | collective-permute-start | bytes 786440 | tf_op jit(solution)/shard_map/ppermute | solution.py:157
  778.2 25.6 %collective-permute-start.19 = (bf16[512,256]{1,0:T(8,128)(2,1)}, bf16[512,256]{1,0:T(8,128)(2,1)}, u32[]{:S(2)}, u32[]{:S(2)}) collective-permute-start(bf16[512,256]{1,0:T(8,128)(2,1)} %get-tuple-element.245), channel_id=1, source_target_pairs={{0,2},{1,3},{2,0},{3,1},{4,6},{5,7},{6,4},{7,5},{8,10},{9,11},{10,... | collective-permute-start | bytes 786440 | tf_op jit(solution)/shard_map/ppermute | solution.py:157
  780.3 23.6 %copy-start.28 = (f32[512,256]{1,0:T(8,128)S(1)}, f32[512,256]{1,0:T(8,128)}, u32[]{:S(2)}) copy-start(f32[512,256]{1,0:T(8,128)} %param.34) | copy-start | bytes 1572868
  780.3 23.6 %copy-start.35 = (f32[512,256]{1,0:T(8,128)S(1)}, f32[512,256]{1,0:T(8,128)}, u32[]{:S(2)}) copy-start(f32[512,256]{1,0:T(8,128)} %param.39) | copy-start | bytes 1572868
  780.3 23.6 %collective-permute-start.20 = (bf16[512,256]{1,0:T(8,128)(2,1)}, bf16[512,256]{1,0:T(8,128)(2,1)}, u32[]{:S(2)}, u32[]{:S(2)}) collective-permute-start(bf16[512,256]{1,0:T(8,128)(2,1)} %get-tuple-element.244), channel_id=1, source_target_pairs={{0,3},{1,0},{2,1},{3,2},{4,7},{5,4},{6,5},{7,6},{8,11},{9,8},{10,9... | collective-permute-start | bytes 786440 | tf_op jit(solution)/shard_map/ppermute | solution.py:157
  782.5 21.3 %copy-start.36 = (f32[512,256]{1,0:T(8,128)S(1)}, f32[512,256]{1,0:T(8,128)}, u32[]{:S(2)}) copy-start(f32[512,256]{1,0:T(8,128)} %param.44) | copy-start | bytes 1572868
  (33 other events, 106.6 us)
Sparse Core Ops, SparseCore 0:
  10.5 47.6 all-gather.4
  60.6 55.9 all-gather.6
  119.1 89.8 all-gather.8
  211.3 55.9 all-gather.10
  508.9 35.9 reduce-scatter.15
  548.1 61.6 reduce-scatter.7
  613.7 71.2 reduce-scatter.9
  688.5 71.2 reduce-scatter.13
  763.8 115.9 reduce-scatter.11

commit v2 on v1

v2 whole, which is shorter than its diff:
```python
import functools
import math

import jax
import jax.numpy as jnp
from jax import lax
from jax.experimental import pallas as pl
from jax.experimental.pallas import tpu as pltpu
from jax.sharding import PartitionSpec as P

D = 2048
H = 16
HD = 128
FF = 8192
SEQ = 1024
STEP = 10
VMEM = 56 << 20


norm_eps = 1e-05
adam_eps = 1e-08
beta_first = 0.5
beta_second = 0.5
weight_decay = 0.1


def step_rates():
    return (
        0.8 / math.sqrt(D),
        0.8 / math.sqrt(max(1, 2 * H * HD // SEQ)),
        0.8 / math.sqrt(D),
        0.8 / math.sqrt(FF),
        0.4,
    )


def rope_tables():
    halfway = HD // 2
    inverse = jnp.exp(-math.log(10000.0) * jnp.arange(halfway, dtype=jnp.float32) * 2.0 / HD)
    angles = jnp.arange(SEQ, dtype=jnp.float32)[:, None] * inverse[None, :]
    return (jnp.cos(angles), jnp.sin(angles))


def norm_forward(values, gain):
    inverse = lax.rsqrt(jnp.mean(values * values, axis=-1, keepdims=True) + norm_eps)
    return (values * inverse * gain, inverse)


def norm_backward(values, inverse, gain, upstream):
    scaled = upstream * gain
    gain_grad = jnp.sum(upstream * values * inverse, axis=0)
    values_grad = inverse * scaled - values * inverse * inverse * inverse * jnp.mean(
        scaled * values, axis=-1, keepdims=True
    )
    return (values_grad, gain_grad)


def adamw(weight, moment_one, moment_two, gradient, step_rate):
    first_new = beta_first * moment_one + (1.0 - beta_first) * gradient
    second_new = beta_second * moment_two + (1.0 - beta_second) * gradient * gradient
    first_hat = first_new / (1.0 - beta_first**STEP)
    second_hat = second_new / (1.0 - beta_second**STEP)
    weight_new = weight - step_rate * (
        first_hat / (jnp.sqrt(second_hat) + adam_eps) + weight_decay * weight
    )
    return (weight_new, first_new, second_new)


CORE, ALONG_X, ALONG_Y = 1, 2, 4
DIAGONAL = ALONG_X + ALONG_Y


def flip(block, bits, name="dp"):
    return lax.ppermute(block, name, [(j, j ^ bits) for j in range(lax.axis_size(name))])


def pick(block, place, width, axis):
    return lax.dynamic_slice_in_dim(block, place * width, width, axis)


def gather_near(shard):
    if lax.axis_size("dp") != 8:
        return [lax.all_gather(shard, "dp", axis=1, tiled=True)], None
    from_x = flip(shard, ALONG_X)
    from_y = flip(shard, ALONG_Y)
    from_core = flip(shard, CORE)
    upper = flip(from_y[:1], ALONG_X)
    lower = flip(from_x[1:], ALONG_Y)
    near = [shard, from_core, from_x, from_y, flip(from_x, CORE), flip(from_y, CORE)]
    return near, (upper, lower)


def gather_far(near, halves, after):
    if halves is None:
        return near, [0]
    me = lax.axis_index("dp")
    upper, lower = halves
    far = jnp.concatenate([tie(upper, after), tie(lower, after)], axis=0)
    bits = [0, CORE, ALONG_X, ALONG_Y, ALONG_X + CORE, ALONG_Y + CORE, DIAGONAL, DIAGONAL + CORE]
    return near + [far, flip(far, CORE)], [me ^ b for b in bits]


def core_columns(block, core):
    width = block.shape[1] // 8
    return jnp.concatenate([pick(block, 2 * q + core, width, 1) for q in range(4)], axis=1)


def reduce_dp(products, sharded, axis, after=()):
    f32, bf16 = jnp.float32, jnp.bfloat16
    if lax.axis_size("dp") != 8:
        full = [part.astype(bf16) for part in products(sharded)]
        done = [lax.psum_scatter(part, "dp", scatter_dimension=axis, tiled=True) for part in full]
        return [part.astype(f32) for part in done], full
    me = lax.axis_index("dp")
    core = lax.rem(me, 2)
    chip = lax.div(me, 2)
    other = [part.astype(bf16) for part in products(core_columns(sharded, 1 - core))]
    other = [flip(part, CORE) for part in other]
    own = products(core_columns(sharded, core))
    total = [(a + b.astype(f32)).astype(bf16) for a, b in zip(own, other)]
    width = total[0].shape[axis] // 4
    upper = flip(pick(total[0], chip ^ 3, width, axis), ALONG_X)
    lower = flip(pick(total[1], chip ^ 3, width, axis), ALONG_Y)
    if after:
        upper, lower = tie(upper, *after), tie(lower, *after)
    near_x = [pick(part, chip ^ 1, width, axis) for part in total]
    near_y = [pick(part, chip ^ 2, width, axis) for part in total]
    to_x = jnp.stack([near_x[0], (near_x[1].astype(f32) + lower.astype(f32)).astype(bf16)])
    to_y = jnp.stack([(near_y[0].astype(f32) + upper.astype(f32)).astype(bf16), near_y[1]])
    from_x = flip(to_x, ALONG_X)
    from_y = flip(to_y, ALONG_Y)
    mine = [pick(part, chip, width, axis).astype(f32) for part in total]
    return [mine[k] + from_x[k].astype(f32) + from_y[k].astype(f32) for k in range(2)], total


def shift_all(take):
    size = lax.axis_size("mp")
    got = [take(0)]
    for k in range(1, size):
        got.append(lax.ppermute(take(k), "mp", [(j, (j + k) % size) for j in range(size)]))
    return got


def gather_line(block):
    size = lax.axis_size("mp")
    me = lax.axis_index("mp")
    if size != 4:
        parts = shift_all(lambda k: block)
        return parts, [lax.rem(me - k + size, size) for k in range(size)]
    from_low = lax.ppermute(block, "mp", [(0, 1), (1, 2), (2, 3)])
    from_high = lax.ppermute(block, "mp", [(1, 0), (2, 1), (3, 2)])
    inward = jnp.where(me == 1, from_low, from_high)
    outward = jnp.where(me == 1, from_high, from_low)
    end = lax.ppermute(inward, "mp", [(2, 0), (1, 3)])
    middle = lax.ppermute(inward, "mp", [(2, 1), (1, 2)])
    edge = lax.ppermute(outward, "mp", [(1, 0), (2, 3)])
    low, high = lax.rem(me + 3, 4), lax.rem(me + 1, 4)
    end_owner = jnp.where(me == 0, 3, jnp.where(me == 3, 0, me))
    return [block, from_low, from_high, end, middle + edge], [
        me,
        low,
        high,
        end_owner,
        lax.rem(me + 2, 4),
    ]


def sum_flips(block, name):
    bits = 1
    while bits < lax.axis_size(name):
        block = block + flip(block, bits, name)
        bits *= 2
    return block


def rotate_wide(block, cosine, sine):
    heads = block.shape[1] // HD
    parts = []
    for h in range(heads):
        head = block[:, h * HD : (h + 1) * HD]
        parts.append(head * cosine + pltpu.roll(head, HD // 2, 1) * sine)
    return parts[0] if heads == 1 else jnp.concatenate(parts, axis=1)


def project_kernel(normed_ref, weight_ref, cosine_ref, sine_ref, out_ref):
    rows = normed_ref.shape[0]
    step = min(1024, rows)
    for begin in range(0, rows, step):
        block = jnp.dot(
            normed_ref[begin : begin + step], weight_ref[...], preferred_element_type=jnp.float32
        )

        @pl.when(pl.program_id(0) < 2)
        def _(block=block, begin=begin):
            out_ref[begin : begin + step] = rotate_wide(
                block, cosine_ref[begin : begin + step], sine_ref[begin : begin + step]
            ).astype(out_ref.dtype)

        @pl.when(pl.program_id(0) == 2)
        def _(block=block, begin=begin):
            out_ref[begin : begin + step] = block.astype(out_ref.dtype)


def project_heads(normed, weight, cosine, sine):
    rows, width = normed.shape
    cols = weight.shape[1] // 3
    return pl.pallas_call(
        project_kernel,
        grid=(3,),
        in_specs=[
            pl.BlockSpec((rows, width), lambda c: (0, 0)),
            pl.BlockSpec((width, cols), lambda c: (0, c)),
            pl.BlockSpec((rows, HD), lambda c: (0, 0)),
            pl.BlockSpec((rows, HD), lambda c: (0, 0)),
        ],
        out_specs=pl.BlockSpec((rows, cols), lambda c: (0, c)),
        out_shape=jax.ShapeDtypeStruct((rows, 3 * cols), jnp.bfloat16),
        compiler_params=pltpu.CompilerParams(vmem_limit_bytes=VMEM),
        cost_estimate=pl.CostEstimate(flops=1, bytes_accessed=1, transcendentals=0),
    )(normed, weight, cosine, sine)


def transposed_dot(a, b):
    return lax.dot_general(a, b, (((1,), (1,)), ((), ())), preferred_element_type=jnp.float32)


def lead_dot(a, b):
    return lax.dot_general(a, b, (((0,), (0,)), ((), ())), preferred_element_type=jnp.float32)


def causal_sigmoid(scores_raw, begin):
    rows, cols = scores_raw.shape
    grown = jnp.exp(math.log(SEQ) - scores_raw * (1.0 / math.sqrt(HD)))
    sigmoid_val = 1.0 / (1.0 + grown)
    row_ids = begin + lax.broadcasted_iota(jnp.int32, (rows, rows), 0)
    col_ids = begin + lax.broadcasted_iota(jnp.int32, (rows, rows), 1)
    last = jnp.where(col_ids <= row_ids, sigmoid_val[:, cols - rows :], 0.0)
    if cols == rows:
        return last
    return jnp.concatenate([sigmoid_val[:, : cols - rows], last], axis=1)


def keep_valid(block, valid_len):
    ids = lax.broadcasted_iota(jnp.int32, block.shape, 0)
    return jnp.where(ids < valid_len, block, jnp.zeros_like(block))


def attend_kernel(lengths_ref, query_ref, key_ref, value_ref, out_ref):
    valid_len = lengths_ref[pl.program_id(0)]
    keys = key_ref[...]
    values = keep_valid(value_ref[...], valid_len)
    step = min(256, SEQ)
    for begin in range(0, SEQ, step):
        end = begin + step
        weights = causal_sigmoid(transposed_dot(query_ref[begin:end], keys[:end]), begin)
        out_ref[begin:end] = jnp.dot(
            weights.astype(jnp.bfloat16), values[:end], preferred_element_type=jnp.float32
        ).astype(out_ref.dtype)


def attend(lengths, heads_all):
    rows, width = heads_all.shape
    heads = width // 3 // HD

    def spec(part):
        return pl.BlockSpec((SEQ, HD), lambda s, h, *_: (s, part * heads + h))

    return pl.pallas_call(
        attend_kernel,
        grid_spec=pltpu.PrefetchScalarGridSpec(
            num_scalar_prefetch=1,
            grid=(rows // SEQ, heads),
            in_specs=[spec(0), spec(1), spec(2)],
            out_specs=pl.BlockSpec((SEQ, HD), lambda s, h, *_: (s, h)),
        ),
        out_shape=jax.ShapeDtypeStruct((rows, width // 3), jnp.bfloat16),
        compiler_params=pltpu.CompilerParams(vmem_limit_bytes=VMEM),
        cost_estimate=pl.CostEstimate(flops=1, bytes_accessed=1, transcendentals=0),
    )(lengths, heads_all, heads_all, heads_all)


def attend_back_kernel(
    heads,
    lengths_ref,
    query_ref,
    key_ref,
    value_ref,
    back_ref,
    cosine_ref,
    sine_ref,
    out_ref,
    key_total,
    value_total,
):
    valid_len = lengths_ref[pl.program_id(0)]
    head = pl.program_id(1)
    keys = key_ref[...]
    keys_kept = keep_valid(keys, valid_len)
    values = value_ref[...]
    key_total[...] = jnp.zeros_like(key_total)
    value_total[...] = jnp.zeros_like(value_total)
    step = min(256, SEQ)

    def column(part):
        return pl.ds(pl.multiple_of(part * heads * HD + head * HD, HD), HD)

    for begin in range(0, SEQ, step):
        end = begin + step
        queries = query_ref[begin:end]
        back = back_ref[begin:end]
        weights = causal_sigmoid(transposed_dot(queries, keys[:end]), begin)
        value_total[:end] += lead_dot(weights.astype(jnp.bfloat16), back)
        weight_back = transposed_dot(back, values[:end])
        score_back = (weight_back * (weights * (1.0 - weights))).astype(jnp.bfloat16)
        query_back = jnp.dot(
            score_back, keys_kept[:end], preferred_element_type=jnp.float32
        ) * (1.0 / math.sqrt(HD))
        key_total[:end] += lead_dot(score_back, queries)
        out_ref[begin:end, column(0)] = rotate_wide(
            query_back, cosine_ref[begin:end], sine_ref[begin:end]
        ).astype(out_ref.dtype)
    key_back = keep_valid(key_total[...] * (1.0 / math.sqrt(HD)), valid_len)
    out_ref[:, column(1)] = rotate_wide(key_back, cosine_ref[...], sine_ref[...]).astype(
        out_ref.dtype
    )
    out_ref[:, column(2)] = keep_valid(value_total[...], valid_len).astype(out_ref.dtype)


def attend_back(lengths, heads_all, mixed_back, cosine, sine):
    rows, width = heads_all.shape
    heads = width // 3 // HD

    def spec(part):
        return pl.BlockSpec((SEQ, HD), lambda s, h, *_: (s, part * heads + h))

    table = pl.BlockSpec((SEQ, HD), lambda s, h, *_: (0, 0))
    return pl.pallas_call(
        functools.partial(attend_back_kernel, heads),
        grid_spec=pltpu.PrefetchScalarGridSpec(
            num_scalar_prefetch=1,
            grid=(rows // SEQ, heads),
            in_specs=[spec(0), spec(1), spec(2), spec(0), table, table],
            out_specs=pl.BlockSpec((SEQ, width), lambda s, h, *_: (s, 0)),
            scratch_shapes=[pltpu.VMEM((SEQ, HD), jnp.float32), pltpu.VMEM((SEQ, HD), jnp.float32)],
        ),
        out_shape=jax.ShapeDtypeStruct((rows, width), jnp.bfloat16),
        compiler_params=pltpu.CompilerParams(vmem_limit_bytes=VMEM),
        cost_estimate=pl.CostEstimate(flops=1, bytes_accessed=1, transcendentals=0),
    )(lengths, heads_all, heads_all, heads_all, mixed_back, cosine, sine)


def feed_kernel(
    count,
    places_ref,
    normed_ref,
    back_ref,
    down_ref,
    *rest,
):
    pieces = rest[:count]
    hidden_ref, pair_back_ref, total_ref, total, pair, arrived = rest[count:]
    rows = normed_ref.shape[0]
    cols = down_ref.shape[0]
    depth = pieces[0].shape[1]
    now = pl.program_id(0)
    first = now == 0
    last = now == pl.num_programs(0) - 1

    def copies(step, slot):
        columns = pl.ds(pl.multiple_of(step * cols, cols), cols)
        return [
            pltpu.make_async_copy(
                piece.at[:, :, columns],
                pair.at[slot, :, pl.ds(pl.multiple_of(places_ref[n] * depth, depth), depth), :],
                arrived.at[slot, n],
            )
            for n, piece in enumerate(pieces)
        ]

    @pl.when(first)
    def _():
        for copy in copies(0, 0):
            copy.start()

    slot = lax.rem(now, 2)
    for copy in copies(now, slot):
        copy.wait()

    @pl.when(now < pl.num_programs(0) - 1)
    def _():
        for copy in copies(now + 1, 1 - slot):
            copy.start()

    step = min(1024, rows)
    for begin in range(0, rows, step):
        span = slice(begin, begin + step)
        normed = normed_ref[span]
        gate = jnp.dot(normed, pair[slot, 0], preferred_element_type=jnp.float32)
        up = jnp.dot(normed, pair[slot, 1], preferred_element_type=jnp.float32)
        hidden_back = transposed_dot(back_ref[span], down_ref[...])
        gate_sig = 1.0 / (1.0 + jnp.exp(-gate))
        silu = gate * gate_sig
        hidden_ref[span] = (silu * up).astype(hidden_ref.dtype)
        gate_back = (hidden_back * up * (gate_sig * (1.0 + gate * (1.0 - gate_sig)))).astype(
            jnp.bfloat16
        )
        up_back = (hidden_back * silu).astype(jnp.bfloat16)
        pair_back_ref[0, span] = gate_back
        pair_back_ref[1, span] = up_back
        part = transposed_dot(gate_back, pair[slot, 0]) + transposed_dot(up_back, pair[slot, 1])
        part = jnp.where(first, part, total[span] + part)
        total[span] = part

        @pl.when(last)
        def _(part=part, span=span):
            total_ref[span] = part.astype(total_ref.dtype)


def feed_forward(normed_two, cotangent, pieces, places, down_weight):
    rows, width = normed_two.shape
    hidden = down_weight.shape[0]
    cols = min(512, hidden)
    whole = pl.BlockSpec((rows, width), lambda j, *_: (0, 0), pipeline_mode=pl.Buffered(1))
    return pl.pallas_call(
        functools.partial(feed_kernel, len(pieces)),
        grid_spec=pltpu.PrefetchScalarGridSpec(
            num_scalar_prefetch=1,
            grid=(hidden // cols,),
            in_specs=[whole, whole, pl.BlockSpec((cols, width), lambda j, *_: (j, 0))]
            + [pl.BlockSpec(memory_space=pl.ANY)] * len(pieces),
            out_specs=[
                pl.BlockSpec((rows, cols), lambda j, *_: (0, j)),
                pl.BlockSpec((2, rows, cols), lambda j, *_: (0, 0, j)),
                pl.BlockSpec((rows, width), lambda j, *_: (0, 0), pipeline_mode=pl.Buffered(1)),
            ],
            scratch_shapes=[
                pltpu.VMEM((rows, width), jnp.float32),
                pltpu.VMEM((2, 2, width, cols), jnp.bfloat16),
                pltpu.SemaphoreType.DMA((2, len(pieces))),
            ],
        ),
        out_shape=[
            jax.ShapeDtypeStruct((rows, hidden), jnp.bfloat16),
            jax.ShapeDtypeStruct((2, rows, hidden), jnp.bfloat16),
            jax.ShapeDtypeStruct((rows, width), jnp.bfloat16),
        ],
        compiler_params=pltpu.CompilerParams(vmem_limit_bytes=VMEM),
        cost_estimate=pl.CostEstimate(flops=1, bytes_accessed=1, transcendentals=0),
    )(jnp.stack(places).astype(jnp.int32), normed_two, cotangent, down_weight, *pieces)


def middle_kernel(count, owners_ref, tokens_ref, gain_ref, out_ref, *rest):
    middle_ref, normed_ref = rest[count:]
    depth = rest[0].shape[1]
    middle = tokens_ref[...].astype(jnp.float32)
    for n, part_ref in enumerate(rest[:count]):
        rows_of = pl.ds(pl.multiple_of(owners_ref[n] * depth, depth), depth)
        middle += jnp.dot(part_ref[...], out_ref[rows_of, :], preferred_element_type=jnp.float32)
    middle_ref[...] = middle
    inverse = lax.rsqrt(jnp.mean(middle * middle, axis=-1, keepdims=True) + norm_eps)
    normed_ref[...] = (middle * inverse * gain_ref[...]).astype(normed_ref.dtype)


def finish_middle(parts, owners, out_weight, tokens, gain):
    rows, width = tokens.shape
    depth = parts[0].shape[1]
    count = len(parts)
    step = min(512, rows)

    def by_rows(cols):
        return pl.BlockSpec((step, cols), lambda i, *_: (i, 0))

    return pl.pallas_call(
        functools.partial(middle_kernel, count),
        grid_spec=pltpu.PrefetchScalarGridSpec(
            num_scalar_prefetch=1,
            grid=(rows // step,),
            in_specs=[
                by_rows(width),
                pl.BlockSpec((1, width), lambda i, *_: (0, 0)),
                pl.BlockSpec(out_weight.shape, lambda i, *_: (0, 0), pipeline_mode=pl.Buffered(1)),
            ]
            + [by_rows(depth)] * count,
            out_specs=[by_rows(width), by_rows(width)],
        ),
        out_shape=[
            jax.ShapeDtypeStruct((rows, width), jnp.float32),
            jax.ShapeDtypeStruct((rows, width), jnp.bfloat16),
        ],
        compiler_params=pltpu.CompilerParams(vmem_limit_bytes=VMEM),
        cost_estimate=pl.CostEstimate(flops=1, bytes_accessed=1, transcendentals=0),
    )(jnp.stack(owners).astype(jnp.int32), tokens, gain, out_weight, *parts)


def tie(value, *others):
    def kernel(*refs):
        pass

    return pl.pallas_call(
        kernel,
        in_specs=[pl.BlockSpec(memory_space=pl.ANY)] * (1 + len(others)),
        out_specs=pl.BlockSpec(memory_space=pl.ANY),
        out_shape=jax.ShapeDtypeStruct(value.shape, value.dtype),
        input_output_aliases={0: 0},
    )(value, *others)


def local(
    tokens,
    cotangent,
    lengths,
    qkv_weight,
    out_weight,
    gate_up_weight,
    down_weight,
    norm_gains,
    qkv_first,
    out_first,
    gate_up_first,
    down_first,
    gains_first,
    qkv_second,
    out_second,
    gate_up_second,
    down_second,
    gains_second,
):
    bf16 = jnp.bfloat16
    f32 = jnp.float32
    size = lax.axis_size("mp")
    me = lax.axis_index("mp")
    head_cols = qkv_weight.shape[2]
    row_count = tokens.shape[0] // size
    row_start = me * row_count

    def own_rows(block):
        return lax.dynamic_slice_in_dim(block, row_start, row_count, 0)

    def gather(shard, axis):
        return lax.all_gather(shard, "dp", axis=axis, tiled=True)

    qkv_low = qkv_weight.astype(bf16).reshape(qkv_weight.shape[0], -1)
    qkv_full = gather(qkv_low, 0)
    gain_low = gather(norm_gains.astype(bf16), 1)
    out_low = out_weight.astype(bf16)
    out_parts = shift_all(lambda k: out_low)
    out_rows = jnp.zeros((size,) + out_weight.shape, bf16)
    for k in range(size):
        out_rows = lax.dynamic_update_index_in_dim(
            out_rows, out_parts[k], lax.rem(me - k + size, size), 0
        )
    out_full = gather(out_rows.reshape(-1, out_weight.shape[1]), 1)
    pair_low = tie(gate_up_weight.astype(bf16).transpose(1, 0, 2), qkv_full)
    near, halves = gather_near(pair_low)
    down_full = gather(down_weight.astype(bf16), 1)

    cosine, sine_table = rope_tables()
    cosine_wide = jnp.concatenate([cosine, cosine], axis=1)
    sine_wide = jnp.concatenate([-sine_table, sine_table], axis=1)
    gain_one = gain_low[0].astype(f32)
    gain_two = gain_low[1].astype(f32)
    normed, scale_one = norm_forward(tokens.astype(f32), gain_one)
    normed_bf = lax.optimization_barrier(normed.astype(bf16))
    heads_all = project_heads(normed_bf, qkv_full, cosine_wide, sine_wide)
    mixed_bf = attend(lengths, heads_all)
    parts, owners = gather_line(mixed_bf)
    mixed_own = jnp.zeros((row_count, size, head_cols), bf16)
    for part, owner in zip(parts[1:] + parts[:1], owners[1:] + owners[:1]):
        mixed_own = lax.dynamic_update_slice_in_dim(mixed_own, own_rows(part)[:, None], owner, 1)
    mixed_own = mixed_own.reshape(row_count, size * head_cols)
    middle, normed_two = finish_middle(parts, owners, out_full, tokens, gain_two[None])

    pieces, places = gather_far(near, halves, normed_two)
    hidden, pair_back, two_back_part = feed_forward(
        normed_two, cotangent, pieces, places, down_full
    )
    two_back = lax.psum_scatter(two_back_part, "mp", scatter_dimension=0, tiled=True)
    feed_part = jnp.dot(hidden, down_full, preferred_element_type=f32).astype(bf16)
    pair_red, pair_total = reduce_dp(
        lambda columns: [lead_dot(columns, pair_back[k]) for k in range(2)], normed_two, 0
    )
    half = hidden.shape[1] // 2
    down_red, down_total = reduce_dp(
        lambda columns: [lead_dot(hidden[:, k * half : (k + 1) * half], columns) for k in range(2)],
        cotangent,
        1,
    )
    two_back = two_back.astype(f32)

    middle_own = own_rows(middle)
    _, scale_two = norm_forward(middle_own, gain_two)
    middle_back, gain_two_grad = norm_backward(middle_own, scale_two, gain_two, two_back)
    middle_back = middle_back + own_rows(cotangent).astype(f32)
    middle_low = middle_back.astype(bf16)
    mixed_back = jnp.einsum("nd,ad->na", middle_low, out_full, preferred_element_type=f32).astype(
        bf16
    )
    back_parts = shift_all(lambda k: pick(mixed_back, lax.rem(me + k, size), head_cols, 1))
    mixed_heads = jnp.zeros((size, row_count, head_cols), bf16)
    for k in range(size):
        mixed_heads = lax.dynamic_update_index_in_dim(
            mixed_heads, back_parts[k], lax.rem(me - k + size, size), 0
        )
    feed_part = tie(feed_part, *back_parts)
    feed_out = lax.psum_scatter(feed_part, "mp", scatter_dimension=0, tiled=True)
    half = mixed_own.shape[1] // 2
    out_red, out_total = reduce_dp(
        lambda columns: [
            lead_dot(mixed_own[:, k * half : (k + 1) * half], columns) for k in range(2)
        ],
        middle_low,
        1,
    )
    out_red = jnp.concatenate(out_red, axis=0).astype(bf16)
    out_sum = shift_all(lambda k: pick(out_red, lax.rem(me + k, size), head_cols, 0))
    out_sum = sum(part.astype(f32) for part in out_sum)
    mixed_heads = tie(mixed_heads.reshape(-1, head_cols), *out_total)

    project_back = attend_back(
        lengths, heads_all, mixed_heads, cosine_wide, -sine_wide
    )
    one_back_part = transposed_dot(project_back, qkv_full).astype(bf16)
    one_back = lax.psum_scatter(tie(one_back_part, feed_out), "mp", scatter_dimension=0, tiled=True).astype(f32)
    gain_one_grad = jnp.sum(one_back_part.astype(f32) * tokens.astype(f32) * scale_one, axis=0)
    half = project_back.shape[1] // 2
    qkv_red, _ = reduce_dp(
        lambda columns: [
            lead_dot(columns, project_back[:, k * half : (k + 1) * half]) for k in range(2)
        ],
        tie(normed_bf, one_back_part),
        0,
    )
    qkv_red = jnp.concatenate(qkv_red, axis=1)
    qkv_grad = tie(
        jnp.stack([qkv_red[:, c * head_cols : (c + 1) * head_cols] for c in range(3)])
    ).transpose(1, 0, 2)
    gains_sum = sum_flips(jnp.stack([gain_one_grad, gain_two_grad]), "dp")
    gains_sum = pick(gains_sum, lax.axis_index("dp"), norm_gains.shape[1], 1)
    gains_red = sum_flips(gains_sum, "mp")

    tokens_part, _ = norm_backward(
        own_rows(tokens).astype(f32), own_rows(scale_one), gain_one, one_back
    )
    tokens_grad = tokens_part + middle_back
    block_out = (middle_own + feed_out.astype(f32)).astype(bf16)
    rates = step_rates()
    pair_grad = tie(jnp.stack(pair_red, axis=1))
    qkv_all = adamw(qkv_weight, qkv_first, qkv_second, qkv_grad, rates[0])
    out_all = adamw(out_weight, out_first, out_second, out_sum, rates[1])
    gate_up_all = adamw(gate_up_weight, gate_up_first, gate_up_second, pair_grad, rates[2])
    down_all = adamw(down_weight, down_first, down_second, jnp.concatenate(down_red, axis=0), rates[3])
    gains_all = adamw(norm_gains, gains_first, gains_second, gains_red, rates[4])
    states = (qkv_all, out_all, gate_up_all, down_all, gains_all)
    return (block_out, tokens_grad) + tuple(state[j] for j in range(3) for state in states)


def solution(mesh):
    in_specs = (
        P("dp", None),
        P("dp", None),
        P("dp"),
        P("dp", None, "mp"),
        P("mp", "dp"),
        P("dp", None, "mp"),
        P("mp", "dp"),
        P(None, "dp"),
        P("dp", None, "mp"),
        P("mp", "dp"),
        P("dp", None, "mp"),
        P("mp", "dp"),
        P(None, "dp"),
        P("dp", None, "mp"),
        P("mp", "dp"),
        P("dp", None, "mp"),
        P("mp", "dp"),
        P(None, "dp"),
    )
    out_specs = (
        P(("dp", "mp"), None),
        P(("dp", "mp"), None),
        P("dp", None, "mp"),
        P("mp", "dp"),
        P("dp", None, "mp"),
        P("mp", "dp"),
        P(None, "dp"),
        P("dp", None, "mp"),
        P("mp", "dp"),
        P("dp", None, "mp"),
        P("mp", "dp"),
        P(None, "dp"),
        P("dp", None, "mp"),
        P("mp", "dp"),
        P("dp", None, "mp"),
        P("mp", "dp"),
        P(None, "dp"),
    )
    return jax.shard_map(local, mesh=mesh, in_specs=in_specs, out_specs=out_specs, check_vma=False)
```

time: 922 us -> 630 us (0.68)
  waiting for transfers between devices: 458 us -> 192 us
  matrix products: 233 us -> 95.8 us
  Pallas kernels: 0 us -> 113 us
  other arithmetic: 70.5 us -> 94 us
  local copies, waits for them, and re-layouts: 79.2 us -> 56 us
    ppermute x24 -> x51, waiting for transfers between devices: 348 us -> 192 us  [the longest x37 79.8 us: flip(): lax.ppermute(block, name, [(j, j ^ bits) for j in range(lax.axis_size(nam...]
    dot_general x26 -> x18, matrix products: 226 us -> 89.9 us  [the longest x16 68.2 us: lead_dot(): lax.dot_general(a, b, (((0,), (0,)), ((), ())), preferred_element_type=jn...]
    pallas_call x0 -> x14, Pallas kernels: none -> 113 us  [the longest x1 56.3 us: feed_forward(): pl.pallas_call(functools.partial(feed_kernel, len(pieces)), grid_spec=plt...]
    reduce_scatter x4 -> x3, waiting for transfers between devices: 73.3 us -> 0.02 us  [the longest x1 0.01 us: local(): lax.psum_scatter(feed_part, 'mp', scatter_dimension=0, tiled=True)]
    all_gather x4 -> x3, waiting for transfers between devices: 36.6 us -> 0.02 us  [gather(): return lax.all_gather(shard, 'dp', axis=axis, tiled=True)]
    another operation x2 -> x22, other arithmetic: 2.78 us -> 25.5 us  [the longest x2 12.1 us: local(): pair_grad = tie(jnp.stack(pair_red, axis=1))]
    unnamed x103 -> x154, local copies, waits for them, and re-layouts: 34.3 us -> 16.7 us
    ppermute x24 -> x51, starting transfers between devices: 50.5 us -> 49.1 us  [the longest x37 30.1 us: flip(): lax.ppermute(block, name, [(j, j ^ bits) for j in range(lax.axis_size(nam...]
  transfers between devices with their start and end apart: 33 -> 57, of which waited for: 14 -> 18; matrix products, arithmetic and copies ran while one was open for 25% -> 36% of each run, Pallas kernels for 0% -> 9%
where the time goes in v2:
time: 630 us; the launch traced here: 625 us
  waiting for transfers between devices  192 us (30%)
  Pallas kernels  113 us (18%)
  matrix products  95.8 us (15%)
  other arithmetic  94 us (15%)
  local copies, waits for them, and re-layouts  56 us (9%)
  starting transfers between devices  49.8 us (8%)
  between operations  16.3 us (3%)
  blocking collectives  9.03 us (1%)
    ppermute x37, waiting for transfers between devices, flip(): lax.ppermute(block, name, [(j, j ^ bits) for j in range(lax.axis_size(nam...  79.8 us
    dot_general x16, matrix products, lead_dot(): lax.dot_general(a, b, (((0,), (0,)), ((), ())), preferred_element_type=jn...  68.2 us
    ppermute x9, waiting for transfers between devices, shift_all(): lax.ppermute(take(k), 'mp', [(j, (j + k) % size) for j in range(size)])  61.7 us
    pallas_call x1, Pallas kernels, feed_forward(): pl.pallas_call(functools.partial(feed_kernel, len(pieces)), grid_spec=plt...  56.3 us
    ppermute x37, starting transfers between devices, flip(): lax.ppermute(block, name, [(j, j ^ bits) for j in range(lax.axis_size(nam...  30.1 us
    sub x5, other arithmetic, adamw(): weight - step_rate * (first_hat / (jnp.sqrt(second_hat) + adam_eps) + wei...  28.2 us
    ppermute x1, waiting for transfers between devices, gather_line(): edge = lax.ppermute(outward, 'mp', [(1, 0), (2, 3)])  27.8 us
    ppermute x1, waiting for transfers between devices, gather_line(): from_low = lax.ppermute(block, 'mp', [(0, 1), (1, 2), (2, 3)])  21 us
  transfers between devices with their start and end apart: 57, of which 18 were waited for; matrix products, arithmetic and copies ran while one was open for 36% of the time, Pallas kernels for 9%

profile of v2, /device:TPU:26, one launch (start us, length us, event | category | flops | bytes accessed | tf_op | source)
XLA Modules:
  0.0 625.4 jit_solution(3536891389731499038)
XLA Ops:
  14.5 6.4 %collective-permute-done = bf16[512,256]{1,0:T(8,128)(2,1)} collective-permute-done((bf16[512,256]{1,0:T(8,128)(2,1)}, bf16[512,256]{1,0:T(8,128)(2,1)}, u32[]{:S(2)}, u32[]{:S(2)}) %collective-permute-start) | collective-permute-done | bytes 262176 | tf_op jit(solution)/shard_map/ppermute | solution.py:140
  21.9 15.4 %collective-permute-done.1 = bf16[512,256]{1,0:T(8,128)(2,1)} collective-permute-done((bf16[512,256]{1,0:T(8,128)(2,1)}, bf16[512,256]{1,0:T(8,128)(2,1)}, u32[]{:S(2)}, u32[]{:S(2)}) %collective-permute-start.1) | collective-permute-done | bytes 262176 | tf_op jit(solution)/shard_map/ppermute | solution.py:140
  40.5 5.9 copy.71
  46.5 9.0 %all_gather.12 = bf16[2,2048]{1,0:T(2,128)(2,1)S(1)} all-gather(bf16[2,256]{1,0:T(2,128)(2,1)S(1)} %convert_element_type.338), channel_id=1, replica_groups=mesh['dp'=8,'mp'=4] {'dp'}, dimensions={1}, use_global_device_ids=true | all-gather | bytes 9216 | tf_op jit(solution)/shard_map/all_gather | solution.py:540
  59.0 5.2 fusion.2.normed_ref.refs_0_
  68.4 12.8 %shard_map.305.query_ref.key_ref.value_ref = bf16[1024,1536]{1,0:T(8,128)(2,1)} custom-call(bf16[1024,2048]{1,0:T(8,128)(2,1)} %fusion.2.normed_ref.refs_0_, bf16[2048,1536]{1,0:T(8,128)(2,1)} %all-gather.6.cloned.1.call-done.weight_ref.refs_1_, f32[1024,128]{1,0:T(8,128)} %get-tuple-element.126.cosine_ref, f32[1024,128]{1,0:T(8,128)} %get-tuple-element.45.sine_ref), custom_call_target="tpu_custom_call" | custom-call | flops 1 | bytes 1 | tf_op jit(solution)/shard_map/pallas_call | solution.py:207
  81.2 7.1 %shard_map.306.rest_0_ = bf16[1024,512]{1,0:T(8,128)(2,1)} custom-call(s32[1]{0:T(128)S(6)} %copy.94.lengths_ref, bf16[1024,1536]{1,0:T(8,128)(2,1)} %shard_map.305.query_ref.key_ref.value_ref, bf16[1024,1536]{1,0:T(8,128)(2,1)} %shard_map.305.query_ref.key_ref.value_ref, bf16[1024,1536]{1,0:T(8,128)(2,1)} %shard_map.305.query_ref.key_ref.value_ref), custom_call_target="tpu_custom_call" | custom-call | flops 1 | bytes 1 | tf_op jit(solution)/shard_map/pallas_call | solution.py:268
  89.5 4.6 collective-permute-start.4
  94.1 21.0 %collective-permute-done.3.rest_1_ = bf16[1024,512]{1,0:T(8,128)(2,1)S(1)} collective-permute-done((bf16[1024,512]{1,0:T(8,128)(2,1)}, bf16[1024,512]{1,0:T(8,128)(2,1)S(1)}, u32[]{:S(2)}, u32[]{:S(2)}) %collective-permute-start.3) | collective-permute-done | bytes 1048608 | tf_op jit(solution)/shard_map/ppermute | solution.py:150
  122.7 9.9 %collective-permute-done.10.rest_3_ = bf16[2,256,2048]{2,1,0:T(8,128)(2,1)} collective-permute-done((bf16[2,256,2048]{2,1,0:T(8,128)(2,1)}, bf16[2,256,2048]{2,1,0:T(8,128)(2,1)}, u32[]{:S(2)}, u32[]{:S(2)}) %collective-permute-start.10) | collective-permute-done | bytes 2097184 | tf_op jit(solution)/shard_map/ppermute | solution.py:74
  140.8 27.8 %collective-permute-done.7 = bf16[1024,512]{1,0:T(8,128)(2,1)} collective-permute-done((bf16[1024,512]{1,0:T(8,128)(2,1)}, bf16[1024,512]{1,0:T(8,128)(2,1)}, u32[]{:S(2)}, u32[]{:S(2)}) %collective-permute-start.7) | collective-permute-done | bytes 1048608 | tf_op jit(solution)/shard_map/ppermute | solution.py:156
  171.9 20.6 %shard_map.307 = (f32[1024,2048]{1,0:T(8,128)}, bf16[1024,2048]{1,0:T(8,128)(2,1)}) custom-call(s32[5]{0:T(128)} %stack.152.owners_ref, bf16[1024,2048]{1,0:T(8,128)(2,1)} %tokens_ref.1, f32[1,2048]{1,0:T(1,128)} %get-tuple-element.120.gain_ref, bf16[2048,2048]{1,0:T(8,128)(2,1)} %all-gather.4.cloned.1.call-done.out_ref, ...), custom_call_target="tpu_custom_call" | custom-call | flops 1 | bytes 1 | tf_op jit(solution)/shard_map/pallas_call | solution.py:473
  198.8 4.3 constant_dynamic-slice_fusion.11
  208.7 4.1 constant_dynamic-slice_fusion.21
  212.9 56.3 %shard_map.311 = (bf16[1024,2048]{1,0:T(8,128)(2,1)}, bf16[2,1024,2048]{2,1,0:T(8,128)(2,1)}, bf16[1024,2048]{1,0:T(8,128)(2,1)}) custom-call(s32[8]{0:T(128)} %stack.161.places_ref, bf16[1024,2048]{1,0:T(8,128)(2,1)} %get-tuple-element.23.refs_1_.normed_ref, bf16[1024,2048]{1,0:T(8,128)(2,1)} %back_ref.1, ...), custom_call_target="tpu_custom_call" | custom-call | flops 1 | bytes 1 | tf_op jit(solution)/shard_map/pallas_call | solution.py:424
  270.8 5.5 convolution_convert_fusion.3
  276.7 6.6 %fusion.17 = bf16[1024,2048]{1,0:T(8,128)(2,1)} fusion(bf16[2,1024,2048]{2,1,0:T(8,128)(2,1)S(1)} %copy-done.70, bf16[1024,256]{1,0:T(8,128)(2,1)S(1)} %copy-done.58, bf16[1024,256]{1,0:T(8,128)(2,1)S(1)} %copy-done.59, bf16[1024,256]{1,0:T(8,128)(2,1)S(1)} %copy-done.60, bf16[1024,256]{1,0:T(8,128)(2,1)S(1)} %copy-done.61), kind=kOutput, calls=%fused_computation.31 | convolution fusion | flops 4305453056 | bytes 10485760 | tf_op jit(solution)/shard_map/dot_general | solution.py:228
  283.4 3.7 convolution_convert_fusion.4
  287.6 6.3 %fusion.14 = bf16[1024,2048]{1,0:T(8,128)(2,1)} fusion(bf16[2,1024,2048]{2,1,0:T(8,128)(2,1)S(1)} %copy-done.70, bf16[1024,256]{1,0:T(8,128)(2,1)S(1)} %copy-done.58, bf16[1024,256]{1,0:T(8,128)(2,1)S(1)} %copy-done.59, bf16[1024,256]{1,0:T(8,128)(2,1)S(1)} %copy-done.60, bf16[1024,256]{1,0:T(8,128)(2,1)S(1)} %copy-done.61), kind=kOutput, calls=%fused_computation.30 | convolution fusion | flops 4305453056 | bytes 10485760 | tf_op jit(solution)/shard_map/dot_general | solution.py:228
  297.7 4.8 add_convert_fusion.2
  303.7 4.0 add_convert_fusion.3
  309.1 7.8 %collective-permute-done.42 = bf16[1024,256]{1,0:T(8,128)(2,1)S(1)} collective-permute-done((bf16[1024,256]{1,0:T(8,128)(2,1)S(1)}, bf16[1024,256]{1,0:T(8,128)(2,1)S(1)}, u32[]{:S(2)}, u32[]{:S(2)}) %collective-permute-start.42) | collective-permute-done | bytes 524320 | tf_op jit(solution)/shard_map/ppermute | solution.py:74
  319.0 8.0 %add_convert_fusion = bf16[1024,2048]{1,0:T(8,128)(2,1)S(1)} fusion(bf16[1024,2048]{1,0:T(8,128)(2,1)} %collective-permute-done.35, bf16[2,1024,2048]{2,1,0:T(8,128)(2,1)} %get-tuple-element.26, bf16[1024,256]{1,0:T(8,128)(2,1)S(1)} %copy-done.43, bf16[1024,256]{1,0:T(8,128)(2,1)S(1)} %copy-done.44, bf16[1024,256]{1,0:T(8,128)(2,1)S(1)} %copy-done.45, ...), kind=kOutput, calls=%fused_computation.8 | convolution fusion | flops 4309647360 | bytes 14680064 | tf_op jit(solution)/shard_map/dot_general | solution.py:228
  328.6 8.2 %add_convert_fusion.1 = bf16[1024,2048]{1,0:T(8,128)(2,1)S(1)} fusion(bf16[1024,2048]{1,0:T(8,128)(2,1)} %collective-permute-done.34, bf16[2,1024,2048]{2,1,0:T(8,128)(2,1)} %get-tuple-element.26, bf16[1024,256]{1,0:T(8,128)(2,1)S(1)} %copy-done.43, bf16[1024,256]{1,0:T(8,128)(2,1)S(1)} %copy-done.44, bf16[1024,256]{1,0:T(8,128)(2,1)S(1)} %copy-done.45, ...), kind=kOutput, calls=%fused_computation.9 | convolution fusion | flops 4309647360 | bytes 14680064 | tf_op jit(solution)/shard_map/dot_general | solution.py:228
  340.4 12.9 %collective-permute-done.36 = bf16[256,2048]{1,0:T(8,128)(2,1)S(1)} collective-permute-done((bf16[256,2048]{1,0:T(8,128)(2,1)S(1)}, bf16[256,2048]{1,0:T(8,128)(2,1)S(1)}, u32[]{:S(2)}, u32[]{:S(2)}) %collective-permute-start.36) | collective-permute-done | bytes 1048608 | tf_op jit(solution)/shard_map/ppermute | solution.py:74
  356.5 11.1 %collective-permute-done.38 = bf16[256,2048]{1,0:T(8,128)(2,1)S(1)} collective-permute-done((bf16[256,2048]{1,0:T(8,128)(2,1)S(1)}, bf16[256,2048]{1,0:T(8,128)(2,1)S(1)}, u32[]{:S(2)}, u32[]{:S(2)}) %collective-permute-start.38) | collective-permute-done | bytes 1048608 | tf_op jit(solution)/shard_map/ppermute | solution.py:74
  374.7 5.9 convolution_convert_fusion.2
  384.8 5.3 collective-permute-done.16.refs_2_
  391.2 6.7 %collective-permute-done.17.refs_3_ = bf16[256,512]{1,0:T(8,128)(2,1)S(1)} collective-permute-done((bf16[256,512]{1,0:T(8,128)(2,1)S(1)}, bf16[256,512]{1,0:T(8,128)(2,1)S(1)}, u32[]{:S(2)}, u32[]{:S(2)}) %collective-permute-start.17) | collective-permute-done | bytes 262176 | tf_op jit(solution)/shard_map/ppermute | solution.py:140
  399.7 10.4 %convolution_convert_fusion.1.refs_0_ = bf16[1024,2048]{1,0:T(8,128)(2,1)} fusion(bf16[1024,2048]{1,0:T(8,128)(2,1)S(1)} %copy-done.73, bf16[2048,2048]{1,0:T(8,128)(2,1)S(1)} %bitcast.202), kind=kOutput, calls=%fused_computation.29 | convolution fusion | flops 8592031744 | bytes 16777216 | tf_op jit(solution)/shard_map/dot_general | solution.py:578
  420.1 3.8 multiply_subtract_fusion.1
  423.9 10.0 %collective-permute-done.39 = bf16[2,256,2048]{2,1,0:T(8,128)(2,1)} collective-permute-done((bf16[2,256,2048]{2,1,0:T(8,128)(2,1)}, bf16[2,256,2048]{2,1,0:T(8,128)(2,1)}, u32[]{:S(2)}, u32[]{:S(2)}) %collective-permute-start.39) | collective-permute-done | bytes 2097184 | tf_op jit(solution)/shard_map/ppermute | solution.py:74
  434.0 4.0 fusion.43
  438.0 3.5 copy.65
  449.4 15.9 %shard_map.314 = bf16[1024,1536]{1,0:T(8,128)(2,1)} custom-call(s32[1]{0:T(128)S(6)} %copy.94.lengths_ref, bf16[1024,1536]{1,0:T(8,128)(2,1)} %shard_map.305.query_ref.key_ref.value_ref, bf16[1024,1536]{1,0:T(8,128)(2,1)} %shard_map.305.query_ref.key_ref.value_ref, bf16[1024,1536]{1,0:T(8,128)(2,1)} %shard_map.305.query_ref.key_ref.value_ref, ...), custom_call_target="tpu_custom_call" | custom-call | flops 1 | bytes 1 | tf_op jit(solution)/shard_map/pallas_call | solution.py:337
  465.4 11.4 %fusion.4 = (f32[2048]{0:T(1024)S(1)}, bf16[1024,2048]{1,0:T(8,128)(2,1)}) fusion(bf16[1024,2048]{1,0:T(8,128)(2,1)S(1)} %copy-done.1, f32[1024]{0:T(1024)S(1)} %add_rsqrt_fusion, bf16[1024,1536]{1,0:T(8,128)(2,1)} %shard_map.314, bf16[2048,1536]{1,0:T(8,128)(2,1)} %all-gather.6.cloned.1.call-done.weight_ref.refs_1_), kind=kOutput, calls=%fused_computation.7 | convolution fusion | flops 6455031808 | bytes 17838080 | tf_op jit(solution)/shard_map/dot_general | solution.py:224
  476.9 3.8 constant_dynamic-slice_fusion.33
  480.7 3.0 convolution_convert_fusion.7
  493.7 9.7 %collective-permute-done.48 = f32[2,2048]{1,0:T(2,128)S(1)} collective-permute-done((f32[2,2048]{1,0:T(2,128)S(1)}, f32[2,2048]{1,0:T(2,128)S(1)}, u32[]{:S(2)}, u32[]{:S(2)}) %collective-permute-start.48) | collective-permute-done | bytes 16416 | tf_op jit(solution)/shard_map/ppermute | solution.py:74
  503.4 8.1 %pad_maximum_fusion.refs_0_ = f32[256,2,2048]{2,1,0:T(2,128)} fusion(f32[256,1,2048]{2,1,0:T(1,128)} %stack.185, f32[256,1,2048]{2,1,0:T(1,128)} %copy.65), kind=kLoop, calls=%fused_computation.13 | loop fusion | flops 1048576 | bytes 8388608 | tf_op jit(solution)/shard_map/stack | solution.py:647
  511.5 3.3 collective-permute-start.50
  520.9 3.5 add_convert_fusion.6
  526.2 3.4 add_convert_fusion.7
  530.7 12.7 %collective-permute-done.28 = bf16[2,1024,256]{2,1,0:T(8,128)(2,1)S(1)} collective-permute-done((bf16[2,1024,256]{2,1,0:T(8,128)(2,1)S(1)}, bf16[2,1024,256]{2,1,0:T(8,128)(2,1)S(1)}, u32[]{:S(2)}, u32[]{:S(2)}) %collective-permute-start.28) | collective-permute-done | bytes 1048608 | tf_op jit(solution)/shard_map/ppermute | solution.py:74
  555.1 16.1 %multiply_subtract_fusion = (f32[256,2,2048]{2,1,0:T(2,128)}, f32[256,2,2048]{2,1,0:T(2,128)}, f32[256,2,2048]{2,1,0:T(2,128)}) fusion(f32[256,2,2048]{2,1,0:T(2,128)S(1)} %copy-done.4, f32[256,2,2048]{2,1,0:T(2,128)S(1)} %copy-done.2, f32[256,2,2048]{2,1,0:T(2,128)S(1)} %copy-done.15, f32[256,2,2048]{2,1,0:T(2,128)S(1)} %copy-done.16), kind=kLoop, calls=%fused_computation.25 | loop fusion | flops 14680064 | bytes 29360128 | tf_op jit(solution)/shard_map/sub | solution.py:63
  571.9 28.0 %collective-permute-done.32 = bf16[512,256]{1,0:T(8,128)(2,1)S(1)} collective-permute-done((bf16[512,256]{1,0:T(8,128)(2,1)S(1)}, bf16[512,256]{1,0:T(8,128)(2,1)S(1)}, u32[]{:S(2)}, u32[]{:S(2)}) %collective-permute-start.32) | collective-permute-done | bytes 262176 | tf_op jit(solution)/shard_map/ppermute | solution.py:140
  605.3 5.4 multiply_subtract_fusion.2
  612.9 5.4 fusion.39
  (362 shorter events, 140.4 us)
Async XLA Ops:
  7.2 49.8 %all-gather.6.cloned.1.call-start = ((), (), s32[]{:S(2)}) async-start(), calls=%async_computation.4 | async-start | bytes 7077888 | tf_op jit(solution)/shard_map/all_gather | solution.py:540
  10.1 161.8 %all-gather.4.cloned.1.call-start = ((), (), s32[]{:S(2)}) async-start(), calls=%async_computation.3 | async-start | bytes 9437184 | tf_op jit(solution)/shard_map/all_gather | solution.py:540
  12.4 24.9 %collective-permute-start.1 = (bf16[512,256]{1,0:T(8,128)(2,1)}, bf16[512,256]{1,0:T(8,128)(2,1)}, u32[]{:S(2)}, u32[]{:S(2)}) collective-permute-start(bf16[512,256]{1,0:T(8,128)(2,1)} %get-tuple-element.49), channel_id=1, source_target_pairs={{0,2},{1,3},{2,0},{3,1},{4,6},{5,7},{6,4},{7,5},{8,10},{9,11},{10,... | collective-permute-start | bytes 786440 | tf_op jit(solution)/shard_map/ppermute | solution.py:140
  14.1 24.2 %collective-permute-start.2 = (bf16[512,256]{1,0:T(8,128)(2,1)}, bf16[512,256]{1,0:T(8,128)(2,1)S(1)}, u32[]{:S(2)}, u32[]{:S(2)}) collective-permute-start(bf16[512,256]{1,0:T(8,128)(2,1)} %get-tuple-element.49), channel_id=1, source_target_pairs={{0,3},{1,0},{2,1},{3,2},{4,7},{5,4},{6,5},{7,6},{8,11},{9,8},{10,9... | collective-permute-start | bytes 786440 | tf_op jit(solution)/shard_map/ppermute | solution.py:140
  39.3 173.5 %all-gather.8.cloned.1.call-start = ((), (), s32[]{:S(2)}) async-start(), calls=%async_computation.5 | async-start | bytes 9437184 | tf_op jit(solution)/shard_map/all_gather | solution.py:540
  40.5 328.6 %reduce-scatter.4.cloned.1.call-start = ((), (), s32[]{:S(2)}) async-start(), calls=%async_computation.6 | async-start | bytes 5242880 | tf_op jit(solution)/shard_map/reduce_scatter | solution.py:577
  57.0 75.5 %collective-permute-start.10 = (bf16[2,256,2048]{2,1,0:T(8,128)(2,1)}, bf16[2,256,2048]{2,1,0:T(8,128)(2,1)}, u32[]{:S(2)}, u32[]{:S(2)}) collective-permute-start(bf16[2,256,2048]{2,1,0:T(8,128)(2,1)} %shard_map.308.rest_0_), channel_id=1, source_target_pairs={{0,16},{4,20},{8,24},{12,28},{16,0},{20,4},{24,8},{28,12},{1,17},{... | collective-permute-start | bytes 6291464 | tf_op jit(solution)/shard_map/ppermute | solution.py:74
  57.6 77.9 %collective-permute-start.9 = (bf16[2,256,2048]{2,1,0:T(8,128)(2,1)}, bf16[2,256,2048]{2,1,0:T(8,128)(2,1)}, u32[]{:S(2)}, u32[]{:S(2)}) collective-permute-start(bf16[2,256,2048]{2,1,0:T(8,128)(2,1)} %shard_map.308.rest_0_), channel_id=1, source_target_pairs={{0,8},{4,12},{8,0},{12,4},{16,24},{20,28},{24,16},{28,20},{1,9},{5... | collective-permute-start | bytes 6291464 | tf_op jit(solution)/shard_map/ppermute | solution.py:74
  88.2 26.9 %collective-permute-start.3 = (bf16[1024,512]{1,0:T(8,128)(2,1)}, bf16[1024,512]{1,0:T(8,128)(2,1)S(1)}, u32[]{:S(2)}, u32[]{:S(2)}) collective-permute-start(bf16[1024,512]{1,0:T(8,128)(2,1)} %shard_map.306.rest_0_), channel_id=1, source_target_pairs={{0,1},{1,2},{2,3},{4,5},{5,6},{6,7},{8,9},{9,10},{10,11},{12,13},{... | collective-permute-start | bytes 3145736 | tf_op jit(solution)/shard_map/ppermute | solution.py:150
  89.5 26.9 %collective-permute-start.4 = (bf16[1024,512]{1,0:T(8,128)(2,1)}, bf16[1024,512]{1,0:T(8,128)(2,1)S(1)}, u32[]{:S(2)}, u32[]{:S(2)}) collective-permute-start(bf16[1024,512]{1,0:T(8,128)(2,1)} %shard_map.306.rest_0_), channel_id=1, source_target_pairs={{1,0},{2,1},{3,2},{5,4},{6,5},{7,6},{9,8},{10,9},{11,10},{13,12},{... | collective-permute-start | bytes 3145736 | tf_op jit(solution)/shard_map/ppermute | solution.py:151
  118.1 22.7 %collective-permute-start.6 = (bf16[1024,512]{1,0:T(8,128)(2,1)}, bf16[1024,512]{1,0:T(8,128)(2,1)}, u32[]{:S(2)}, u32[]{:S(2)}) collective-permute-start(bf16[1024,512]{1,0:T(8,128)(2,1)} %get-tuple-element.95), channel_id=1, source_target_pairs={{2,1},{1,2},{6,5},{5,6},{10,9},{9,10},{14,13},{13,14},{18,17},{17,... | collective-permute-start | bytes 3145736 | tf_op jit(solution)/shard_map/ppermute | solution.py:155
  119.7 48.9 %collective-permute-start.7 = (bf16[1024,512]{1,0:T(8,128)(2,1)}, bf16[1024,512]{1,0:T(8,128)(2,1)}, u32[]{:S(2)}, u32[]{:S(2)}) collective-permute-start(bf16[1024,512]{1,0:T(8,128)(2,1)} %get-tuple-element.94), channel_id=1, source_target_pairs={{1,0},{2,3},{5,4},{6,7},{9,8},{10,11},{13,12},{14,15},{17,16},{18,... | collective-permute-start | bytes 3145736 | tf_op jit(solution)/shard_map/ppermute | solution.py:156
  121.1 50.3 %collective-permute-start.5 = (bf16[1024,512]{1,0:T(8,128)(2,1)}, bf16[1024,512]{1,0:T(8,128)(2,1)}, u32[]{:S(2)}, u32[]{:S(2)}) collective-permute-start(bf16[1024,512]{1,0:T(8,128)(2,1)} %get-tuple-element.95), channel_id=1, source_target_pairs={{2,0},{1,3},{6,4},{5,7},{10,8},{9,11},{14,12},{13,15},{18,16},{17,... | collective-permute-start | bytes 3145736 | tf_op jit(solution)/shard_map/ppermute | solution.py:154
  134.9 57.6 %collective-permute-start.13 = (bf16[1,256,2048]{2,1,0:T(8,128)(2,1)}, bf16[1,256,2048]{2,1,0:T(8,128)(2,1)S(1)}, u32[]{:S(2)}, u32[]{:S(2)}) collective-permute-start(bf16[1,256,2048]{2,1,0:T(8,128)(2,1)} %slice.134), channel_id=1, source_target_pairs={{0,8},{4,12},{8,0},{12,4},{16,24},{20,28},{24,16},{28,20},{1,9},{5... | collective-permute-start | bytes 3145736 | tf_op jit(solution)/shard_map/ppermute | solution.py:74
  137.8 55.7 %collective-permute-start.14 = (bf16[1,256,2048]{2,1,0:T(8,128)(2,1)}, bf16[1,256,2048]{2,1,0:T(8,128)(2,1)}, u32[]{:S(2)}, u32[]{:S(2)}) collective-permute-start(bf16[1,256,2048]{2,1,0:T(8,128)(2,1)} %slice.135), channel_id=1, source_target_pairs={{0,16},{4,20},{8,24},{12,28},{16,0},{20,4},{24,8},{28,12},{1,17},{... | collective-permute-start | bytes 3145736 | tf_op jit(solution)/shard_map/ppermute | solution.py:74
  140.8 72.0 %collective-permute-start.8 = (bf16[2,256,2048]{2,1,0:T(8,128)(2,1)S(1)}, bf16[2,256,2048]{2,1,0:T(8,128)(2,1)}, u32[]{:S(2)}, u32[]{:S(2)}) collective-permute-start(bf16[2,256,2048]{2,1,0:T(8,128)(2,1)S(1)} %copy-done.3), channel_id=1, source_target_pairs={{0,4},{4,0},{8,12},{12,8},{16,20},{20,16},{24,28},{28,24},{1,5},{5... | collective-permute-start | bytes 6291464 | tf_op jit(solution)/shard_map/ppermute | solution.py:74
  168.6 44.2 %collective-permute-start.11 = (bf16[2,256,2048]{2,1,0:T(8,128)(2,1)}, bf16[2,256,2048]{2,1,0:T(8,128)(2,1)}, u32[]{:S(2)}, u32[]{:S(2)}) collective-permute-start(bf16[2,256,2048]{2,1,0:T(8,128)(2,1)} %collective-permute-done.9.rest_2_), channel_id=1, source_target_pairs={{0,4},{4,0},{8,12},{12,8},{16,20},{20,16},{24,28},{28,24},{1,5},{5... | collective-permute-start | bytes 6291464 | tf_op jit(solution)/shard_map/ppermute | solution.py:74
  171.4 41.4 %collective-permute-start.12 = (bf16[2,256,2048]{2,1,0:T(8,128)(2,1)}, bf16[2,256,2048]{2,1,0:T(8,128)(2,1)}, u32[]{:S(2)}, u32[]{:S(2)}) collective-permute-start(bf16[2,256,2048]{2,1,0:T(8,128)(2,1)} %collective-permute-done.10.rest_3_), channel_id=1, source_target_pairs={{0,4},{4,0},{8,12},{12,8},{16,20},{20,16},{24,28},{28,24},{1,5},{5... | collective-permute-start | bytes 6291464 | tf_op jit(solution)/shard_map/ppermute | solution.py:74
  197.5 15.3 %collective-permute-start.15 = (bf16[2,256,2048]{2,1,0:T(8,128)(2,1)}, bf16[2,256,2048]{2,1,0:T(8,128)(2,1)}, u32[]{:S(2)}, u32[]{:S(2)}) collective-permute-start(bf16[2,256,2048]{2,1,0:T(8,128)(2,1)} %pad_maximum_fusion.1.rest_6_), channel_id=1, source_target_pairs={{0,4},{4,0},{8,12},{12,8},{16,20},{20,16},{24,28},{28,24},{1,5},{5... | collective-permute-start | bytes 6291464 | tf_op jit(solution)/shard_map/ppermute | solution.py:74
  269.3 234.1 %reduce-scatter.6.cloned.1.call-start = ((), (), s32[]{:S(2)}) async-start(), calls=%async_computation.7 | async-start | bytes 5242880 | tf_op jit(solution)/shard_map/reduce_scatter | solution.py:605
  276.2 21.4 %collective-permute-start.41 = (bf16[1024,1024]{1,0:T(8,128)(2,1)}, bf16[1024,1024]{1,0:T(8,128)(2,1)}, u32[]{:S(2)}, u32[]{:S(2)}) collective-permute-start(bf16[1024,1024]{1,0:T(8,128)(2,1)} %convolution_convert_fusion.3), channel_id=1, source_target_pairs={{0,4},{4,0},{8,12},{12,8},{16,20},{20,16},{24,28},{28,24},{1,5},{5... | collective-permute-start | bytes 6291464 | tf_op jit(solution)/shard_map/ppermute | solution.py:74
  283.3 35.6 %collective-permute-start.35 = (bf16[1024,2048]{1,0:T(8,128)(2,1)}, bf16[1024,2048]{1,0:T(8,128)(2,1)}, u32[]{:S(2)}, u32[]{:S(2)}) collective-permute-start(bf16[1024,2048]{1,0:T(8,128)(2,1)} %fusion.17), channel_id=1, source_target_pairs={{0,4},{4,0},{8,12},{12,8},{16,20},{20,16},{24,28},{28,24},{1,5},{5... | collective-permute-start | bytes 12582920 | tf_op jit(solution)/shard_map/ppermute | solution.py:74
  287.1 16.5 %collective-permute-start.40 = (bf16[1024,1024]{1,0:T(8,128)(2,1)}, bf16[1024,1024]{1,0:T(8,128)(2,1)}, u32[]{:S(2)}, u32[]{:S(2)}) collective-permute-start(bf16[1024,1024]{1,0:T(8,128)(2,1)} %convolution_convert_fusion.4), channel_id=1, source_target_pairs={{0,4},{4,0},{8,12},{12,8},{16,20},{20,16},{24,28},{28,24},{1,5},{5... | collective-permute-start | bytes 6291464 | tf_op jit(solution)/shard_map/ppermute | solution.py:74
  293.9 34.7 %collective-permute-start.34 = (bf16[1024,2048]{1,0:T(8,128)(2,1)}, bf16[1024,2048]{1,0:T(8,128)(2,1)}, u32[]{:S(2)}, u32[]{:S(2)}) collective-permute-start(bf16[1024,2048]{1,0:T(8,128)(2,1)} %fusion.14), channel_id=1, source_target_pairs={{0,4},{4,0},{8,12},{12,8},{16,20},{20,16},{24,28},{28,24},{1,5},{5... | collective-permute-start | bytes 12582920 | tf_op jit(solution)/shard_map/ppermute | solution.py:74
  307.9 30.3 %collective-permute-start.44 = (bf16[1024,256]{1,0:T(8,128)(2,1)S(1)}, bf16[1024,256]{1,0:T(8,128)(2,1)S(1)}, u32[]{:S(2)}, u32[]{:S(2)}) collective-permute-start(bf16[1024,256]{1,0:T(8,128)(2,1)S(1)} %get-tuple-element.85), channel_id=1, source_target_pairs={{0,8},{4,12},{8,0},{12,4},{16,24},{20,28},{24,16},{28,20},{1,9},{5... | collective-permute-start | bytes 1572872 | tf_op jit(solution)/shard_map/ppermute | solution.py:74
  318.2 93.2 %collective-permute-start.43 = (bf16[2,1024,256]{2,1,0:T(8,128)(2,1)}, bf16[2,1024,256]{2,1,0:T(8,128)(2,1)}, u32[]{:S(2)}, u32[]{:S(2)}) collective-permute-start(bf16[2,1024,256]{2,1,0:T(8,128)(2,1)} %pad_maximum_fusion.14), channel_id=1, source_target_pairs={{0,8},{4,12},{8,0},{12,4},{16,24},{20,28},{24,16},{28,20},{1,9},{5... | collective-permute-start | bytes 3145736 | tf_op jit(solution)/shard_map/ppermute | solution.py:74
  327.2 26.2 %collective-permute-start.36 = (bf16[256,2048]{1,0:T(8,128)(2,1)S(1)}, bf16[256,2048]{1,0:T(8,128)(2,1)S(1)}, u32[]{:S(2)}, u32[]{:S(2)}) collective-permute-start(bf16[256,2048]{1,0:T(8,128)(2,1)S(1)} %get-tuple-element.64), channel_id=1, source_target_pairs={{0,16},{4,20},{8,24},{12,28},{16,0},{20,4},{24,8},{28,12},{1,17},{... | collective-permute-start | bytes 3145736 | tf_op jit(solution)/shard_map/ppermute | solution.py:74
  337.1 30.6 %collective-permute-start.38 = (bf16[256,2048]{1,0:T(8,128)(2,1)S(1)}, bf16[256,2048]{1,0:T(8,128)(2,1)S(1)}, u32[]{:S(2)}, u32[]{:S(2)}) collective-permute-start(bf16[256,2048]{1,0:T(8,128)(2,1)S(1)} %get-tuple-element.63), channel_id=1, source_target_pairs={{0,8},{4,12},{8,0},{12,4},{16,24},{20,28},{24,16},{28,20},{1,9},{5... | collective-permute-start | bytes 3145736 | tf_op jit(solution)/shard_map/ppermute | solution.py:74
  339.5 71.9 %collective-permute-start.45 = (bf16[2,1024,256]{2,1,0:T(8,128)(2,1)}, bf16[2,1024,256]{2,1,0:T(8,128)(2,1)}, u32[]{:S(2)}, u32[]{:S(2)}) collective-permute-start(bf16[2,1024,256]{2,1,0:T(8,128)(2,1)} %pad_maximum_fusion.15), channel_id=1, source_target_pairs={{0,16},{4,20},{8,24},{12,28},{16,0},{20,4},{24,8},{28,12},{1,17},{... | collective-permute-start | bytes 3145736 | tf_op jit(solution)/shard_map/ppermute | solution.py:74
  355.2 68.7 %collective-permute-start.37 = (bf16[2,256,2048]{2,1,0:T(8,128)(2,1)}, bf16[2,256,2048]{2,1,0:T(8,128)(2,1)}, u32[]{:S(2)}, u32[]{:S(2)}) collective-permute-start(bf16[2,256,2048]{2,1,0:T(8,128)(2,1)} %pad_maximum_fusion.6), channel_id=1, source_target_pairs={{0,8},{4,12},{8,0},{12,4},{16,24},{20,28},{24,16},{28,20},{1,9},{5... | collective-permute-start | bytes 6291464 | tf_op jit(solution)/shard_map/ppermute | solution.py:74
  390.1 43.9 %collective-permute-start.39 = (bf16[2,256,2048]{2,1,0:T(8,128)(2,1)}, bf16[2,256,2048]{2,1,0:T(8,128)(2,1)}, u32[]{:S(2)}, u32[]{:S(2)}) collective-permute-start(bf16[2,256,2048]{2,1,0:T(8,128)(2,1)} %pad_maximum_fusion.7), channel_id=1, source_target_pairs={{0,16},{4,20},{8,24},{12,28},{16,0},{20,4},{24,8},{28,12},{1,17},{... | collective-permute-start | bytes 6291464 | tf_op jit(solution)/shard_map/ppermute | solution.py:74
  410.9 199.8 %reduce-scatter.8.cloned.1.call-start = ((), (), s32[]{:S(2)}) async-start(), calls=%async_computation.8 | async-start | bytes 5242880 | tf_op jit(solution)/shard_map/reduce_scatter | solution.py:623
  416.9 28.4 %collective-permute-start.20 = (bf16[1024,1024]{1,0:T(8,128)(2,1)}, bf16[1024,1024]{1,0:T(8,128)(2,1)S(1)}, u32[]{:S(2)}, u32[]{:S(2)}) collective-permute-start(bf16[1024,1024]{1,0:T(8,128)(2,1)} %convolution_convert_fusion.5), channel_id=1, source_target_pairs={{0,4},{4,0},{8,12},{12,8},{16,20},{20,16},{24,28},{28,24},{1,5},{5... | collective-permute-start | bytes 6291464 | tf_op jit(solution)/shard_map/ppermute | solution.py:74
  418.9 28.5 %collective-permute-start.19 = (bf16[1024,1024]{1,0:T(8,128)(2,1)}, bf16[1024,1024]{1,0:T(8,128)(2,1)S(1)}, u32[]{:S(2)}, u32[]{:S(2)}) collective-permute-start(bf16[1024,1024]{1,0:T(8,128)(2,1)} %convolution_convert_fusion.6), channel_id=1, source_target_pairs={{0,4},{4,0},{8,12},{12,8},{16,20},{20,16},{24,28},{28,24},{1,5},{5... | collective-permute-start | bytes 6291464 | tf_op jit(solution)/shard_map/ppermute | solution.py:74
  488.8 26.0 %collective-permute-start.27 = (bf16[1024,256]{1,0:T(8,128)(2,1)}, bf16[1024,256]{1,0:T(8,128)(2,1)}, u32[]{:S(2)}, u32[]{:S(2)}) collective-permute-start(bf16[1024,256]{1,0:T(8,128)(2,1)} %get-tuple-element.92), channel_id=1, source_target_pairs={{0,16},{4,20},{8,24},{12,28},{16,0},{20,4},{24,8},{28,12},{1,17},{... | collective-permute-start | bytes 1572872 | tf_op jit(solution)/shard_map/ppermute | solution.py:74
  489.8 31.0 %collective-permute-start.22 = (bf16[1024,768]{1,0:T(8,128)(2,1)}, bf16[1024,768]{1,0:T(8,128)(2,1)}, u32[]{:S(2)}, u32[]{:S(2)}) collective-permute-start(bf16[1024,768]{1,0:T(8,128)(2,1)} %convolution_convert_fusion.7), channel_id=1, source_target_pairs={{0,4},{4,0},{8,12},{12,8},{16,20},{20,16},{24,28},{28,24},{1,5},{5... | collective-permute-start | bytes 4718600 | tf_op jit(solution)/shard_map/ppermute | solution.py:74
  492.5 26.4 %collective-permute-start.29 = (bf16[1024,256]{1,0:T(8,128)(2,1)}, bf16[1024,256]{1,0:T(8,128)(2,1)}, u32[]{:S(2)}, u32[]{:S(2)}) collective-permute-start(bf16[1024,256]{1,0:T(8,128)(2,1)} %get-tuple-element.91), channel_id=1, source_target_pairs={{0,8},{4,12},{8,0},{12,4},{16,24},{20,28},{24,16},{28,20},{1,9},{5... | collective-permute-start | bytes 1572872 | tf_op jit(solution)/shard_map/ppermute | solution.py:74
  493.7 32.5 %collective-permute-start.21 = (bf16[1024,768]{1,0:T(8,128)(2,1)}, bf16[1024,768]{1,0:T(8,128)(2,1)}, u32[]{:S(2)}, u32[]{:S(2)}) collective-permute-start(bf16[1024,768]{1,0:T(8,128)(2,1)} %convolution_convert_fusion.8), channel_id=1, source_target_pairs={{0,4},{4,0},{8,12},{12,8},{16,20},{20,16},{24,28},{28,24},{1,5},{5... | collective-permute-start | bytes 4718600 | tf_op jit(solution)/shard_map/ppermute | solution.py:74
  511.5 42.5 %collective-permute-start.50 = (f32[2,256]{1,0:T(2,128)S(1)}, f32[2,256]{1,0:T(2,128)S(1)}, u32[]{:S(2)}, u32[]{:S(2)}) collective-permute-start(f32[2,256]{1,0:T(2,128)S(1)} %add.555), channel_id=1, source_target_pairs={{0,2},{1,3},{2,0},{3,1},{4,6},{5,7},{6,4},{7,5},{8,10},{9,11},{10,... | collective-permute-start | bytes 6152 | tf_op jit(solution)/shard_map/ppermute | solution.py:74
  517.3 26.2 %collective-permute-start.28 = (bf16[2,1024,256]{2,1,0:T(8,128)(2,1)S(1)}, bf16[2,1024,256]{2,1,0:T(8,128)(2,1)S(1)}, u32[]{:S(2)}, u32[]{:S(2)}) collective-permute-start(bf16[2,1024,256]{2,1,0:T(8,128)(2,1)S(1)} %pad_maximum_fusion.12), channel_id=1, source_target_pairs={{0,8},{4,12},{8,0},{12,4},{16,24},{20,28},{24,16},{28,20},{1,9},{5... | collective-permute-start | bytes 3145736 | tf_op jit(solution)/shard_map/ppermute | solution.py:74
  520.2 26.2 %collective-permute-start.30 = (bf16[2,1024,256]{2,1,0:T(8,128)(2,1)S(1)}, bf16[2,1024,256]{2,1,0:T(8,128)(2,1)S(1)}, u32[]{:S(2)}, u32[]{:S(2)}) collective-permute-start(bf16[2,1024,256]{2,1,0:T(8,128)(2,1)S(1)} %pad_maximum_fusion.13), channel_id=1, source_target_pairs={{0,16},{4,20},{8,24},{12,28},{16,0},{20,4},{24,8},{28,12},{1,17},{... | collective-permute-start | bytes 3145736 | tf_op jit(solution)/shard_map/ppermute | solution.py:74
  524.6 27.7 %collective-permute-start.23 = (bf16[256,768]{1,0:T(8,128)(2,1)S(1)}, bf16[256,768]{1,0:T(8,128)(2,1)S(1)}, u32[]{:S(2)}, u32[]{:S(2)}) collective-permute-start(bf16[256,768]{1,0:T(8,128)(2,1)S(1)} %get-tuple-element.100), channel_id=1, source_target_pairs={{0,16},{4,20},{8,24},{12,28},{16,0},{20,4},{24,8},{28,12},{1,17},{... | collective-permute-start | bytes 1179656 | tf_op jit(solution)/shard_map/ppermute | solution.py:74
  529.7 23.2 %collective-permute-start.25 = (bf16[256,768]{1,0:T(8,128)(2,1)S(1)}, bf16[256,768]{1,0:T(8,128)(2,1)S(1)}, u32[]{:S(2)}, u32[]{:S(2)}) collective-permute-start(bf16[256,768]{1,0:T(8,128)(2,1)S(1)} %get-tuple-element.99), channel_id=1, source_target_pairs={{0,8},{4,12},{8,0},{12,4},{16,24},{20,28},{24,16},{28,20},{1,9},{5... | collective-permute-start | bytes 1179656 | tf_op jit(solution)/shard_map/ppermute | solution.py:74
  549.0 22.9 %collective-permute-start.31 = (bf16[512,256]{1,0:T(8,128)(2,1)S(1)}, bf16[512,256]{1,0:T(8,128)(2,1)S(1)}, u32[]{:S(2)}, u32[]{:S(2)}) collective-permute-start(bf16[512,256]{1,0:T(8,128)(2,1)S(1)} %get-tuple-element.102), channel_id=1, source_target_pairs={{0,1},{1,2},{2,3},{3,0},{4,5},{5,6},{6,7},{7,4},{8,9},{9,10},{10,1... | collective-permute-start | bytes 786440 | tf_op jit(solution)/shard_map/ppermute | solution.py:140
  549.8 50.0 %collective-permute-start.32 = (bf16[512,256]{1,0:T(8,128)(2,1)S(1)}, bf16[512,256]{1,0:T(8,128)(2,1)S(1)}, u32[]{:S(2)}, u32[]{:S(2)}) collective-permute-start(bf16[512,256]{1,0:T(8,128)(2,1)S(1)} %get-tuple-element.103), channel_id=1, source_target_pairs={{0,2},{1,3},{2,0},{3,1},{4,6},{5,7},{6,4},{7,5},{8,10},{9,11},{10,... | collective-permute-start | bytes 786440 | tf_op jit(solution)/shard_map/ppermute | solution.py:140
  552.3 47.5 %collective-permute-start.33 = (bf16[512,256]{1,0:T(8,128)(2,1)S(1)}, bf16[512,256]{1,0:T(8,128)(2,1)S(1)}, u32[]{:S(2)}, u32[]{:S(2)}) collective-permute-start(bf16[512,256]{1,0:T(8,128)(2,1)S(1)} %get-tuple-element.104), channel_id=1, source_target_pairs={{0,3},{1,0},{2,1},{3,2},{4,7},{5,4},{6,5},{7,6},{8,11},{9,8},{10,9... | collective-permute-start | bytes 786440 | tf_op jit(solution)/shard_map/ppermute | solution.py:140
  552.9 49.2 %collective-permute-start.24 = (bf16[2,256,768]{2,1,0:T(8,128)(2,1)S(1)}, bf16[2,256,768]{2,1,0:T(8,128)(2,1)S(1)}, u32[]{:S(2)}, u32[]{:S(2)}) collective-permute-start(bf16[2,256,768]{2,1,0:T(8,128)(2,1)S(1)} %pad_maximum_fusion.16), channel_id=1, source_target_pairs={{0,8},{4,12},{8,0},{12,4},{16,24},{20,28},{24,16},{28,20},{1,9},{5... | collective-permute-start | bytes 2359304 | tf_op jit(solution)/shard_map/ppermute | solution.py:74
  554.0 48.1 %collective-permute-start.26 = (bf16[2,256,768]{2,1,0:T(8,128)(2,1)S(1)}, bf16[2,256,768]{2,1,0:T(8,128)(2,1)S(1)}, u32[]{:S(2)}, u32[]{:S(2)}) collective-permute-start(bf16[2,256,768]{2,1,0:T(8,128)(2,1)S(1)} %pad_maximum_fusion.17), channel_id=1, source_target_pairs={{0,16},{4,20},{8,24},{12,28},{16,0},{20,4},{24,8},{28,12},{1,17},{... | collective-permute-start | bytes 2359304 | tf_op jit(solution)/shard_map/ppermute | solution.py:74
  (85 other events, 850.6 us)
Sparse Core Ops, SparseCore 0:
  10.5 46.4 all-gather.5
  59.5 86.3 all-gather.3
  148.3 59.5 all-gather.7
  269.4 76.7 reduce-scatter.3
  411.0 77.6 reduce-scatter.5
  503.5 94.2 reduce-scatter.7

commit v3 on v2

--- a/solution.py
+++ b/solution.py
@@ -623,7 +623,7 @@
     one_back = lax.psum_scatter(tie(one_back_part, feed_out), "mp", scatter_dimension=0, tiled=True).astype(f32)
     gain_one_grad = jnp.sum(one_back_part.astype(f32) * tokens.astype(f32) * scale_one, axis=0)
     half = project_back.shape[1] // 2
-    qkv_red, _ = reduce_dp(
+    qkv_red, qkv_total = reduce_dp(
         lambda columns: [
             lead_dot(columns, project_back[:, k * half : (k + 1) * half]) for k in range(2)
         ],
@@ -634,7 +634,7 @@
     qkv_grad = tie(
         jnp.stack([qkv_red[:, c * head_cols : (c + 1) * head_cols] for c in range(3)])
     ).transpose(1, 0, 2)
-    gains_sum = sum_flips(jnp.stack([gain_one_grad, gain_two_grad]), "dp")
+    gains_sum = sum_flips(tie(jnp.stack([gain_one_grad, gain_two_grad]), *qkv_total), "dp")
     gains_sum = pick(gains_sum, lax.axis_index("dp"), norm_gains.shape[1], 1)
     gains_red = sum_flips(gains_sum, "mp")
 

time: 630 us -> 670 us (1.063)
  waiting for transfers between devices: 192 us -> 214 us
    ppermute x37, waiting for transfers between devices: 79.8 us -> 124 us  [flip(): lax.ppermute(block, name, [(j, j ^ bits) for j in range(lax.axis_size(nam...]
    ppermute x9, waiting for transfers between devices: 61.7 us -> 39.3 us  [shift_all(): lax.ppermute(take(k), 'mp', [(j, (j + k) % size) for j in range(size)])]
    unnamed x154 -> x172, local copies, waits for them, and re-layouts: 16.7 us -> 18.9 us
  transfers between devices with their start and end apart: 57 -> 57, of which waited for: 18 -> 19; matrix products, arithmetic and copies ran while one was open for 36% -> 34% of each run, Pallas kernels for 9% -> 9%
where the time goes in v3:
time: 670 us; the launch traced here: 662 us
  waiting for transfers between devices  214 us (32%)
  Pallas kernels  113 us (17%)
  matrix products  101 us (15%)
  other arithmetic  99.5 us (15%)
  local copies, waits for them, and re-layouts  61.3 us (9%)
  starting transfers between devices  48.7 us (7%)
  between operations  16.3 us (2%)
  blocking collectives  9.03 us (1%)
    ppermute x37, waiting for transfers between devices, flip(): lax.ppermute(block, name, [(j, j ^ bits) for j in range(lax.axis_size(nam...  124 us
    dot_general x16, matrix products, lead_dot(): lax.dot_general(a, b, (((0,), (0,)), ((), ())), preferred_element_type=jn...  72.7 us
    pallas_call x1, Pallas kernels, feed_forward(): pl.pallas_call(functools.partial(feed_kernel, len(pieces)), grid_spec=plt...  56.5 us
    ppermute x9, waiting for transfers between devices, shift_all(): lax.ppermute(take(k), 'mp', [(j, (j + k) % size) for j in range(size)])  39.3 us
    sub x5, other arithmetic, adamw(): weight - step_rate * (first_hat / (jnp.sqrt(second_hat) + adam_eps) + wei...  29.7 us
    ppermute x1, waiting for transfers between devices, gather_line(): edge = lax.ppermute(outward, 'mp', [(1, 0), (2, 3)])  27.9 us
    ppermute x37, starting transfers between devices, flip(): lax.ppermute(block, name, [(j, j ^ bits) for j in range(lax.axis_size(nam...  27.7 us
    ppermute x1, waiting for transfers between devices, gather_line(): from_low = lax.ppermute(block, 'mp', [(0, 1), (1, 2), (2, 3)])  21 us
  transfers between devices with their start and end apart: 57, of which 19 were waited for; matrix products, arithmetic and copies ran while one was open for 34% of the time, Pallas kernels for 9%

profile of v3, /device:TPU:26, one launch (start us, length us, event | category | flops | bytes accessed | tf_op | source)
XLA Modules:
  0.0 661.9 jit_solution(12566488055258978468)
XLA Ops:
  14.5 6.4 collective-permute-done
  21.9 15.4 %collective-permute-done.1 = bf16[512,256]{1,0:T(8,128)(2,1)} collective-permute-done((bf16[512,256]{1,0:T(8,128)(2,1)}, bf16[512,256]{1,0:T(8,128)(2,1)}, u32[]{:S(2)}, u32[]{:S(2)}) %collective-permute-start.1) | collective-permute-done | bytes 262176 | tf_op jit(solution)/shard_map/ppermute | solution.py:140
  40.5 5.9 copy.72
  46.5 9.0 %all_gather.12 = bf16[2,2048]{1,0:T(2,128)(2,1)S(1)} all-gather(bf16[2,256]{1,0:T(2,128)(2,1)S(1)} %convert_element_type.338), channel_id=1, replica_groups=mesh['dp'=8,'mp'=4] {'dp'}, dimensions={1}, use_global_device_ids=true | all-gather | bytes 9216 | tf_op jit(solution)/shard_map/all_gather | solution.py:540
  59.1 5.2 fusion.2.normed_ref.refs_0_
  68.4 12.8 %shard_map.305.query_ref.key_ref.value_ref = bf16[1024,1536]{1,0:T(8,128)(2,1)} custom-call(bf16[1024,2048]{1,0:T(8,128)(2,1)} %fusion.2.normed_ref.refs_0_, bf16[2048,1536]{1,0:T(8,128)(2,1)} %all-gather.6.cloned.1.call-done.weight_ref.refs_1_, f32[1024,128]{1,0:T(8,128)} %get-tuple-element.126.cosine_ref, f32[1024,128]{1,0:T(8,128)} %get-tuple-element.45.sine_ref), custom_call_target="tpu_custom_call" | custom-call | flops 1 | bytes 1 | tf_op jit(solution)/shard_map/pallas_call | solution.py:207
  81.1 7.1 %shard_map.306.rest_0_ = bf16[1024,512]{1,0:T(8,128)(2,1)} custom-call(s32[1]{0:T(128)S(6)} %copy.96.lengths_ref, bf16[1024,1536]{1,0:T(8,128)(2,1)} %shard_map.305.query_ref.key_ref.value_ref, bf16[1024,1536]{1,0:T(8,128)(2,1)} %shard_map.305.query_ref.key_ref.value_ref, bf16[1024,1536]{1,0:T(8,128)(2,1)} %shard_map.305.query_ref.key_ref.value_ref), custom_call_target="tpu_custom_call" | custom-call | flops 1 | bytes 1 | tf_op jit(solution)/shard_map/pallas_call | solution.py:268
  89.5 4.6 collective-permute-start.4
  94.1 21.0 %collective-permute-done.3.rest_1_ = bf16[1024,512]{1,0:T(8,128)(2,1)S(1)} collective-permute-done((bf16[1024,512]{1,0:T(8,128)(2,1)}, bf16[1024,512]{1,0:T(8,128)(2,1)S(1)}, u32[]{:S(2)}, u32[]{:S(2)}) %collective-permute-start.3) | collective-permute-done | bytes 1048608 | tf_op jit(solution)/shard_map/ppermute | solution.py:150
  122.7 9.9 %collective-permute-done.10.rest_3_ = bf16[2,256,2048]{2,1,0:T(8,128)(2,1)} collective-permute-done((bf16[2,256,2048]{2,1,0:T(8,128)(2,1)}, bf16[2,256,2048]{2,1,0:T(8,128)(2,1)}, u32[]{:S(2)}, u32[]{:S(2)}) %collective-permute-start.10) | collective-permute-done | bytes 2097184 | tf_op jit(solution)/shard_map/ppermute | solution.py:74
  140.7 27.9 %collective-permute-done.7 = bf16[1024,512]{1,0:T(8,128)(2,1)} collective-permute-done((bf16[1024,512]{1,0:T(8,128)(2,1)}, bf16[1024,512]{1,0:T(8,128)(2,1)}, u32[]{:S(2)}, u32[]{:S(2)}) %collective-permute-start.7) | collective-permute-done | bytes 1048608 | tf_op jit(solution)/shard_map/ppermute | solution.py:156
  171.9 20.6 %shard_map.307 = (f32[1024,2048]{1,0:T(8,128)}, bf16[1024,2048]{1,0:T(8,128)(2,1)}) custom-call(s32[5]{0:T(128)} %stack.152.owners_ref, bf16[1024,2048]{1,0:T(8,128)(2,1)} %tokens_ref.1, f32[1,2048]{1,0:T(1,128)} %get-tuple-element.120.gain_ref, bf16[2048,2048]{1,0:T(8,128)(2,1)} %all-gather.4.cloned.1.call-done.out_ref, ...), custom_call_target="tpu_custom_call" | custom-call | flops 1 | bytes 1 | tf_op jit(solution)/shard_map/pallas_call | solution.py:473
  198.8 4.0 constant_dynamic-slice_fusion.11
  213.5 4.1 constant_dynamic-slice_fusion.21
  217.8 56.5 %shard_map.311 = (bf16[1024,2048]{1,0:T(8,128)(2,1)}, bf16[2,1024,2048]{2,1,0:T(8,128)(2,1)}, bf16[1024,2048]{1,0:T(8,128)(2,1)}) custom-call(s32[8]{0:T(128)} %stack.161.places_ref, bf16[1024,2048]{1,0:T(8,128)(2,1)} %get-tuple-element.23.refs_1_.normed_ref, bf16[1024,2048]{1,0:T(8,128)(2,1)} %back_ref.1, ...), custom_call_target="tpu_custom_call" | custom-call | flops 1 | bytes 1 | tf_op jit(solution)/shard_map/pallas_call | solution.py:424
  274.4 8.8 %fusion.17 = bf16[1024,2048]{1,0:T(8,128)(2,1)} fusion(bf16[2,1024,2048]{2,1,0:T(8,128)(2,1)} %get-tuple-element.26, bf16[1024,256]{1,0:T(8,128)(2,1)S(1)} %copy-done.57, bf16[1024,256]{1,0:T(8,128)(2,1)S(1)} %copy-done.58, bf16[1024,256]{1,0:T(8,128)(2,1)S(1)} %copy-done.59, bf16[1024,256]{1,0:T(8,128)(2,1)S(1)} %copy-done.60), kind=kOutput, calls=%fused_computation.31 | convolution fusion | flops 4305453056 | bytes 10485760 | tf_op jit(solution)/shard_map/dot_general | solution.py:228
  283.1 6.6 fusion.14
  291.3 5.4 convolution_convert_fusion.3
  300.5 10.6 %convolution_convert_fusion.1.refs_0_ = bf16[1024,2048]{1,0:T(8,128)(2,1)} fusion(bf16[1024,2048]{1,0:T(8,128)(2,1)S(1)} %copy-done.80, bf16[2048,2048]{1,0:T(8,128)(2,1)S(1)} %bitcast.202), kind=kOutput, calls=%fused_computation.29 | convolution fusion | flops 8592031744 | bytes 16777216 | tf_op jit(solution)/shard_map/dot_general | solution.py:578
  312.4 4.0 add_convert_fusion.2
  322.5 7.9 %add_convert_fusion = bf16[1024,2048]{1,0:T(8,128)(2,1)S(1)} fusion(bf16[1024,2048]{1,0:T(8,128)(2,1)} %collective-permute-done.35, bf16[2,1024,2048]{2,1,0:T(8,128)(2,1)} %get-tuple-element.26, bf16[1024,256]{1,0:T(8,128)(2,1)S(1)} %copy-done.46, bf16[1024,256]{1,0:T(8,128)(2,1)S(1)} %copy-done.47, bf16[1024,256]{1,0:T(8,128)(2,1)S(1)} %copy-done.48, ...), kind=kOutput, calls=%fused_computation.8 | convolution fusion | flops 4309647360 | bytes 14680064 | tf_op jit(solution)/shard_map/dot_general | solution.py:228
  332.7 8.1 %add_convert_fusion.1 = bf16[1024,2048]{1,0:T(8,128)(2,1)S(1)} fusion(bf16[1024,2048]{1,0:T(8,128)(2,1)} %collective-permute-done.34, bf16[2,1024,2048]{2,1,0:T(8,128)(2,1)} %get-tuple-element.26, bf16[1024,256]{1,0:T(8,128)(2,1)S(1)} %copy-done.46, bf16[1024,256]{1,0:T(8,128)(2,1)S(1)} %copy-done.47, bf16[1024,256]{1,0:T(8,128)(2,1)S(1)} %copy-done.48, ...), kind=kOutput, calls=%fused_computation.9 | convolution fusion | flops 4309647360 | bytes 14680064 | tf_op jit(solution)/shard_map/dot_general | solution.py:228
  346.9 11.0 %collective-permute-done.36 = bf16[256,2048]{1,0:T(8,128)(2,1)S(1)} collective-permute-done((bf16[256,2048]{1,0:T(8,128)(2,1)S(1)}, bf16[256,2048]{1,0:T(8,128)(2,1)S(1)}, u32[]{:S(2)}, u32[]{:S(2)}) %collective-permute-start.36) | collective-permute-done | bytes 1048608 | tf_op jit(solution)/shard_map/ppermute | solution.py:74
  359.3 7.9 %collective-permute-done.38 = bf16[256,2048]{1,0:T(8,128)(2,1)S(1)} collective-permute-done((bf16[256,2048]{1,0:T(8,128)(2,1)S(1)}, bf16[256,2048]{1,0:T(8,128)(2,1)S(1)}, u32[]{:S(2)}, u32[]{:S(2)}) %collective-permute-start.38) | collective-permute-done | bytes 1048608 | tf_op jit(solution)/shard_map/ppermute | solution.py:74
  374.1 5.7 convolution_convert_fusion.2
  379.9 3.0 collective-permute-start.16
  385.9 3.8 collective-permute-done.16.refs_2_
  390.3 13.7 %collective-permute-done.17.refs_3_ = bf16[256,512]{1,0:T(8,128)(2,1)} collective-permute-done((bf16[256,512]{1,0:T(8,128)(2,1)S(1)}, bf16[256,512]{1,0:T(8,128)(2,1)}, u32[]{:S(2)}, u32[]{:S(2)}) %collective-permute-start.17) | collective-permute-done | bytes 262176 | tf_op jit(solution)/shard_map/ppermute | solution.py:140
  416.5 3.8 multiply_subtract_fusion.1
  420.3 13.2 %collective-permute-done.37 = bf16[2,256,2048]{2,1,0:T(8,128)(2,1)} collective-permute-done((bf16[2,256,2048]{2,1,0:T(8,128)(2,1)}, bf16[2,256,2048]{2,1,0:T(8,128)(2,1)}, u32[]{:S(2)}, u32[]{:S(2)}) %collective-permute-start.37) | collective-permute-done | bytes 2097184 | tf_op jit(solution)/shard_map/ppermute | solution.py:74
  433.5 19.5 %collective-permute-done.39 = bf16[2,256,2048]{2,1,0:T(8,128)(2,1)S(1)} collective-permute-done((bf16[2,256,2048]{2,1,0:T(8,128)(2,1)S(1)}, bf16[2,256,2048]{2,1,0:T(8,128)(2,1)S(1)}, u32[]{:S(2)}, u32[]{:S(2)}) %collective-permute-start.39) | collective-permute-done | bytes 2097184 | tf_op jit(solution)/shard_map/ppermute | solution.py:74
  453.0 3.3 fusion.43
  460.0 6.0 pad_maximum_fusion.refs_0_
  468.9 4.4 add_convert_fusion.4.refs_2_
  473.3 3.6 add_convert_fusion.5.refs_1_
  477.0 15.9 %shard_map.314 = bf16[1024,1536]{1,0:T(8,128)(2,1)} custom-call(s32[1]{0:T(128)S(6)} %copy.96.lengths_ref, bf16[1024,1536]{1,0:T(8,128)(2,1)} %shard_map.305.query_ref.key_ref.value_ref, bf16[1024,1536]{1,0:T(8,128)(2,1)} %shard_map.305.query_ref.key_ref.value_ref, bf16[1024,1536]{1,0:T(8,128)(2,1)} %shard_map.305.query_ref.key_ref.value_ref, ...), custom_call_target="tpu_custom_call" | custom-call | flops 1 | bytes 1 | tf_op jit(solution)/shard_map/pallas_call | solution.py:337
  492.8 11.4 %fusion.4 = (f32[2048]{0:T(1024)S(1)}, bf16[1024,2048]{1,0:T(8,128)(2,1)}) fusion(bf16[1024,2048]{1,0:T(8,128)(2,1)S(1)} %copy-done.1, f32[1024]{0:T(1024)S(1)} %copy-done.68, bf16[1024,1536]{1,0:T(8,128)(2,1)} %shard_map.314, bf16[2048,1536]{1,0:T(8,128)(2,1)} %all-gather.6.cloned.1.call-done.weight_ref.refs_1_), kind=kOutput, calls=%fused_computation.7 | convolution fusion | flops 6455031808 | bytes 17838080 | tf_op jit(solution)/shard_map/dot_general | solution.py:224
  504.3 3.8 constant_dynamic-slice_fusion.33
  518.7 8.2 %collective-permute-done.27 = bf16[1024,256]{1,0:T(8,128)(2,1)} collective-permute-done((bf16[1024,256]{1,0:T(8,128)(2,1)}, bf16[1024,256]{1,0:T(8,128)(2,1)}, u32[]{:S(2)}, u32[]{:S(2)}) %collective-permute-start.27) | collective-permute-done | bytes 524320 | tf_op jit(solution)/shard_map/ppermute | solution.py:74
  535.5 4.4 add_convert_fusion.7.refs_1_
  539.9 4.4 add_convert_fusion.6.refs_2_
  550.1 7.0 %collective-permute-done.47 = f32[2,2048]{1,0:T(2,128)S(1)} collective-permute-done((f32[2,2048]{1,0:T(2,128)S(1)}, f32[2,2048]{1,0:T(2,128)S(1)}, u32[]{:S(2)}, u32[]{:S(2)}) %collective-permute-start.47) | collective-permute-done | bytes 16416 | tf_op jit(solution)/shard_map/ppermute | solution.py:74
  563.5 4.9 collective-permute-done.48
  570.8 3.2 collective-permute-start.31
  578.7 37.8 %collective-permute-done.50 = f32[2,256]{1,0:T(2,128)S(1)} collective-permute-done((f32[2,256]{1,0:T(2,128)S(1)}, f32[2,256]{1,0:T(2,128)S(1)}, u32[]{:S(2)}, u32[]{:S(2)}) %collective-permute-start.50) | collective-permute-done | bytes 2080 | tf_op jit(solution)/shard_map/ppermute | solution.py:74
  618.0 17.7 %multiply_subtract_fusion = (f32[256,2,2048]{2,1,0:T(2,128)}, f32[256,2,2048]{2,1,0:T(2,128)}, f32[256,2,2048]{2,1,0:T(2,128)}) fusion(f32[256,2,2048]{2,1,0:T(2,128)S(1)} %copy-done.4, f32[256,2,2048]{2,1,0:T(2,128)S(1)} %copy-done.2, f32[256,2,2048]{2,1,0:T(2,128)} %param.28, f32[256,2,2048]{2,1,0:T(2,128)} %param.33), kind=kLoop, calls=%fused_computation.25 | loop fusion | flops 14680064 | bytes 29360128 | tf_op jit(solution)/shard_map/sub | solution.py:63
  641.8 5.4 multiply_subtract_fusion.2
  649.4 5.5 fusion.39
  (381 shorter events, 155.3 us)
Async XLA Ops:
  7.2 49.8 %all-gather.6.cloned.1.call-start = ((), (), s32[]{:S(2)}) async-start(), calls=%async_computation.4 | async-start | bytes 7077888 | tf_op jit(solution)/shard_map/all_gather | solution.py:540
  10.1 161.8 %all-gather.4.cloned.1.call-start = ((), (), s32[]{:S(2)}) async-start(), calls=%async_computation.3 | async-start | bytes 9437184 | tf_op jit(solution)/shard_map/all_gather | solution.py:540
  12.4 24.9 %collective-permute-start.1 = (bf16[512,256]{1,0:T(8,128)(2,1)}, bf16[512,256]{1,0:T(8,128)(2,1)}, u32[]{:S(2)}, u32[]{:S(2)}) collective-permute-start(bf16[512,256]{1,0:T(8,128)(2,1)} %get-tuple-element.49), channel_id=1, source_target_pairs={{0,2},{1,3},{2,0},{3,1},{4,6},{5,7},{6,4},{7,5},{8,10},{9,11},{10,... | collective-permute-start | bytes 786440 | tf_op jit(solution)/shard_map/ppermute | solution.py:140
  14.1 24.2 %collective-permute-start.2 = (bf16[512,256]{1,0:T(8,128)(2,1)}, bf16[512,256]{1,0:T(8,128)(2,1)S(1)}, u32[]{:S(2)}, u32[]{:S(2)}) collective-permute-start(bf16[512,256]{1,0:T(8,128)(2,1)} %get-tuple-element.49), channel_id=1, source_target_pairs={{0,3},{1,0},{2,1},{3,2},{4,7},{5,4},{6,5},{7,6},{8,11},{9,8},{10,9... | collective-permute-start | bytes 786440 | tf_op jit(solution)/shard_map/ppermute | solution.py:140
  39.3 178.5 %all-gather.8.cloned.1.call-start = ((), (), s32[]{:S(2)}) async-start(), calls=%async_computation.5 | async-start | bytes 9437184 | tf_op jit(solution)/shard_map/all_gather | solution.py:540
  40.5 328.2 %reduce-scatter.4.cloned.1.call-start = ((), (), s32[]{:S(2)}) async-start(), calls=%async_computation.6 | async-start | bytes 5242880 | tf_op jit(solution)/shard_map/reduce_scatter | solution.py:577
  57.0 75.5 %collective-permute-start.10 = (bf16[2,256,2048]{2,1,0:T(8,128)(2,1)}, bf16[2,256,2048]{2,1,0:T(8,128)(2,1)}, u32[]{:S(2)}, u32[]{:S(2)}) collective-permute-start(bf16[2,256,2048]{2,1,0:T(8,128)(2,1)} %shard_map.308.rest_0_), channel_id=1, source_target_pairs={{0,16},{4,20},{8,24},{12,28},{16,0},{20,4},{24,8},{28,12},{1,17},{... | collective-permute-start | bytes 6291464 | tf_op jit(solution)/shard_map/ppermute | solution.py:74
  57.6 77.8 %collective-permute-start.9 = (bf16[2,256,2048]{2,1,0:T(8,128)(2,1)}, bf16[2,256,2048]{2,1,0:T(8,128)(2,1)}, u32[]{:S(2)}, u32[]{:S(2)}) collective-permute-start(bf16[2,256,2048]{2,1,0:T(8,128)(2,1)} %shard_map.308.rest_0_), channel_id=1, source_target_pairs={{0,8},{4,12},{8,0},{12,4},{16,24},{20,28},{24,16},{28,20},{1,9},{5... | collective-permute-start | bytes 6291464 | tf_op jit(solution)/shard_map/ppermute | solution.py:74
  88.2 26.9 %collective-permute-start.3 = (bf16[1024,512]{1,0:T(8,128)(2,1)}, bf16[1024,512]{1,0:T(8,128)(2,1)S(1)}, u32[]{:S(2)}, u32[]{:S(2)}) collective-permute-start(bf16[1024,512]{1,0:T(8,128)(2,1)} %shard_map.306.rest_0_), channel_id=1, source_target_pairs={{0,1},{1,2},{2,3},{4,5},{5,6},{6,7},{8,9},{9,10},{10,11},{12,13},{... | collective-permute-start | bytes 3145736 | tf_op jit(solution)/shard_map/ppermute | solution.py:150
  89.5 26.9 %collective-permute-start.4 = (bf16[1024,512]{1,0:T(8,128)(2,1)}, bf16[1024,512]{1,0:T(8,128)(2,1)S(1)}, u32[]{:S(2)}, u32[]{:S(2)}) collective-permute-start(bf16[1024,512]{1,0:T(8,128)(2,1)} %shard_map.306.rest_0_), channel_id=1, source_target_pairs={{1,0},{2,1},{3,2},{5,4},{6,5},{7,6},{9,8},{10,9},{11,10},{13,12},{... | collective-permute-start | bytes 3145736 | tf_op jit(solution)/shard_map/ppermute | solution.py:151
  118.1 22.6 %collective-permute-start.6 = (bf16[1024,512]{1,0:T(8,128)(2,1)}, bf16[1024,512]{1,0:T(8,128)(2,1)}, u32[]{:S(2)}, u32[]{:S(2)}) collective-permute-start(bf16[1024,512]{1,0:T(8,128)(2,1)} %get-tuple-element.95), channel_id=1, source_target_pairs={{2,1},{1,2},{6,5},{5,6},{10,9},{9,10},{14,13},{13,14},{18,17},{17,... | collective-permute-start | bytes 3145736 | tf_op jit(solution)/shard_map/ppermute | solution.py:155
  119.7 48.9 %collective-permute-start.7 = (bf16[1024,512]{1,0:T(8,128)(2,1)}, bf16[1024,512]{1,0:T(8,128)(2,1)}, u32[]{:S(2)}, u32[]{:S(2)}) collective-permute-start(bf16[1024,512]{1,0:T(8,128)(2,1)} %get-tuple-element.94), channel_id=1, source_target_pairs={{1,0},{2,3},{5,4},{6,7},{9,8},{10,11},{13,12},{14,15},{17,16},{18,... | collective-permute-start | bytes 3145736 | tf_op jit(solution)/shard_map/ppermute | solution.py:156
  121.1 50.3 %collective-permute-start.5 = (bf16[1024,512]{1,0:T(8,128)(2,1)}, bf16[1024,512]{1,0:T(8,128)(2,1)}, u32[]{:S(2)}, u32[]{:S(2)}) collective-permute-start(bf16[1024,512]{1,0:T(8,128)(2,1)} %get-tuple-element.95), channel_id=1, source_target_pairs={{2,0},{1,3},{6,4},{5,7},{10,8},{9,11},{14,12},{13,15},{18,16},{17,... | collective-permute-start | bytes 3145736 | tf_op jit(solution)/shard_map/ppermute | solution.py:154
  134.8 57.6 %collective-permute-start.13 = (bf16[1,256,2048]{2,1,0:T(8,128)(2,1)}, bf16[1,256,2048]{2,1,0:T(8,128)(2,1)S(1)}, u32[]{:S(2)}, u32[]{:S(2)}) collective-permute-start(bf16[1,256,2048]{2,1,0:T(8,128)(2,1)} %slice.134), channel_id=1, source_target_pairs={{0,8},{4,12},{8,0},{12,4},{16,24},{20,28},{24,16},{28,20},{1,9},{5... | collective-permute-start | bytes 3145736 | tf_op jit(solution)/shard_map/ppermute | solution.py:74
  137.7 55.8 %collective-permute-start.14 = (bf16[1,256,2048]{2,1,0:T(8,128)(2,1)}, bf16[1,256,2048]{2,1,0:T(8,128)(2,1)}, u32[]{:S(2)}, u32[]{:S(2)}) collective-permute-start(bf16[1,256,2048]{2,1,0:T(8,128)(2,1)} %slice.135), channel_id=1, source_target_pairs={{0,16},{4,20},{8,24},{12,28},{16,0},{20,4},{24,8},{28,12},{1,17},{... | collective-permute-start | bytes 3145736 | tf_op jit(solution)/shard_map/ppermute | solution.py:74
  140.7 77.0 %collective-permute-start.8 = (bf16[2,256,2048]{2,1,0:T(8,128)(2,1)S(1)}, bf16[2,256,2048]{2,1,0:T(8,128)(2,1)}, u32[]{:S(2)}, u32[]{:S(2)}) collective-permute-start(bf16[2,256,2048]{2,1,0:T(8,128)(2,1)S(1)} %copy-done.3), channel_id=1, source_target_pairs={{0,4},{4,0},{8,12},{12,8},{16,20},{20,16},{24,28},{28,24},{1,5},{5... | collective-permute-start | bytes 6291464 | tf_op jit(solution)/shard_map/ppermute | solution.py:74
  168.6 49.2 %collective-permute-start.11 = (bf16[2,256,2048]{2,1,0:T(8,128)(2,1)}, bf16[2,256,2048]{2,1,0:T(8,128)(2,1)}, u32[]{:S(2)}, u32[]{:S(2)}) collective-permute-start(bf16[2,256,2048]{2,1,0:T(8,128)(2,1)} %collective-permute-done.9.rest_2_), channel_id=1, source_target_pairs={{0,4},{4,0},{8,12},{12,8},{16,20},{20,16},{24,28},{28,24},{1,5},{5... | collective-permute-start | bytes 6291464 | tf_op jit(solution)/shard_map/ppermute | solution.py:74
  171.4 46.4 %collective-permute-start.12 = (bf16[2,256,2048]{2,1,0:T(8,128)(2,1)}, bf16[2,256,2048]{2,1,0:T(8,128)(2,1)}, u32[]{:S(2)}, u32[]{:S(2)}) collective-permute-start(bf16[2,256,2048]{2,1,0:T(8,128)(2,1)} %collective-permute-done.10.rest_3_), channel_id=1, source_target_pairs={{0,4},{4,0},{8,12},{12,8},{16,20},{20,16},{24,28},{28,24},{1,5},{5... | collective-permute-start | bytes 6291464 | tf_op jit(solution)/shard_map/ppermute | solution.py:74
  197.5 20.3 %collective-permute-start.15 = (bf16[2,256,2048]{2,1,0:T(8,128)(2,1)}, bf16[2,256,2048]{2,1,0:T(8,128)(2,1)}, u32[]{:S(2)}, u32[]{:S(2)}) collective-permute-start(bf16[2,256,2048]{2,1,0:T(8,128)(2,1)} %pad_maximum_fusion.1.rest_6_), channel_id=1, source_target_pairs={{0,4},{4,0},{8,12},{12,8},{16,20},{20,16},{24,28},{28,24},{1,5},{5... | collective-permute-start | bytes 6291464 | tf_op jit(solution)/shard_map/ppermute | solution.py:74
  289.8 228.9 %reduce-scatter.6.cloned.1.call-start = ((), (), s32[]{:S(2)}) async-start(), calls=%async_computation.7 | async-start | bytes 5242880 | tf_op jit(solution)/shard_map/reduce_scatter | solution.py:605
  297.1 24.4 %collective-permute-start.35 = (bf16[1024,2048]{1,0:T(8,128)(2,1)S(1)}, bf16[1024,2048]{1,0:T(8,128)(2,1)}, u32[]{:S(2)}, u32[]{:S(2)}) collective-permute-start(bf16[1024,2048]{1,0:T(8,128)(2,1)S(1)} %copy-done.81), channel_id=1, source_target_pairs={{0,4},{4,0},{8,12},{12,8},{16,20},{20,16},{24,28},{28,24},{1,5},{5... | collective-permute-start | bytes 12582920 | tf_op jit(solution)/shard_map/ppermute | solution.py:74
  299.7 18.2 %collective-permute-start.40 = (bf16[1024,1024]{1,0:T(8,128)(2,1)S(1)}, bf16[1024,1024]{1,0:T(8,128)(2,1)S(1)}, u32[]{:S(2)}, u32[]{:S(2)}) collective-permute-start(bf16[1024,1024]{1,0:T(8,128)(2,1)S(1)} %convolution_convert_fusion.4), channel_id=1, source_target_pairs={{0,4},{4,0},{8,12},{12,8},{16,20},{20,16},{24,28},{28,24},{1,5},{5... | collective-permute-start | bytes 6291464 | tf_op jit(solution)/shard_map/ppermute | solution.py:74
  300.1 32.6 %collective-permute-start.34 = (bf16[1024,2048]{1,0:T(8,128)(2,1)S(1)}, bf16[1024,2048]{1,0:T(8,128)(2,1)}, u32[]{:S(2)}, u32[]{:S(2)}) collective-permute-start(bf16[1024,2048]{1,0:T(8,128)(2,1)S(1)} %copy-done.79), channel_id=1, source_target_pairs={{0,4},{4,0},{8,12},{12,8},{16,20},{20,16},{24,28},{28,24},{1,5},{5... | collective-permute-start | bytes 12582920 | tf_op jit(solution)/shard_map/ppermute | solution.py:74
  316.6 25.1 %collective-permute-start.42 = (bf16[1024,256]{1,0:T(8,128)(2,1)S(1)}, bf16[1024,256]{1,0:T(8,128)(2,1)S(1)}, u32[]{:S(2)}, u32[]{:S(2)}) collective-permute-start(bf16[1024,256]{1,0:T(8,128)(2,1)S(1)} %get-tuple-element.86), channel_id=1, source_target_pairs={{0,16},{4,20},{8,24},{12,28},{16,0},{20,4},{24,8},{28,12},{1,17},{... | collective-permute-start | bytes 1572872 | tf_op jit(solution)/shard_map/ppermute | solution.py:74
  320.6 23.9 %collective-permute-start.44 = (bf16[1024,256]{1,0:T(8,128)(2,1)S(1)}, bf16[1024,256]{1,0:T(8,128)(2,1)S(1)}, u32[]{:S(2)}, u32[]{:S(2)}) collective-permute-start(bf16[1024,256]{1,0:T(8,128)(2,1)S(1)} %get-tuple-element.85), channel_id=1, source_target_pairs={{0,8},{4,12},{8,0},{12,4},{16,24},{20,28},{24,16},{28,20},{1,9},{5... | collective-permute-start | bytes 1572872 | tf_op jit(solution)/shard_map/ppermute | solution.py:74
  331.9 26.0 %collective-permute-start.36 = (bf16[256,2048]{1,0:T(8,128)(2,1)S(1)}, bf16[256,2048]{1,0:T(8,128)(2,1)S(1)}, u32[]{:S(2)}, u32[]{:S(2)}) collective-permute-start(bf16[256,2048]{1,0:T(8,128)(2,1)S(1)} %get-tuple-element.64), channel_id=1, source_target_pairs={{0,16},{4,20},{8,24},{12,28},{16,0},{20,4},{24,8},{28,12},{1,17},{... | collective-permute-start | bytes 3145736 | tf_op jit(solution)/shard_map/ppermute | solution.py:74
  341.1 26.1 %collective-permute-start.38 = (bf16[256,2048]{1,0:T(8,128)(2,1)S(1)}, bf16[256,2048]{1,0:T(8,128)(2,1)S(1)}, u32[]{:S(2)}, u32[]{:S(2)}) collective-permute-start(bf16[256,2048]{1,0:T(8,128)(2,1)S(1)} %get-tuple-element.63), channel_id=1, source_target_pairs={{0,8},{4,12},{8,0},{12,4},{16,24},{20,28},{24,16},{28,20},{1,9},{5... | collective-permute-start | bytes 3145736 | tf_op jit(solution)/shard_map/ppermute | solution.py:74
  343.2 64.8 %collective-permute-start.43 = (bf16[2,1024,256]{2,1,0:T(8,128)(2,1)}, bf16[2,1024,256]{2,1,0:T(8,128)(2,1)}, u32[]{:S(2)}, u32[]{:S(2)}) collective-permute-start(bf16[2,1024,256]{2,1,0:T(8,128)(2,1)} %pad_maximum_fusion.14), channel_id=1, source_target_pairs={{0,8},{4,12},{8,0},{12,4},{16,24},{20,28},{24,16},{28,20},{1,9},{5... | collective-permute-start | bytes 3145736 | tf_op jit(solution)/shard_map/ppermute | solution.py:74
  345.7 62.3 %collective-permute-start.45 = (bf16[2,1024,256]{2,1,0:T(8,128)(2,1)}, bf16[2,1024,256]{2,1,0:T(8,128)(2,1)}, u32[]{:S(2)}, u32[]{:S(2)}) collective-permute-start(bf16[2,1024,256]{2,1,0:T(8,128)(2,1)} %pad_maximum_fusion.15), channel_id=1, source_target_pairs={{0,16},{4,20},{8,24},{12,28},{16,0},{20,4},{24,8},{28,12},{1,17},{... | collective-permute-start | bytes 3145736 | tf_op jit(solution)/shard_map/ppermute | solution.py:74
  383.0 21.0 %collective-permute-start.17 = (bf16[256,512]{1,0:T(8,128)(2,1)S(1)}, bf16[256,512]{1,0:T(8,128)(2,1)}, u32[]{:S(2)}, u32[]{:S(2)}) collective-permute-start(bf16[256,512]{1,0:T(8,128)(2,1)S(1)} %get-tuple-element.114), channel_id=1, source_target_pairs={{0,2},{1,3},{2,0},{3,1},{4,6},{5,7},{6,4},{7,5},{8,10},{9,11},{10,... | collective-permute-start | bytes 786440 | tf_op jit(solution)/shard_map/ppermute | solution.py:140
  383.0 21.0 %collective-permute-start.18 = (bf16[256,512]{1,0:T(8,128)(2,1)S(1)}, bf16[256,512]{1,0:T(8,128)(2,1)}, u32[]{:S(2)}, u32[]{:S(2)}) collective-permute-start(bf16[256,512]{1,0:T(8,128)(2,1)S(1)} %get-tuple-element.113), channel_id=1, source_target_pairs={{0,3},{1,0},{2,1},{3,2},{4,7},{5,4},{6,5},{7,6},{8,11},{9,8},{10,9... | collective-permute-start | bytes 786440 | tf_op jit(solution)/shard_map/ppermute | solution.py:140
  389.7 43.8 %collective-permute-start.37 = (bf16[2,256,2048]{2,1,0:T(8,128)(2,1)}, bf16[2,256,2048]{2,1,0:T(8,128)(2,1)}, u32[]{:S(2)}, u32[]{:S(2)}) collective-permute-start(bf16[2,256,2048]{2,1,0:T(8,128)(2,1)} %pad_maximum_fusion.6), channel_id=1, source_target_pairs={{0,8},{4,12},{8,0},{12,4},{16,24},{20,28},{24,16},{28,20},{1,9},{5... | collective-permute-start | bytes 6291464 | tf_op jit(solution)/shard_map/ppermute | solution.py:74
  404.0 243.2 %reduce-scatter.8.cloned.1.call-start = ((), (), s32[]{:S(2)}) async-start(), calls=%async_computation.8 | async-start | bytes 5242880 | tf_op jit(solution)/shard_map/reduce_scatter | solution.py:623
  406.4 46.7 %collective-permute-start.39 = (bf16[2,256,2048]{2,1,0:T(8,128)(2,1)S(1)}, bf16[2,256,2048]{2,1,0:T(8,128)(2,1)S(1)}, u32[]{:S(2)}, u32[]{:S(2)}) collective-permute-start(bf16[2,256,2048]{2,1,0:T(8,128)(2,1)S(1)} %pad_maximum_fusion.7), channel_id=1, source_target_pairs={{0,16},{4,20},{8,24},{12,28},{16,0},{20,4},{24,8},{28,12},{1,17},{... | collective-permute-start | bytes 6291464 | tf_op jit(solution)/shard_map/ppermute | solution.py:74
  413.5 55.4 %collective-permute-start.20 = (bf16[1024,1024]{1,0:T(8,128)(2,1)}, bf16[1024,1024]{1,0:T(8,128)(2,1)}, u32[]{:S(2)}, u32[]{:S(2)}) collective-permute-start(bf16[1024,1024]{1,0:T(8,128)(2,1)} %convolution_convert_fusion.5), channel_id=1, source_target_pairs={{0,4},{4,0},{8,12},{12,8},{16,20},{20,16},{24,28},{28,24},{1,5},{5... | collective-permute-start | bytes 6291464 | tf_op jit(solution)/shard_map/ppermute | solution.py:74
  415.6 57.7 %collective-permute-start.19 = (bf16[1024,1024]{1,0:T(8,128)(2,1)}, bf16[1024,1024]{1,0:T(8,128)(2,1)}, u32[]{:S(2)}, u32[]{:S(2)}) collective-permute-start(bf16[1024,1024]{1,0:T(8,128)(2,1)} %convolution_convert_fusion.6), channel_id=1, source_target_pairs={{0,4},{4,0},{8,12},{12,8},{16,20},{20,16},{24,28},{28,24},{1,5},{5... | collective-permute-start | bytes 6291464 | tf_op jit(solution)/shard_map/ppermute | solution.py:74
  511.1 24.3 %collective-permute-start.21 = (bf16[1024,768]{1,0:T(8,128)(2,1)}, bf16[1024,768]{1,0:T(8,128)(2,1)}, u32[]{:S(2)}, u32[]{:S(2)}) collective-permute-start(bf16[1024,768]{1,0:T(8,128)(2,1)} %convolution_convert_fusion.8), channel_id=1, source_target_pairs={{0,4},{4,0},{8,12},{12,8},{16,20},{20,16},{24,28},{28,24},{1,5},{5... | collective-permute-start | bytes 4718600 | tf_op jit(solution)/shard_map/ppermute | solution.py:74
  516.7 23.2 %collective-permute-start.22 = (bf16[1024,768]{1,0:T(8,128)(2,1)}, bf16[1024,768]{1,0:T(8,128)(2,1)}, u32[]{:S(2)}, u32[]{:S(2)}) collective-permute-start(bf16[1024,768]{1,0:T(8,128)(2,1)} %convolution_convert_fusion.7), channel_id=1, source_target_pairs={{0,4},{4,0},{8,12},{12,8},{16,20},{20,16},{24,28},{28,24},{1,5},{5... | collective-permute-start | bytes 4718600 | tf_op jit(solution)/shard_map/ppermute | solution.py:74
  530.4 28.2 %collective-permute-start.28 = (bf16[2,1024,256]{2,1,0:T(8,128)(2,1)}, bf16[2,1024,256]{2,1,0:T(8,128)(2,1)}, u32[]{:S(2)}, u32[]{:S(2)}) collective-permute-start(bf16[2,1024,256]{2,1,0:T(8,128)(2,1)} %pad_maximum_fusion.12), channel_id=1, source_target_pairs={{0,8},{4,12},{8,0},{12,4},{16,24},{20,28},{24,16},{28,20},{1,9},{5... | collective-permute-start | bytes 3145736 | tf_op jit(solution)/shard_map/ppermute | solution.py:74
  534.9 26.4 %collective-permute-start.30 = (bf16[2,1024,256]{2,1,0:T(8,128)(2,1)}, bf16[2,1024,256]{2,1,0:T(8,128)(2,1)}, u32[]{:S(2)}, u32[]{:S(2)}) collective-permute-start(bf16[2,1024,256]{2,1,0:T(8,128)(2,1)} %pad_maximum_fusion.13), channel_id=1, source_target_pairs={{0,16},{4,20},{8,24},{12,28},{16,0},{20,4},{24,8},{28,12},{1,17},{... | collective-permute-start | bytes 3145736 | tf_op jit(solution)/shard_map/ppermute | solution.py:74
  547.4 27.2 %collective-permute-start.23 = (bf16[256,768]{1,0:T(8,128)(2,1)S(1)}, bf16[256,768]{1,0:T(8,128)(2,1)S(1)}, u32[]{:S(2)}, u32[]{:S(2)}) collective-permute-start(bf16[256,768]{1,0:T(8,128)(2,1)S(1)} %get-tuple-element.100), channel_id=1, source_target_pairs={{0,16},{4,20},{8,24},{12,28},{16,0},{20,4},{24,8},{28,12},{1,17},{... | collective-permute-start | bytes 1179656 | tf_op jit(solution)/shard_map/ppermute | solution.py:74
  548.3 28.9 %collective-permute-start.25 = (bf16[256,768]{1,0:T(8,128)(2,1)S(1)}, bf16[256,768]{1,0:T(8,128)(2,1)S(1)}, u32[]{:S(2)}, u32[]{:S(2)}) collective-permute-start(bf16[256,768]{1,0:T(8,128)(2,1)S(1)} %get-tuple-element.99), channel_id=1, source_target_pairs={{0,8},{4,12},{8,0},{12,4},{16,24},{20,28},{24,16},{28,20},{1,9},{5... | collective-permute-start | bytes 1179656 | tf_op jit(solution)/shard_map/ppermute | solution.py:74
  570.8 65.5 %collective-permute-start.31 = (bf16[512,256]{1,0:T(8,128)(2,1)S(1)}, bf16[512,256]{1,0:T(8,128)(2,1)S(1)}, u32[]{:S(2)}, u32[]{:S(2)}) collective-permute-start(bf16[512,256]{1,0:T(8,128)(2,1)S(1)} %get-tuple-element.102), channel_id=1, source_target_pairs={{0,1},{1,2},{2,3},{3,0},{4,5},{5,6},{6,7},{7,4},{8,9},{9,10},{10,1... | collective-permute-start | bytes 786440 | tf_op jit(solution)/shard_map/ppermute | solution.py:140
  574.0 62.3 %collective-permute-start.32 = (bf16[512,256]{1,0:T(8,128)(2,1)S(1)}, bf16[512,256]{1,0:T(8,128)(2,1)S(1)}, u32[]{:S(2)}, u32[]{:S(2)}) collective-permute-start(bf16[512,256]{1,0:T(8,128)(2,1)S(1)} %get-tuple-element.103), channel_id=1, source_target_pairs={{0,2},{1,3},{2,0},{3,1},{4,6},{5,7},{6,4},{7,5},{8,10},{9,11},{10,... | collective-permute-start | bytes 786440 | tf_op jit(solution)/shard_map/ppermute | solution.py:140
  574.3 62.0 %collective-permute-start.33 = (bf16[512,256]{1,0:T(8,128)(2,1)S(1)}, bf16[512,256]{1,0:T(8,128)(2,1)S(1)}, u32[]{:S(2)}, u32[]{:S(2)}) collective-permute-start(bf16[512,256]{1,0:T(8,128)(2,1)S(1)} %get-tuple-element.104), channel_id=1, source_target_pairs={{0,3},{1,0},{2,1},{3,2},{4,7},{5,4},{6,5},{7,6},{8,11},{9,8},{10,9... | collective-permute-start | bytes 786440 | tf_op jit(solution)/shard_map/ppermute | solution.py:140
  574.6 41.9 %collective-permute-start.50 = (f32[2,256]{1,0:T(2,128)S(1)}, f32[2,256]{1,0:T(2,128)S(1)}, u32[]{:S(2)}, u32[]{:S(2)}) collective-permute-start(f32[2,256]{1,0:T(2,128)S(1)} %add.555), channel_id=1, source_target_pairs={{0,2},{1,3},{2,0},{3,1},{4,6},{5,7},{6,4},{7,5},{8,10},{9,11},{10,... | collective-permute-start | bytes 6152 | tf_op jit(solution)/shard_map/ppermute | solution.py:74
  577.2 61.4 %collective-permute-start.24 = (bf16[2,256,768]{2,1,0:T(8,128)(2,1)S(1)}, bf16[2,256,768]{2,1,0:T(8,128)(2,1)S(1)}, u32[]{:S(2)}, u32[]{:S(2)}) collective-permute-start(bf16[2,256,768]{2,1,0:T(8,128)(2,1)S(1)} %pad_maximum_fusion.16), channel_id=1, source_target_pairs={{0,8},{4,12},{8,0},{12,4},{16,24},{20,28},{24,16},{28,20},{1,9},{5... | collective-permute-start | bytes 2359304 | tf_op jit(solution)/shard_map/ppermute | solution.py:74
  616.5 22.1 %collective-permute-start.26 = (bf16[2,256,768]{2,1,0:T(8,128)(2,1)S(1)}, bf16[2,256,768]{2,1,0:T(8,128)(2,1)S(1)}, u32[]{:S(2)}, u32[]{:S(2)}) collective-permute-start(bf16[2,256,768]{2,1,0:T(8,128)(2,1)S(1)} %pad_maximum_fusion.17), channel_id=1, source_target_pairs={{0,16},{4,20},{8,24},{12,28},{16,0},{20,4},{24,8},{28,12},{1,17},{... | collective-permute-start | bytes 2359304 | tf_op jit(solution)/shard_map/ppermute | solution.py:74
  (94 other events, 1526.7 us)
Sparse Core Ops, SparseCore 0:
  10.5 46.4 all-gather.5
  59.5 86.2 all-gather.3
  148.2 59.5 all-gather.7
  289.9 76.6 reduce-scatter.3
  404.2 77.1 reduce-scatter.5
  518.8 93.7 reduce-scatter.7
